TPU v7x, 32 devices: a whole 2x2x4 slice. The times are simulated.
32 devices in a mesh: tgt: 8 (over z, x), sec: 4 (over y, core).
Axes of the slice: x: 2, y: 2, z: 4, core: 2. Of those that a mesh axis runs over, the one named last changes fastest.
Arguments:
- queries: bfloat16 [2048, 4096], P('tgt', 'sec'), may hold values from -210 to 210
- key_values: bfloat16 [2, 2048, 4096], P(None, 'tgt', 'sec'), may hold values from -6.06 to 6.06
- grad_out: bfloat16 [2048, 4096], P('tgt', 'sec'), may hold values from -192 to 192
- block_ids: int32 [16, 4], P('tgt'), may hold values from 0 to 15, as said below
- block_count: int32 [16], P('tgt'), may hold values from 1 to 4, as said below
- kv_weight: bfloat16 [2, 4096, 4096], P(None, 'tgt', 'sec'), may hold values from -0.0625 to 0.0625
Outputs:
- grad_queries: bfloat16 [2048, 4096], P('tgt', 'sec')
- grad_memory: bfloat16 [2048, 4096], P('tgt', 'sec')
Inputs may be any that keep to these rules, and one draw needn't show every extreme that they name: `block_ids`: target block i, which lies in the rows of index t = i // 2 of tgt, lists only source blocks in the rows of indices t - 1, t and t + 1; its first entry is block i itself; its live entries are distinct; entries past its count repeat block i. `block_count`: every eighth block, starting at block 3, has all slots live.
All inputs are finite; a program needn't handle non-finite values.
Results may differ from a plain program's by a relative error of at most 0.013.
Values may be sent and summed in bfloat16 or wider, within the bound.
No kernel may reach another device: no remote copies, remote signals or barrier semaphores. Data moves between devices by JAX's collectives and lax.ppermute only.
A program may use at most 128 MiB of HBM per device.

v0:
```python
import jax
import jax.numpy as jnp
from jax import lax
from jax.sharding import PartitionSpec as P

HEAD_DIM = 64
BLOCK = 128
SLOTS = 4


def from_behind(block, axis, distance):
    devices = range(lax.axis_size(axis))
    route = [(i - distance, i) for i in devices if i - distance in devices]
    return lax.ppermute(block, axis, route)


def with_halo(block, sides, width):
    for axis, dim in sides:
        count = lax.axis_size(axis)
        forward = [(i, i + 1) for i in range(count - 1)]
        backward = [(target, source) for source, target in forward]
        low = lax.ppermute(
            lax.slice_in_dim(block, block.shape[dim] - width, None, axis=dim), axis, forward
        )
        high = lax.ppermute(lax.slice_in_dim(block, 0, width, axis=dim), axis, backward)
        block = jnp.concatenate([low, block, high], axis=dim)
    return block


def send_back(part_grads, offset):
    return from_behind(part_grads.astype(jnp.bfloat16), "tgt", offset).astype(part_grads.dtype)


def per_device(queries, key_values, grad_out, block_ids, block_count, kv_weight):
    rows_here = queries.shape[0]
    width_here = queries.shape[1]
    heads_here = width_here // HEAD_DIM
    blocks_here = rows_here // BLOCK
    device_pos = lax.axis_index("tgt")
    extended = with_halo(key_values, (("tgt", 1),), rows_here)
    local_ids = block_ids - (device_pos - 1) * blocks_here
    ext_blocks = extended.reshape(2, 3 * blocks_here, BLOCK, width_here)
    ext_range = jnp.arange(3 * blocks_here)

    def block_step(carry, inputs):
        query_block, upstream_block, listed, count = inputs
        picked = ext_blocks[:, listed]
        key_rows = picked[0].reshape(SLOTS * BLOCK, heads_here, HEAD_DIM)
        value_rows = picked[1].reshape(SLOTS * BLOCK, heads_here, HEAD_DIM)
        query_rows = query_block.reshape(BLOCK, heads_here, HEAD_DIM)
        upstream = upstream_block.reshape(BLOCK, heads_here, HEAD_DIM)
        slot_live = jnp.arange(SLOTS) < count
        key_live = jnp.repeat(slot_live, BLOCK)
        scores = 0.125 * jnp.einsum(
            "qhd,khd->hqk", query_rows, key_rows, preferred_element_type=jnp.float32
        )
        scores = jnp.where(key_live[None, None, :], scores, -jnp.inf)
        row_max = jnp.max(scores, axis=-1, keepdims=True)
        expo = jnp.exp(scores - row_max)
        probs = expo / jnp.sum(expo, axis=-1, keepdims=True)
        probs_half = probs.astype(jnp.bfloat16)
        attended = jnp.einsum(
            "hqk,khd->qhd", probs_half, value_rows, preferred_element_type=jnp.float32
        )
        delta = jnp.sum(upstream.astype(jnp.float32) * attended, axis=-1)
        grad_probs = jnp.einsum(
            "qhd,khd->hqk", upstream, value_rows, preferred_element_type=jnp.float32
        )
        grad_scores = probs * (grad_probs - jnp.transpose(delta)[:, :, None])
        grad_half = grad_scores.astype(jnp.bfloat16)
        grad_query = 0.125 * jnp.einsum(
            "hqk,khd->qhd", grad_half, key_rows, preferred_element_type=jnp.float32
        )
        grad_key = 0.125 * jnp.einsum(
            "hqk,qhd->khd", grad_half, query_rows, preferred_element_type=jnp.float32
        )
        grad_value = jnp.einsum(
            "hqk,qhd->khd", probs_half, upstream, preferred_element_type=jnp.float32
        )
        pair_grads = jnp.stack([grad_key, grad_value]).reshape(2, SLOTS, BLOCK, width_here)
        targets = ((listed[:, None] == ext_range[None, :]) & slot_live[:, None]).astype(jnp.float32)
        carry = carry + jnp.einsum(
            "sj,csrx->cjrx", targets, pair_grads, precision=lax.Precision.HIGHEST
        )
        return (carry, grad_query.reshape(BLOCK, width_here).astype(jnp.bfloat16))

    start = jnp.zeros((2, 3 * blocks_here, BLOCK, width_here), jnp.float32)
    inputs = (
        queries.reshape(blocks_here, BLOCK, width_here),
        grad_out.reshape(blocks_here, BLOCK, width_here),
        local_ids,
        block_count,
    )
    spread_blocks, query_blocks = lax.scan(block_step, start, inputs)
    spread = spread_blocks.reshape(2, 3 * rows_here, width_here)
    own_grads = spread[:, rows_here : 2 * rows_here]
    own_grads = (
        own_grads + send_back(spread[:, :rows_here], -1) + send_back(spread[:, 2 * rows_here :], 1)
    )
    grads_half = own_grads.astype(jnp.bfloat16)
    partial_memory = jnp.einsum(
        "crx,cnx->rn",
        grads_half,
        lax.all_gather(kv_weight, "tgt", axis=1, tiled=True),
        preferred_element_type=jnp.float32,
    )
    total_memory = lax.psum(partial_memory.astype(jnp.bfloat16), "sec").astype(jnp.float32)
    columns = total_memory.shape[1] // lax.axis_size("sec")
    grad_memory = lax.dynamic_slice_in_dim(
        total_memory, lax.axis_index("sec") * columns, columns, 1
    ).astype(jnp.bfloat16)
    grad_queries = query_blocks.reshape(rows_here, width_here)
    return (grad_queries, grad_memory)


def solution(mesh):
    return jax.shard_map(
        per_device,
        mesh=mesh,
        in_specs=(
            P("tgt", "sec"),
            P(None, "tgt", "sec"),
            P("tgt", "sec"),
            P("tgt", None),
            P("tgt"),
            P(None, "tgt", "sec"),
        ),
        out_specs=(P("tgt", "sec"), P("tgt", "sec")),
        check_vma=False,
    )
```

profile of v0, /device:TPU:0, one launch (start us, length us, event | category | flops | bytes accessed | tf_op | source)
XLA Modules:
  0.0 352.7 jit_solution(11192809723274626078)
XLA Ops:
  7.9 4.9 %collective-permute-start = (bf16[2,256,1024]{2,1,0:T(8,128)(2,1)}, bf16[2,256,1024]{2,1,0:T(8,128)(2,1)S(1)}, u32[]{:S(2)}, u32[]{:S(2)}) collective-permute-start(bf16[2,256,1024]{2,1,0:T(8,128)(2,1)} %param.9), channel_id=1, source_target_pairs={{0,4},{4,8},{8,12},{12,16},{16,20},{20,24},{24,28},{1,5},{5,9},{9,... | collective-permute-start | bytes 3145736 | tf_op jit(solution)/shard_map/ppermute | solution.py:22
  14.9 62.4 %collective-permute-done = bf16[2,256,1024]{2,1,0:T(8,128)(2,1)S(1)} collective-permute-done((bf16[2,256,1024]{2,1,0:T(8,128)(2,1)}, bf16[2,256,1024]{2,1,0:T(8,128)(2,1)S(1)}, u32[]{:S(2)}, u32[]{:S(2)}) %collective-permute-start) | collective-permute-done | bytes 1048608 | tf_op jit(solution)/shard_map/ppermute | solution.py:22
  77.3 2.8 pad_maximum_fusion
  80.1 116.7 %while.13 = (s32[]{:T(128)}, f32[2,6,128,1024]{3,1,2,0:T(8,128)}, bf16[2,128,1024]{2,1,0:T(8,128)(2,1)}, bf16[2,128,1024]{2,1,0:T(8,128)(2,1)}, s32[2]{0:T(128)S...) while((s32[]{:T(128)}, f32[2,6,128,1024]{3,1,2,0:T(8,128)}, ...), condition=%wide.region_4.5_spmd.clone, body=%wide.region_0.4_spmd.clone.sunk | while | flops 896663104 | bytes 128497184 | solution.py:94
  80.1 2.6 gather_fusion
  87.5 3.4 fusion.88
  90.9 2.6 fusion.89
  93.4 2.4 copy.37
  95.9 2.3 squeeze.24
  101.4 2.8 multiply_convert_fusion.2
  107.4 2.9 stack.15
  110.3 3.9 %copy.38 = f32[1,4,128,1024]{3,1,2,0:T(4,128)} copy(f32[1,4,128,1024]{2,1,3,0:T(4,128)} %stack.15) | data formatting | bytes 4194304 | tf_op jit(solution)/shard_map/while/body/eval_jaxpr/stack | solution.py:80
  116.0 2.9 stack.14
  118.8 4.8 %copy.36 = f32[1,4,128,1024]{3,1,2,0:T(4,128)} copy(f32[1,4,128,1024]{2,1,3,0:T(4,128)} %stack.14) | data formatting | bytes 4194304 | tf_op jit(solution)/shard_map/while/body/eval_jaxpr/stack | solution.py:80
  123.7 12.1 %bitcast_add_fusion.2 = f32[2,6,128,1024]{3,1,2,0:T(8,128)} fusion(f32[2,6,128,1024]{3,1,2,0:T(8,128)} %get-tuple-element.185, pred[]{:T(512)S(6)} %compare.3, f32[1,4,128,1024]{3,1,2,0:T(4,128)} %copy.36, f32[1,4,128,1024]{3,1,2,0:T(4,128)S(1)} %copy-done, s32[4]{0:T(128)S(1)} %fusion.91, pred[4]{0:T(512)(128)(4,1)S(1)} %iota_compare_fusion.3), kind=kOutput, calls=%fused_computation.3.clone.1 | convolution fusion | flops 79691824 | bytes 16777236 | tf_op jit(solution)/shard_map/while/body/eval_jaxpr/sj,csrx->cjrx/dot_general | solution.py:82
  137.6 2.6 gather_fusion
  145.0 3.4 fusion.88
  148.3 2.6 fusion.89
  150.9 2.4 copy.37
  158.9 2.8 multiply_convert_fusion.2
  164.8 2.9 stack.15
  167.7 3.9 %copy.38 = f32[1,4,128,1024]{3,1,2,0:T(4,128)} copy(f32[1,4,128,1024]{2,1,3,0:T(4,128)} %stack.15) | data formatting | bytes 4194304 | tf_op jit(solution)/shard_map/while/body/eval_jaxpr/stack | solution.py:80
  173.4 2.9 stack.14
  176.3 4.1 %copy.36 = f32[1,4,128,1024]{3,1,2,0:T(4,128)} copy(f32[1,4,128,1024]{2,1,3,0:T(4,128)} %stack.14) | data formatting | bytes 4194304 | tf_op jit(solution)/shard_map/while/body/eval_jaxpr/stack | solution.py:80
  180.4 14.5 %bitcast_add_fusion.2 = f32[2,6,128,1024]{3,1,2,0:T(8,128)} fusion(f32[2,6,128,1024]{3,1,2,0:T(8,128)} %get-tuple-element.185, pred[]{:T(512)S(6)} %compare.3, f32[1,4,128,1024]{3,1,2,0:T(4,128)} %copy.36, f32[1,4,128,1024]{3,1,2,0:T(4,128)S(1)} %copy-done, s32[4]{0:T(128)S(1)} %fusion.91, pred[4]{0:T(512)(128)(4,1)S(1)} %iota_compare_fusion.3), kind=kOutput, calls=%fused_computation.3.clone.1 | convolution fusion | flops 79691824 | bytes 16777236 | tf_op jit(solution)/shard_map/while/body/eval_jaxpr/sj,csrx->cjrx/dot_general | solution.py:82
  196.8 7.0 %copy.20 = f32[2,6,128,1024]{3,2,1,0:T(8,128)S(1)} copy(f32[2,6,128,1024]{3,1,2,0:T(8,128)} %get-tuple-element.51) | data formatting | bytes 12582912 | tf_op jit(solution)/shard_map/while | solution.py:94
  207.9 4.7 %collective-permute-start.3 = (bf16[2,256,1024]{2,1,0:T(8,128)(2,1)S(1)}, bf16[2,256,1024]{2,1,0:T(8,128)(2,1)S(1)}, u32[]{:S(2)}, u32[]{:S(2)}) collective-permute-start(bf16[2,256,1024]{2,1,0:T(8,128)(2,1)S(1)} %get-tuple-element.112), channel_id=1, source_target_pairs={{0,4},{4,8},{8,12},{12,16},{16,20},{20,24},{24,28},{1,5},{5,9},{9,... | collective-permute-start | bytes 3145736 | tf_op jit(solution)/shard_map/ppermute | solution.py:14
  212.6 20.4 %collective-permute-done.2 = bf16[2,256,1024]{2,1,0:T(8,128)(2,1)S(1)} collective-permute-done((bf16[2,256,1024]{2,1,0:T(8,128)(2,1)S(1)}, bf16[2,256,1024]{2,1,0:T(8,128)(2,1)S(1)}, u32[]{:S(2)}, u32[]{:S(2)}) %collective-permute-start.2) | collective-permute-done | bytes 1048608 | tf_op jit(solution)/shard_map/ppermute | solution.py:14
  233.0 7.4 %collective-permute-done.3 = bf16[2,256,1024]{2,1,0:T(8,128)(2,1)S(1)} collective-permute-done((bf16[2,256,1024]{2,1,0:T(8,128)(2,1)S(1)}, bf16[2,256,1024]{2,1,0:T(8,128)(2,1)S(1)}, u32[]{:S(2)}, u32[]{:S(2)}) %collective-permute-start.3) | collective-permute-done | bytes 1048608 | tf_op jit(solution)/shard_map/ppermute | solution.py:14
  240.4 41.3 %all-gather.2.cloned.1.call-done = bf16[2,4096,1024]{2,1,0:T(8,128)(2,1)} async-done(((bf16[2,512,1024]{2,1,0:T(8,128)(2,1)}), bf16[2,4096,1024]{2,1,0:T(8,128)(2,1)}) %all-gather.2.cloned.1.call-update) | async-done | bytes 16777232 | tf_op jit(solution)/shard_map/all_gather | solution.py:104
  281.6 12.3 %fusion.29 = bf16[256,4096]{1,0:T(8,128)(2,1)} fusion(bf16[2,4096,1024]{2,1,0:T(8,128)(2,1)} %all-gather.2.cloned.1.call-done, f32[2,768,1024]{2,1,0:T(8,128)} %bitcast.128, bf16[2,256,1024]{2,1,0:T(8,128)(2,1)S(1)} %collective-permute-done.3, bf16[2,256,1024]{2,1,0:T(8,128)(2,1)S(1)} %collective-permute-done.2), kind=kOutput, calls=%fused_computation.44 | convolution fusion | flops 4298637312 | bytes 23068672 | tf_op jit(solution)/shard_map/crx,cnx->rn/dot_general | solution.py:101
  293.9 50.1 %all-reduce.2.cloned.1.call-done = bf16[256,4096]{1,0:T(8,128)(2,1)} async-done(((bf16[256,4096]{1,0:T(8,128)(2,1)}), bf16[256,4096]{1,0:T(8,128)(2,1)}) %all-reduce.2.cloned.1.call-update) | async-done | bytes 2097168 | tf_op jit(solution)/shard_map/psum | solution.py:107
  (94 shorter events, 40.4 us)
Async XLA Ops:
  7.2 274.5 %all-gather.2.cloned.1.call-start = ((), (), s32[]{:S(2)}) async-start(), calls=%async_computation | async-start | bytes 18874368 | tf_op jit(solution)/shard_map/all_gather | solution.py:104
  7.9 336.1 %all-reduce.2.cloned.1.call-start = ((), (), s32[]{:S(2)}) async-start(), calls=%async_computation.1 | async-start | bytes 4194304 | tf_op jit(solution)/shard_map/psum | solution.py:107
  7.9 69.3 %collective-permute-start = (bf16[2,256,1024]{2,1,0:T(8,128)(2,1)}, bf16[2,256,1024]{2,1,0:T(8,128)(2,1)S(1)}, u32[]{:S(2)}, u32[]{:S(2)}) collective-permute-start(bf16[2,256,1024]{2,1,0:T(8,128)(2,1)} %param.9), channel_id=1, source_target_pairs={{0,4},{4,8},{8,12},{12,16},{16,20},{20,24},{24,28},{1,5},{5,9},{9,... | collective-permute-start | bytes 3145736 | tf_op jit(solution)/shard_map/ppermute | solution.py:22
  12.9 64.4 %collective-permute-start.1 = (bf16[2,256,1024]{2,1,0:T(8,128)(2,1)}, bf16[2,256,1024]{2,1,0:T(8,128)(2,1)S(1)}, u32[]{:S(2)}, u32[]{:S(2)}) collective-permute-start(bf16[2,256,1024]{2,1,0:T(8,128)(2,1)} %param.9), channel_id=1, source_target_pairs={{4,0},{8,4},{12,8},{16,12},{20,16},{24,20},{28,24},{5,1},{9,5},{13... | collective-permute-start | bytes 3145736 | tf_op jit(solution)/shard_map/ppermute | solution.py:25
  14.9 65.2 %copy-start.11 = (s32[2]{0:T(128)S(1)}, s32[2]{0:T(128)}, u32[]{:S(2)}) copy-start(s32[2]{0:T(128)} %param.12) | copy-start | bytes 28
  84.0 1.2 copy-start.7
  84.0 1.2 copy-start.8
  86.1 4.8 %copy-start.4 = (bf16[1,128,1024]{1,2,0:T(8,128)(2,1)}, bf16[1,128,1024]{1,2,0:T(8,128)(2,1)S(1)}, u32[]{:S(2)}) copy-start(bf16[1,128,1024]{1,2,0:T(8,128)(2,1)S(1)} %copy.34) | copy-start | bytes 786436 | tf_op jit(solution)/shard_map/while
  99.3 2.2 copy-start.3
  101.4 4.2 %copy-start.5 = (bf16[1,128,1024]{1,2,0:T(8,128)(2,1)S(1)}, bf16[1,128,1024]{1,2,0:T(8,128)(2,1)}, u32[]{:S(2)}) copy-start(bf16[1,128,1024]{1,2,0:T(8,128)(2,1)} %copy-done.4) | copy-start | bytes 786436 | tf_op jit(solution)/shard_map/while
  104.3 1.4 copy-start.1
  118.8 4.8 %copy-start = (f32[1,4,128,1024]{3,1,2,0:T(4,128)S(1)}, f32[1,4,128,1024]{3,1,2,0:T(4,128)}, u32[]{:S(2)}) copy-start(f32[1,4,128,1024]{3,1,2,0:T(4,128)} %copy.38) | copy-start | bytes 6291460 | tf_op jit(solution)/shard_map/while
  123.7 12.1 %copy-start.2 = (bf16[16,128,512]{2,1,0:T(8,128)(2,1)S(1)}, bf16[16,128,512]{2,1,0:T(8,128)(2,1)}, u32[]{:S(2)}) copy-start(bf16[16,128,512]{2,1,0:T(8,128)(2,1)} %copy-done.1) | copy-start | bytes 6291460 | tf_op jit(solution)/shard_map/while
  135.7 1.0 copy-start.9
  136.8 0.8 copy-start.10
  141.4 1.2 copy-start.7
  141.4 1.2 copy-start.8
  143.6 4.8 %copy-start.4 = (bf16[1,128,1024]{1,2,0:T(8,128)(2,1)}, bf16[1,128,1024]{1,2,0:T(8,128)(2,1)S(1)}, u32[]{:S(2)}) copy-start(bf16[1,128,1024]{1,2,0:T(8,128)(2,1)S(1)} %copy.34) | copy-start | bytes 786436 | tf_op jit(solution)/shard_map/while
  156.7 2.2 copy-start.3
  158.9 4.2 %copy-start.5 = (bf16[1,128,1024]{1,2,0:T(8,128)(2,1)S(1)}, bf16[1,128,1024]{1,2,0:T(8,128)(2,1)}, u32[]{:S(2)}) copy-start(bf16[1,128,1024]{1,2,0:T(8,128)(2,1)} %copy-done.4) | copy-start | bytes 786436 | tf_op jit(solution)/shard_map/while
  161.7 1.4 copy-start.1
  176.3 4.1 %copy-start = (f32[1,4,128,1024]{3,1,2,0:T(4,128)S(1)}, f32[1,4,128,1024]{3,1,2,0:T(4,128)}, u32[]{:S(2)}) copy-start(f32[1,4,128,1024]{3,1,2,0:T(4,128)} %copy.38) | copy-start | bytes 6291460 | tf_op jit(solution)/shard_map/while
  180.4 14.5 %copy-start.2 = (bf16[16,128,512]{2,1,0:T(8,128)(2,1)S(1)}, bf16[16,128,512]{2,1,0:T(8,128)(2,1)}, u32[]{:S(2)}) copy-start(bf16[16,128,512]{2,1,0:T(8,128)(2,1)} %copy-done.1) | copy-start | bytes 6291460 | tf_op jit(solution)/shard_map/while
  194.9 1.0 copy-start.9
  196.0 0.8 copy-start.10
  203.8 2.7 copy-start.6
  206.6 26.4 %collective-permute-start.2 = (bf16[2,256,1024]{2,1,0:T(8,128)(2,1)S(1)}, bf16[2,256,1024]{2,1,0:T(8,128)(2,1)S(1)}, u32[]{:S(2)}, u32[]{:S(2)}) collective-permute-start(bf16[2,256,1024]{2,1,0:T(8,128)(2,1)S(1)} %get-tuple-element.111), channel_id=1, source_target_pairs={{4,0},{8,4},{12,8},{16,12},{20,16},{24,20},{28,24},{5,1},{9,5},{13... | collective-permute-start | bytes 3145736 | tf_op jit(solution)/shard_map/ppermute | solution.py:14
  207.9 32.5 %collective-permute-start.3 = (bf16[2,256,1024]{2,1,0:T(8,128)(2,1)S(1)}, bf16[2,256,1024]{2,1,0:T(8,128)(2,1)S(1)}, u32[]{:S(2)}, u32[]{:S(2)}) collective-permute-start(bf16[2,256,1024]{2,1,0:T(8,128)(2,1)S(1)} %get-tuple-element.112), channel_id=1, source_target_pairs={{0,4},{4,8},{8,12},{12,16},{16,20},{20,24},{24,28},{1,5},{5,9},{9,... | collective-permute-start | bytes 3145736 | tf_op jit(solution)/shard_map/ppermute | solution.py:14
Sparse Core Ops, SparseCore 0:
  10.2 271.4 all-gather.1
  294.1 49.9 all-reduce.1
where the time goes:
time: 354 us; the launch traced here: 353 us
  waiting for transfers between devices  182 us (51%)
  local copies, waits for them, and re-layouts  67.4 us (19%)
  matrix products  64.1 us (18%)
  between operations  14.1 us (4%)
  other arithmetic  12.3 us (3%)
  starting transfers between devices  12.2 us (3%)
    ppermute x1, waiting for transfers between devices, with_halo(): lax.ppermute(lax.slice_in_dim(block, block.shape[dim] - width, None, axis...  62.4 us
    psum x1, waiting for transfers between devices, per_device(): lax.psum(partial_memory.astype(jnp.bfloat16), 'sec').astype(jnp.float32)  50.1 us
    all_gather x1, waiting for transfers between devices, per_device(): lax.all_gather(kv_weight, 'tgt', axis=1, tiled=True)  41.3 us
    another operation x8, local copies, waits for them, and re-layouts, block_step(): jnp.stack([grad_key, grad_value]).reshape(2, SLOTS, BLOCK, width_here)  28.3 us
    ppermute x2, waiting for transfers between devices, from_behind(): return lax.ppermute(block, axis, route)  27.8 us
    dot_general x2, matrix products, block_step(): jnp.einsum('sj,csrx->cjrx', targets, pair_grads, precision=lax.Precision....  26.5 us
    dot_general x1, matrix products, per_device(): jnp.einsum('crx,cnx->rn', grads_half, lax.all_gather(kv_weight, 'tgt', ax...  12.3 us
    slice x4, local copies, waits for them, and re-layouts, block_step(): value_rows = picked[1].reshape(SLOTS * BLOCK, heads_here, HEAD_DIM)  7.31 us
  transfers between devices with their start and end apart: 6, of which 5 were waited for; matrix products, arithmetic and copies ran while one was open for 35% of the time, Pallas kernels for 0%

commit v1 on v0

v1 whole, which is shorter than its diff:
```python
import functools
import math

import jax
import jax.numpy as jnp
from jax import lax
from jax.experimental import pallas as pl
from jax.experimental.pallas import tpu as pltpu
from jax.sharding import PartitionSpec as P

HEAD_DIM = 64
BLOCK = 128
SLOTS = 4
GROUP = 4
AXES = ("tgt", "sec")
SCALE = 0.125
NT = (((1,), (1,)), ((), ()))
TN = (((0,), (0,)), ((), ()))


def send(block, route):
    rows, secs = lax.axis_size("tgt"), lax.axis_size("sec")
    pairs = []
    for t in range(rows):
        for s in range(secs):
            target = route(t, s)
            if target is not None and 0 <= target[0] < rows:
                pairs.append((t * secs + s, target[0] * secs + target[1]))
    return lax.ppermute(block, AXES, pairs)


def swap(block, a):
    return send(block, lambda t, s: (t ^ a, s))


def attend_kernel(meta, pos, *refs):
    pairs, targets = refs[:GROUP], refs[GROUP : 2 * GROUP]
    refs = refs[2 * GROUP :]
    n_halo = (len(refs) - GROUP - 2 - 10) // 2
    halos, refs = refs[:n_halo], refs[n_halo:]
    dq_outs, refs = refs[:GROUP], refs[GROUP:]
    inner, edge, refs = refs[0], refs[1], refs[2:]
    backs, refs = refs[:n_halo], refs[n_halo:]
    keys, values, rows, ups, acc, dq_all, kg, vg, qm, om = refs
    per_dev, width = pairs[0].shape[1], pairs[0].shape[3]
    heads = width // HEAD_DIM
    own = GROUP * per_dev
    here, start = pos[0], pos[1]
    for a in range(GROUP):
        place = pl.ds((here ^ a) * per_dev, per_dev)
        block = (per_dev, BLOCK, width)
        rows[place] = targets[a][: per_dev * BLOCK].reshape(block)
        ups[place] = targets[a][per_dev * BLOCK : 2 * per_dev * BLOCK].reshape(block)
        keys[place] = pairs[a][0]
        values[place] = pairs[a][1]
    for n in range(n_halo):
        part = slice(own + n * per_dev, own + (n + 1) * per_dev)
        keys[part] = halos[n][0]
        values[part] = halos[n][1]
    acc[...] = jnp.zeros_like(acc)
    lane_head = lax.broadcasted_iota(jnp.int32, (BLOCK, width), 1) // HEAD_DIM
    key_row = lax.broadcasted_iota(jnp.int32, (SLOTS * BLOCK, heads * BLOCK), 0)

    def step(i, carry):
        a = here ^ (i // per_dev)
        r = i % per_dev
        count = meta[a, r, SLOTS]
        ids = [meta[a, r, s] for s in range(SLOTS)]
        for s in range(SLOTS):
            kg[s * BLOCK : (s + 1) * BLOCK] = keys[ids[s]]
            vg[s * BLOCK : (s + 1) * BLOCK] = values[ids[s]]
        q, o = rows[i], ups[i]
        for h in range(heads):
            qm[h * BLOCK : (h + 1) * BLOCK] = jnp.where(lane_head == h, q, 0)
            om[h * BLOCK : (h + 1) * BLOCK] = jnp.where(lane_head == h, o, 0)
        scores = lax.dot_general(kg[...], qm[...], NT, preferred_element_type=jnp.float32)
        scores = jnp.where(key_row < count * BLOCK, scores, -jnp.inf)
        top = jnp.max(scores, axis=0, keepdims=True)
        expo = jnp.exp2((scores - top) * (SCALE * math.log2(math.e)))
        probs = expo * (1.0 / jnp.sum(expo, axis=0, keepdims=True))
        probs_half = probs.astype(jnp.bfloat16)
        grad_probs = lax.dot_general(vg[...], om[...], NT, preferred_element_type=jnp.float32)
        delta = jnp.sum(probs_half.astype(jnp.float32) * grad_probs, axis=0, keepdims=True)
        grad_half = (probs * (grad_probs - delta)).astype(jnp.bfloat16)
        grad_value = jnp.dot(probs_half, om[...], preferred_element_type=jnp.float32)
        grad_key = SCALE * jnp.dot(grad_half, qm[...], preferred_element_type=jnp.float32)
        for s in range(SLOTS):
            part = slice(s * BLOCK, (s + 1) * BLOCK)
            acc[0, ids[s]] += grad_key[part]
            acc[1, ids[s]] += grad_value[part]
        flipped = lax.dot_general(kg[...], grad_half, TN, preferred_element_type=jnp.float32)
        flipped = jnp.concatenate(
            [
                flipped[h * HEAD_DIM : (h + 1) * HEAD_DIM, h * BLOCK : (h + 1) * BLOCK]
                for h in range(heads)
            ],
            axis=0,
        )
        dq_all[i] = (SCALE * flipped.T).astype(jnp.bfloat16)
        return carry

    lax.fori_loop(0, own, step, 0)
    for a in range(GROUP):
        dq_outs[a][...] = dq_all[pl.ds((here ^ a) * per_dev, per_dev)]
    half = jnp.bfloat16
    for p in range(GROUP):
        m = lax.rem(start + 1 + p, GROUP)
        taken = acc[:, pl.ds(m * per_dev, per_dev)]
        if p < GROUP - n_halo:
            inner[:, p * per_dev : (p + 1) * per_dev] = taken.astype(half)
        else:
            p -= GROUP - n_halo
            edge[:, p * per_dev : (p + 1) * per_dev] = taken
    for n in range(n_halo):
        part = slice(own + n * per_dev, own + (n + 1) * per_dev)
        backs[n][...] = acc[:, part].astype(half)


def attend(meta, pos, pairs, targets, halos):
    _, per_dev, _, width = pairs[0].shape
    n_halo = len(halos)
    own = GROUP * per_dev
    total = own + n_halo * per_dev
    heads = width // HEAD_DIM
    half = jnp.bfloat16
    block = (BLOCK, width)
    shapes = (
        [jax.ShapeDtypeStruct((per_dev,) + block, half)] * GROUP
        + [
            jax.ShapeDtypeStruct((2, own - n_halo * per_dev) + block, half),
            jax.ShapeDtypeStruct((2, n_halo * per_dev) + block, jnp.float32),
        ]
        + [jax.ShapeDtypeStruct((2, per_dev) + block, half)] * n_halo
    )
    scratch = [
        pltpu.VMEM((total,) + block, half),
        pltpu.VMEM((total,) + block, half),
        pltpu.VMEM((own,) + block, half),
        pltpu.VMEM((own,) + block, half),
        pltpu.VMEM((2, total) + block, jnp.float32),
        pltpu.VMEM((own,) + block, half),
        pltpu.VMEM((SLOTS * BLOCK, width), half),
        pltpu.VMEM((SLOTS * BLOCK, width), half),
        pltpu.VMEM((heads * BLOCK, width), half),
        pltpu.VMEM((heads * BLOCK, width), half),
    ]
    whole = pl.BlockSpec(memory_space=pltpu.VMEM)
    scalars = pl.BlockSpec(memory_space=pltpu.SMEM)
    results = pl.pallas_call(
        attend_kernel,
        out_shape=shapes,
        in_specs=[scalars] * 2 + [whole] * (2 * GROUP + n_halo),
        out_specs=[whole] * len(shapes),
        scratch_shapes=scratch,
        compiler_params=pltpu.CompilerParams(vmem_limit_bytes=40 * 2**20),
        cost_estimate=pl.CostEstimate(
            flops=own * 10 * SLOTS * BLOCK * heads * BLOCK * width,
            bytes_accessed=8 * 2**20,
            transcendentals=own * SLOTS * heads * BLOCK * BLOCK,
        ),
        name="attend",
    )(meta, pos, *pairs, *targets, *halos)
    return results[:GROUP], results[GROUP], results[GROUP + 1], results[GROUP + 2 :]


def project_kernel(ranges, n_out, pos, *refs):
    inner, edge, refs = refs[:GROUP], refs[GROUP : 2 * GROUP], refs[2 * GROUP :]
    weights, refs = refs[: len(ranges)], refs[len(ranges) :]
    outs, (left, result) = refs[:n_out], refs[n_out:]
    width = inner[0].shape[3]
    n_inner, n_edge = inner[0].shape[1], edge[0].shape[1]
    per_dev = (n_inner + n_edge) // GROUP
    rows = per_dev * BLOCK
    depth = GROUP * width
    here, start, flip = pos[0], pos[1], pos[2]

    def step(j, carry):
        p = lax.rem(pos[3 + j] + (GROUP - 1) - start, GROUP) * per_dev

        def fill(sources, first):
            for a in range(GROUP):
                column = (here ^ a) * width
                for c in range(2):
                    piece = sources[a][c, pl.ds(p - first, per_dev)].reshape(rows, width)
                    left[:, pl.ds(pl.multiple_of(c * depth + column, width), width)] = piece

        @pl.when(p < n_inner)
        def _():
            fill(inner, 0)

        @pl.when(p >= n_inner)
        def _():
            fill(edge, n_inner)

        for weight, (k, first, size, column) in zip(weights, ranges):
            total = None
            for c in range(2):
                term = lax.dot_general(
                    left[:, c * depth : (c + 1) * depth],
                    weight[c, first : first + size],
                    NT,
                    preferred_element_type=jnp.float32,
                )
                total = term if total is None else total + term
            result[j, k, :, column : column + size] = total.astype(result.dtype)
        return carry

    lax.fori_loop(0, GROUP, step, 0)
    n_k = n_out // GROUP
    for j in range(GROUP):
        for k in range(n_k):
            outs[j * n_k + k][...] = result[j, (k ^ flip) if n_k == 2 else k]


def project(pos, inner, edge, weights, ranges):
    per_dev = (inner[0].shape[1] + edge[0].shape[1]) // GROUP
    rows = per_dev * BLOCK
    width = inner[0].shape[3]
    whole = pl.BlockSpec(memory_space=pltpu.VMEM)
    columns = max(column + size for _, _, size, column in ranges)
    n_k = max(k for k, _, _, _ in ranges) + 1
    half = jnp.bfloat16
    n_out = n_k * GROUP
    return pl.pallas_call(
        functools.partial(project_kernel, ranges, n_out),
        out_shape=[jax.ShapeDtypeStruct((rows, columns), half)] * n_out,
        in_specs=[pl.BlockSpec(memory_space=pltpu.SMEM)] + [whole] * (2 * GROUP + len(weights)),
        out_specs=[whole] * n_out,
        scratch_shapes=[
            pltpu.VMEM((rows, 2 * GROUP * width), half),
            pltpu.VMEM((GROUP, n_k, rows, columns), half),
        ],
        compiler_params=pltpu.CompilerParams(vmem_limit_bytes=40 * 2**20),
        cost_estimate=pl.CostEstimate(
            flops=4 * n_out * rows * columns * GROUP * width,
            bytes_accessed=8 * 2**20,
            transcendentals=0,
        ),
        name="project",
    )(pos, *inner, *edge, *weights)


def collect_kernel(sizes, pos, *refs):
    out = refs[-1]
    wide = out.shape[1] // 2
    x = pos[0]
    column = 0
    for b, size in enumerate(sizes):
        parts = refs[8 * b : 8 * b + 8]
        for a in range(2):
            total = None
            for n, part in enumerate(parts):
                if (n // 2) % 2 == a:
                    term = part[...].astype(jnp.float32)
                    total = term if total is None else total + term
            place = pl.multiple_of((x ^ a) * wide + column, BLOCK)
            out[:, pl.ds(place, size)] = total.astype(out.dtype)
        column += size


def collect(pos, batches):
    sizes = [batch[0].shape[1] for batch in batches]
    rows = batches[0][0].shape[0]
    whole = pl.BlockSpec(memory_space=pltpu.VMEM)
    return pl.pallas_call(
        functools.partial(collect_kernel, sizes),
        out_shape=jax.ShapeDtypeStruct((rows, 2 * sum(sizes)), jnp.bfloat16),
        in_specs=[pl.BlockSpec(memory_space=pltpu.SMEM)] + [whole] * (8 * len(sizes)),
        out_specs=whole,
        compiler_params=pltpu.CompilerParams(vmem_limit_bytes=16 * 2**20),
        name="collect",
    )(pos, *[part for batch in batches for part in batch])


def place_kernel(pos, *refs):
    out = refs[-1]
    for a, part in enumerate(refs[:-1]):
        rows, width = out.shape[0], part.shape[2]
        start = pl.multiple_of((pos[0] ^ a) * width, width)
        out[:, pl.ds(start, width)] = part[...].reshape(rows, width)


def place_columns(pos, parts):
    per_dev, block, width = parts[0].shape
    whole = pl.BlockSpec(memory_space=pltpu.VMEM)
    return pl.pallas_call(
        place_kernel,
        out_shape=jax.ShapeDtypeStruct((per_dev * block, GROUP * width), parts[0].dtype),
        in_specs=[pl.BlockSpec(memory_space=pltpu.SMEM)] + [whole] * len(parts),
        out_specs=whole,
        name="place_columns",
    )(pos, *parts)


def deliver(parts):
    arrived = []
    for n, part in enumerate(parts):
        a0, a1, a2 = n // 4, (n // 2) % 2, n % 2

        def route(t, s):
            g, z, x = t // GROUP, (t // 2) % 2, t % 2
            y, core = s // 2, s % 2
            return (g * GROUP + 2 * (core ^ a0) + (x ^ a1), 2 * (y ^ a2) + z)

        arrived.append(send(part, route))
    return arrived


def deliver_any(parts, group):
    groups = len(parts)
    secs = lax.axis_size("sec")
    rows, wide = parts[0].shape[1:]
    stacked = jnp.roll(jnp.stack(parts[::-1]), group + 1, axis=0)
    shape = (secs, groups // secs, GROUP, rows, wide)
    mine = lax.psum_scatter(stacked.reshape(shape), "sec", scatter_dimension=0, tiled=False)
    mine = jnp.moveaxis(mine, 1, 0)
    n_tgt = lax.axis_size("tgt")
    lists = [list(range(g, g + GROUP)) for g in range(0, n_tgt, GROUP)]
    mine = lax.all_to_all(mine, "tgt", 0, 0, axis_index_groups=lists)
    return jnp.transpose(mine, (2, 1, 0, 3)).reshape(rows, -1)


def after(block, *earlier):
    return lax.optimization_barrier((block, *earlier))[0]


def per_device(queries, key_values, grad_out, block_ids, block_count, kv_weight):
    rows_here, width_here = queries.shape
    blocks_here = rows_here // BLOCK
    width = width_here // GROUP
    n_tgt = lax.axis_size("tgt")
    groups = n_tgt // GROUP
    paired = groups == 2
    n_halo = 1 if paired else 2
    t, s = lax.axis_index("tgt"), lax.axis_index("sec")
    group, here = t // GROUP, t % GROUP
    start = jnp.where(group == 0, GROUP - 1, 0) if paired else 0

    def other_group(block):
        return send(block, lambda t, s: (t ^ GROUP, s))

    def shifted(block, k):
        return send(block, lambda t, s: (t + GROUP * k, s))

    wide = kv_weight.shape[1]
    if paired:
        cuts = [0, wide // 8, 3 * wide // 8, 3 * wide // 4, wide]
        chunks = [kv_weight[:, lo:hi] for lo, hi in zip(cuts, cuts[1:])]
        chunks[0] = other_group(chunks[0])

    total = (GROUP + n_halo) * blocks_here
    slots = (block_ids - group * GROUP * blocks_here) % total
    listed = jnp.concatenate([slots, block_count[:, None]], axis=1).astype(jnp.bfloat16)
    listed = jnp.pad(listed, ((0, 16 - blocks_here), (0, width - SLOTS - 1)))
    pairs, targets = [], []
    for a in range(GROUP):
        first = (here ^ a) * width
        pair = lax.dynamic_slice_in_dim(key_values, first, width, axis=2)
        pair = pair.reshape(2, blocks_here, BLOCK, width)
        pairs.append(pair if a == 0 else swap(pair, a))
    for a in range(GROUP):
        first = (here ^ a) * width
        target = jnp.concatenate(
            [lax.dynamic_slice_in_dim(part, first, width, axis=1) for part in (queries, grad_out)]
            + [listed]
        )
        targets.append(target if a == 0 else swap(target, a))
    def member(m):
        chosen = pairs[0]
        for a in range(1, GROUP):
            chosen = jnp.where(here ^ a == m, pairs[a], chosen)
        return chosen

    if paired:
        halos = [other_group(member(start))]
        chunks[1] = other_group(after(chunks[1], targets[1]))
    else:
        halos = [shifted(member(0), -1), shifted(member(GROUP - 1), 1)]

    meta = jnp.stack([target[2 * rows_here : 2 * rows_here + blocks_here, : SLOTS + 1] for target in targets])
    pos = jnp.stack([here, start]).astype(jnp.int32)
    dq, inner, edge, backs = attend(meta.astype(jnp.int32), pos, pairs, targets, halos)

    if paired:
        returned = other_group(backs[0])
        chunks[2] = other_group(after(chunks[2], returned))
    else:
        returned = jnp.concatenate([shifted(backs[1], -1), shifted(backs[0], 1)], axis=1)
    edge = (edge + returned.astype(jnp.float32)).astype(jnp.bfloat16)
    inners = [inner] + [swap(inner, a) for a in range(1, GROUP)]
    if paired:
        chunks[3] = other_group(after(chunks[3], inners[1]))
    edges = [edge] + [swap(edge, a) for a in range(1, GROUP)]

    core, y, x = s % 2, s // 2, t % 2
    if paired:
        order = [2 * (core ^ (j // 2)) + (x ^ (j % 2)) for j in range(GROUP)]
        pos = jnp.stack([here, start, y ^ group] + order).astype(jnp.int32)
        cut = cuts[3]
        ranges = [(0, 0, cut, 0)] + [(1, 0, hi - lo, lo) for lo, hi in zip(cuts[:3], cuts[1:4])]
        batch = deliver(project(pos, inners, edges, [kv_weight] + chunks[:3], ranges))
        ranges = [(0, cut, wide - cut, 0), (1, 0, wide - cut, 0)]
        last = deliver(project(pos, inners, edges, [kv_weight, chunks[3]], ranges))
        grad_memory = collect(x.astype(jnp.int32).reshape(1), [batch, last])
    else:
        pos = jnp.stack([here, start, 0] + list(range(GROUP))).astype(jnp.int32)
        weights = [kv_weight] + [
            send(kv_weight, lambda t, s, k=k: ((t + GROUP * k) % n_tgt, s))
            for k in range(1, groups)
        ]
        parts = [project(pos, inners, edges, [w], [(0, 0, wide, 0)]) for w in weights]
        grad_memory = deliver_any([jnp.stack(part) for part in parts], group)

    dq = [dq[0]] + [swap(dq[a], a) for a in range(1, GROUP)]
    return place_columns(here.astype(jnp.int32).reshape(1), dq), grad_memory


def solution(mesh):
    return jax.shard_map(
        per_device,
        mesh=mesh,
        in_specs=(
            P("tgt", "sec"),
            P(None, "tgt", "sec"),
            P("tgt", "sec"),
            P("tgt", None),
            P("tgt"),
            P(None, "tgt", "sec"),
        ),
        out_specs=(P("tgt", "sec"), P("tgt", "sec")),
        check_vma=False,
    )
```

time: 354 us -> 221 us (0.62)
  waiting for transfers between devices: 182 us -> 109 us
  matrix products: 64.1 us -> 0 us
  local copies, waits for them, and re-layouts: 67.4 us -> 27.2 us
  starting transfers between devices: 12.2 us -> 50.6 us
  Pallas kernels: 0 us -> 30.5 us
  between operations: 14.1 us -> 0.92 us
  other arithmetic: 12.3 us -> 2.66 us
    dot_general x13 -> x0, matrix products: 57.4 us -> none  [the longest x2 26.5 us: block_step(): jnp.einsum('sj,csrx->cjrx', targets, pair_grads, precision=lax.Precision....]
    psum x1 -> x0, waiting for transfers between devices: 50.1 us -> none  [per_device(): lax.psum(partial_memory.astype(jnp.bfloat16), 'sec').astype(jnp.float32)]
    all_gather x1 -> x0, waiting for transfers between devices: 41.3 us -> none  [per_device(): lax.all_gather(kv_weight, 'tgt', axis=1, tiled=True)]
    ppermute x4 -> x37, starting transfers between devices: 12.2 us -> 50.6 us  [send(): return lax.ppermute(block, AXES, pairs)]
    pallas_call x0 -> x5, Pallas kernels: none -> 30.5 us  [the longest x2 14.6 us: project(): pl.pallas_call(functools.partial(project_kernel, ranges, n_out), out_shap...]
    another operation x8 -> x4, local copies, waits for them, and re-layouts: 28.3 us -> 1.4 us  [the longest x3 1.31 us: per_device(): jnp.stack([target[2 * rows_here:2 * rows_here + blocks_here, :SLOTS + 1]...]
    unnamed x4 -> x74, local copies, waits for them, and re-layouts: 2.17 us -> 21.2 us
    ppermute x4 -> x37, waiting for transfers between devices: 90.2 us -> 109 us  [send(): return lax.ppermute(block, AXES, pairs)]
  transfers between devices with their start and end apart: 6 -> 37, of which waited for: 5 -> 9; matrix products, arithmetic and copies ran while one was open for 35% -> 2% of each run, Pallas kernels for 0% -> 13%
where the time goes in v1:
time: 221 us; the launch traced here: 220 us
  waiting for transfers between devices  109 us (49%)
  starting transfers between devices  50.6 us (23%)
  Pallas kernels  30.5 us (14%)
  local copies, waits for them, and re-layouts  27.2 us (12%)
  other arithmetic  2.66 us (1%)
    ppermute x37, waiting for transfers between devices, send(): return lax.ppermute(block, AXES, pairs)  109 us
    ppermute x37, starting transfers between devices, send(): return lax.ppermute(block, AXES, pairs)  50.6 us
    unnamed x74, local copies, waits for them, and re-layouts  21.2 us
    pallas_call x2, Pallas kernels, project(): pl.pallas_call(functools.partial(project_kernel, ranges, n_out), out_shap...  14.6 us
    pallas_call x1, Pallas kernels, attend(): pl.pallas_call(attend_kernel, out_shape=shapes, in_specs=[scalars] * 2 +...  12.9 us
  transfers between devices with their start and end apart: 37, of which 9 were waited for; matrix products, arithmetic and copies ran while one was open for 2% of the time, Pallas kernels for 13%

profile of v1, /device:TPU:0, one launch (start us, length us, event | category | flops | bytes accessed | tf_op | source)
XLA Modules:
  0.0 220.4 jit_solution(1323759605398779101)
XLA Ops:
  2.2 1.4 constant_dynamic-slice_fusion
  4.6 3.0 %collective-permute-start.1 = (bf16[528,256]{1,0:T(8,128)(2,1)}, bf16[528,256]{1,0:T(8,128)(2,1)}, u32[]{:S(2)}, u32[]{:S(2)}) collective-permute-start(bf16[528,256]{1,0:T(8,128)(2,1)} %get-tuple-element.69), channel_id=1, source_target_pairs={{0,8},{1,9},{2,10},{3,11},{4,12},{5,13},{6,14},{7,15},{8,0},{9,1},... | collective-permute-start | bytes 811016 | tf_op jit(solution)/shard_map/ppermute | solution.py:29
  7.6 1.5 collective-permute-start
  10.6 1.4 collective-permute-start.5
  12.0 1.6 collective-permute-start.4
  14.8 12.2 %collective-permute-done.3.refs_1_ = bf16[2,2,128,256]{3,2,1,0:T(8,128)(2,1)S(1)} collective-permute-done((bf16[2,2,128,256]{3,2,1,0:T(8,128)(2,1)}, bf16[2,2,128,256]{3,2,1,0:T(8,128)(2,1)S(1)}, u32[]{:S(2)}, u32[]{:S(2)}) %collective-permute-start.3) | collective-permute-done | bytes 262176 | tf_op jit(solution)/shard_map/ppermute | solution.py:29
  27.0 1.4 collective-permute-start.2
  28.5 2.7 %collective-permute-start.6 = (bf16[2,2,128,256]{3,2,1,0:T(8,128)(2,1)S(1)}, bf16[2,2,128,256]{3,2,1,0:T(8,128)(2,1)S(1)}, u32[]{:S(2)}, u32[]{:S(2)}) collective-permute-start(bf16[2,2,128,256]{3,2,1,0:T(8,128)(2,1)S(1)} %select_select_fusion), channel_id=1, source_target_pairs={{0,16},{1,17},{2,18},{3,19},{4,20},{5,21},{6,22},{7,23},{8,24},{9,... | collective-permute-start | bytes 786440 | tf_op jit(solution)/shard_map/ppermute | solution.py:29
  32.8 9.1 %collective-permute-done.2.refs_7_ = bf16[528,256]{1,0:T(8,128)(2,1)S(1)} collective-permute-done((bf16[528,256]{1,0:T(8,128)(2,1)}, bf16[528,256]{1,0:T(8,128)(2,1)S(1)}, u32[]{:S(2)}, u32[]{:S(2)}) %collective-permute-start.2) | collective-permute-done | bytes 270368 | tf_op jit(solution)/shard_map/ppermute | solution.py:29
  42.0 13.6 %collective-permute-done.6.refs_8_ = bf16[2,2,128,256]{3,2,1,0:T(8,128)(2,1)S(1)} collective-permute-done((bf16[2,2,128,256]{3,2,1,0:T(8,128)(2,1)S(1)}, bf16[2,2,128,256]{3,2,1,0:T(8,128)(2,1)S(1)}, u32[]{:S(2)}, u32[]{:S(2)}) %collective-permute-start.6) | collective-permute-done | bytes 262176 | tf_op jit(solution)/shard_map/ppermute | solution.py:29
  58.4 12.9 %attend.1 = (bf16[2,128,256]{2,1,0:T(8,128)(2,1)S(1)}, bf16[2,128,256]{2,1,0:T(8,128)(2,1)S(1)}, bf16[2,128,256]{2,1,0:T(8,128)(2,1)S(1)}, bf16[2,128,256]{2,1,0...) custom-call(s32[4,2,5]{2,1,0:T(2,128)S(1)} %maximum_convert_fusion.m, ...), custom_call_target="tpu_custom_call" | custom-call | flops 5368709120 | bytes 8388608 | tf_op jit(solution)/shard_map/attend/pallas_call | solution.py:149
  72.3 3.0 %collective-permute-start.17 = (bf16[2,64,1024]{2,1,0:T(8,128)(2,1)S(1)}, bf16[2,64,1024]{2,1,0:T(8,128)(2,1)S(1)}, u32[]{:S(2)}, u32[]{:S(2)}) collective-permute-start(bf16[2,64,1024]{2,1,0:T(8,128)(2,1)S(1)} %slice.25), channel_id=1, source_target_pairs={{0,16},{1,17},{2,18},{3,19},{4,20},{5,21},{6,22},{7,23},{8,24},{9,... | collective-permute-start | bytes 786440 | tf_op jit(solution)/shard_map/ppermute | solution.py:29
  76.2 1.6 collective-permute-start.12
  77.8 10.3 %collective-permute-done.13 = bf16[2,2,128,256]{3,2,1,0:T(8,128)(2,1)S(1)} collective-permute-done((bf16[2,2,128,256]{3,2,1,0:T(8,128)(2,1)S(1)}, bf16[2,2,128,256]{3,2,1,0:T(8,128)(2,1)S(1)}, u32[]{:S(2)}, u32[]{:S(2)}) %collective-permute-start.13) | collective-permute-done | bytes 262176 | tf_op jit(solution)/shard_map/ppermute | solution.py:29
  88.1 5.8 %collective-permute-done.17.refs_9_ = bf16[2,64,1024]{2,1,0:T(8,128)(2,1)S(1)} collective-permute-done((bf16[2,64,1024]{2,1,0:T(8,128)(2,1)S(1)}, bf16[2,64,1024]{2,1,0:T(8,128)(2,1)S(1)}, u32[]{:S(2)}, u32[]{:S(2)}) %collective-permute-start.17) | collective-permute-done | bytes 262176 | tf_op jit(solution)/shard_map/ppermute | solution.py:29
  95.5 42.8 %collective-permute-done.16.refs_7_ = bf16[2,2,128,256]{3,2,1,0:T(8,128)(2,1)S(1)} collective-permute-done((bf16[2,2,128,256]{3,2,1,0:T(8,128)(2,1)S(1)}, bf16[2,2,128,256]{3,2,1,0:T(8,128)(2,1)S(1)}, u32[]{:S(2)}, u32[]{:S(2)}) %collective-permute-start.16) | collective-permute-done | bytes 262176 | tf_op jit(solution)/shard_map/ppermute | solution.py:29
  140.4 2.5 %collective-permute-start.14 = (bf16[2,2,128,256]{3,2,1,0:T(8,128)(2,1)S(1)}, bf16[2,2,128,256]{3,2,1,0:T(8,128)(2,1)}, u32[]{:S(2)}, u32[]{:S(2)}) collective-permute-start(bf16[2,2,128,256]{3,2,1,0:T(8,128)(2,1)S(1)} %add_convert_fusion.refs_4_), channel_id=1, source_target_pairs={{0,4},{1,5},{2,6},{3,7},{4,0},{5,1},{6,2},{7,3},{8,12},{9,13},{10,... | collective-permute-start | bytes 786440 | tf_op jit(solution)/shard_map/ppermute | solution.py:29
  143.0 3.2 %collective-permute-done.15.refs_6_ = bf16[2,2,128,256]{3,2,1,0:T(8,128)(2,1)} collective-permute-done((bf16[2,2,128,256]{3,2,1,0:T(8,128)(2,1)S(1)}, bf16[2,2,128,256]{3,2,1,0:T(8,128)(2,1)}, u32[]{:S(2)}, u32[]{:S(2)}) %collective-permute-start.15) | collective-permute-done | bytes 262176 | tf_op jit(solution)/shard_map/ppermute | solution.py:29
  146.2 1.7 collective-permute-start.7
  147.9 2.0 collective-permute-start.8
  149.9 2.7 %collective-permute-start.28 = (bf16[2,128,1024]{2,1,0:T(8,128)(2,1)}, bf16[2,128,1024]{2,1,0:T(8,128)(2,1)S(1)}, u32[]{:S(2)}, u32[]{:S(2)}) collective-permute-start(bf16[2,128,1024]{2,1,0:T(8,128)(2,1)} %get-tuple-element.45), channel_id=1, source_target_pairs={{0,16},{1,17},{2,18},{3,19},{4,20},{5,21},{6,22},{7,23},{8,24},{9,... | collective-permute-start | bytes 1572872 | tf_op jit(solution)/shard_map/ppermute | solution.py:29
  155.8 8.9 %project.2 = (bf16[256,384]{1,0:T(8,128)(2,1)S(1)}, bf16[256,384]{1,0:T(8,128)(2,1)S(1)}, bf16[256,384]{1,0:T(8,128)(2,1)S(1)}, bf16[256,384]{1,0:T(8,128)(2,1)S...) custom-call(s32[7]{0:T(128)S(1)} %stack.51.pos, ...), custom_call_target="tpu_custom_call" | custom-call | flops 3221225472 | bytes 8388608 | tf_op jit(solution)/shard_map/project/pallas_call | solution.py:224
  165.4 1.6 collective-permute-start.21
  167.9 3.9 %collective-permute-start.9 = (bf16[2,128,256]{2,1,0:T(8,128)(2,1)S(1)}, bf16[2,128,256]{2,1,0:T(8,128)(2,1)S(1)}, u32[]{:S(2)}, u32[]{:S(2)}) collective-permute-start(bf16[2,128,256]{2,1,0:T(8,128)(2,1)S(1)} %get-tuple-element.31), channel_id=1, source_target_pairs={{0,12},{1,13},{2,14},{3,15},{4,8},{5,9},{6,10},{7,11},{8,4},{9,5},... | collective-permute-start | bytes 393224 | tf_op jit(solution)/shard_map/ppermute | solution.py:29
  171.8 8.5 %collective-permute-done.9.refs_3_ = bf16[2,128,256]{2,1,0:T(8,128)(2,1)S(1)} collective-permute-done((bf16[2,128,256]{2,1,0:T(8,128)(2,1)S(1)}, bf16[2,128,256]{2,1,0:T(8,128)(2,1)S(1)}, u32[]{:S(2)}, u32[]{:S(2)}) %collective-permute-start.9) | collective-permute-done | bytes 131104 | tf_op jit(solution)/shard_map/ppermute | solution.py:29
  180.3 2.4 %collective-permute-start.23 = (bf16[256,384]{1,0:T(8,128)(2,1)S(1)}, bf16[256,384]{1,0:T(8,128)(2,1)S(1)}, u32[]{:S(2)}, u32[]{:S(2)}) collective-permute-start(bf16[256,384]{1,0:T(8,128)(2,1)S(1)} %get-tuple-element.40), channel_id=1, source_target_pairs={{0,6},{1,14},{2,4},{3,12},{4,2},{5,10},{6,0},{7,8},{8,7},{9,15},{1... | collective-permute-start | bytes 589832 | tf_op jit(solution)/shard_map/ppermute | solution.py:29
  185.0 3.3 %collective-permute-start.27 = (bf16[256,384]{1,0:T(8,128)(2,1)S(1)}, bf16[256,384]{1,0:T(8,128)(2,1)S(1)}, u32[]{:S(2)}, u32[]{:S(2)}) collective-permute-start(bf16[256,384]{1,0:T(8,128)(2,1)S(1)} %get-tuple-element.44), channel_id=1, source_target_pairs={{0,14},{1,6},{2,12},{3,4},{4,10},{5,2},{6,8},{7,0},{8,15},{9,7},{1... | collective-permute-start | bytes 589832 | tf_op jit(solution)/shard_map/ppermute | solution.py:29
  188.3 5.7 %project.3 = (bf16[256,128]{1,0:T(8,128)(2,1)S(1)}, bf16[256,128]{1,0:T(8,128)(2,1)S(1)}, bf16[256,128]{1,0:T(8,128)(2,1)S(1)}, bf16[256,128]{1,0:T(8,128)(2,1)}...) custom-call(s32[7]{0:T(128)S(1)} %stack.51.pos, ...), custom_call_target="tpu_custom_call" | custom-call | flops 1073741824 | bytes 8388608 | tf_op jit(solution)/shard_map/project/pallas_call | solution.py:224
  198.5 2.4 %collective-permute-start.32 = (bf16[256,128]{1,0:T(8,128)(2,1)}, bf16[256,128]{1,0:T(8,128)(2,1)S(1)}, u32[]{:S(2)}, u32[]{:S(2)}) collective-permute-start(bf16[256,128]{1,0:T(8,128)(2,1)} %get-tuple-element.49), channel_id=1, source_target_pairs={{0,6},{1,14},{2,4},{3,12},{4,2},{5,10},{6,0},{7,8},{8,7},{9,15},{1... | collective-permute-start | bytes 196616 | tf_op jit(solution)/shard_map/ppermute | solution.py:29
  201.6 3.3 %collective-permute-start.33 = (bf16[256,128]{1,0:T(8,128)(2,1)}, bf16[256,128]{1,0:T(8,128)(2,1)S(1)}, u32[]{:S(2)}, u32[]{:S(2)}) collective-permute-start(bf16[256,128]{1,0:T(8,128)(2,1)} %get-tuple-element.50), channel_id=1, source_target_pairs={{0,8},{1,0},{2,10},{3,2},{4,12},{5,4},{6,14},{7,6},{8,9},{9,1},{10... | collective-permute-start | bytes 196616 | tf_op jit(solution)/shard_map/ppermute | solution.py:29
  207.0 2.0 place_columns.1
  208.9 3.0 %collective-permute-done.36.refs_15_ = bf16[256,128]{1,0:T(8,128)(2,1)S(1)} collective-permute-done((bf16[256,128]{1,0:T(8,128)(2,1)}, bf16[256,128]{1,0:T(8,128)(2,1)S(1)}, u32[]{:S(2)}, u32[]{:S(2)}) %collective-permute-start.36) | collective-permute-done | bytes 65568 | tf_op jit(solution)/shard_map/ppermute | solution.py:29
  (141 shorter events, 38.2 us)
Async XLA Ops:
  4.6 27.5 %collective-permute-start.1 = (bf16[528,256]{1,0:T(8,128)(2,1)}, bf16[528,256]{1,0:T(8,128)(2,1)}, u32[]{:S(2)}, u32[]{:S(2)}) collective-permute-start(bf16[528,256]{1,0:T(8,128)(2,1)} %get-tuple-element.69), channel_id=1, source_target_pairs={{0,8},{1,9},{2,10},{3,11},{4,12},{5,13},{6,14},{7,15},{8,0},{9,1},... | collective-permute-start | bytes 811016 | tf_op jit(solution)/shard_map/ppermute | solution.py:29
  7.6 23.5 %collective-permute-start = (bf16[528,256]{1,0:T(8,128)(2,1)}, bf16[528,256]{1,0:T(8,128)(2,1)}, u32[]{:S(2)}, u32[]{:S(2)}) collective-permute-start(bf16[528,256]{1,0:T(8,128)(2,1)} %get-tuple-element.71), channel_id=1, source_target_pairs={{0,4},{1,5},{2,6},{3,7},{4,0},{5,1},{6,2},{7,3},{8,12},{9,13},{10,... | collective-permute-start | bytes 811016 | tf_op jit(solution)/shard_map/ppermute | solution.py:29
  10.1 17.0 %collective-permute-start.3 = (bf16[2,2,128,256]{3,2,1,0:T(8,128)(2,1)}, bf16[2,2,128,256]{3,2,1,0:T(8,128)(2,1)S(1)}, u32[]{:S(2)}, u32[]{:S(2)}) collective-permute-start(bf16[2,2,128,256]{3,2,1,0:T(8,128)(2,1)} %bitcast.9), channel_id=1, source_target_pairs={{0,4},{1,5},{2,6},{3,7},{4,0},{5,1},{6,2},{7,3},{8,12},{9,13},{10,... | collective-permute-start | bytes 786440 | tf_op jit(solution)/shard_map/ppermute | solution.py:29
  10.6 17.8 %collective-permute-start.5 = (bf16[2,2,128,256]{3,2,1,0:T(8,128)(2,1)}, bf16[2,2,128,256]{3,2,1,0:T(8,128)(2,1)S(1)}, u32[]{:S(2)}, u32[]{:S(2)}) collective-permute-start(bf16[2,2,128,256]{3,2,1,0:T(8,128)(2,1)} %bitcast.11), channel_id=1, source_target_pairs={{0,12},{1,13},{2,14},{3,15},{4,8},{5,9},{6,10},{7,11},{8,4},{9,5},... | collective-permute-start | bytes 786440 | tf_op jit(solution)/shard_map/ppermute | solution.py:29
  12.0 16.4 %collective-permute-start.4 = (bf16[2,2,128,256]{3,2,1,0:T(8,128)(2,1)}, bf16[2,2,128,256]{3,2,1,0:T(8,128)(2,1)S(1)}, u32[]{:S(2)}, u32[]{:S(2)}) collective-permute-start(bf16[2,2,128,256]{3,2,1,0:T(8,128)(2,1)} %bitcast.10), channel_id=1, source_target_pairs={{0,8},{1,9},{2,10},{3,11},{4,12},{5,13},{6,14},{7,15},{8,0},{9,1},... | collective-permute-start | bytes 786440 | tf_op jit(solution)/shard_map/ppermute | solution.py:29
  27.0 14.9 %collective-permute-start.2 = (bf16[528,256]{1,0:T(8,128)(2,1)}, bf16[528,256]{1,0:T(8,128)(2,1)S(1)}, u32[]{:S(2)}, u32[]{:S(2)}) collective-permute-start(bf16[528,256]{1,0:T(8,128)(2,1)} %get-tuple-element.70), channel_id=1, source_target_pairs={{0,12},{1,13},{2,14},{3,15},{4,8},{5,9},{6,10},{7,11},{8,4},{9,5},... | collective-permute-start | bytes 811016 | tf_op jit(solution)/shard_map/ppermute | solution.py:29
  28.5 27.1 %collective-permute-start.6 = (bf16[2,2,128,256]{3,2,1,0:T(8,128)(2,1)S(1)}, bf16[2,2,128,256]{3,2,1,0:T(8,128)(2,1)S(1)}, u32[]{:S(2)}, u32[]{:S(2)}) collective-permute-start(bf16[2,2,128,256]{3,2,1,0:T(8,128)(2,1)S(1)} %select_select_fusion), channel_id=1, source_target_pairs={{0,16},{1,17},{2,18},{3,19},{4,20},{5,21},{6,22},{7,23},{8,24},{9,... | collective-permute-start | bytes 786440 | tf_op jit(solution)/shard_map/ppermute | solution.py:29
  31.2 63.6 %collective-permute-start.18 = (bf16[2,128,1024]{2,1,0:T(8,128)(2,1)}, bf16[2,128,1024]{2,1,0:T(8,128)(2,1)S(1)}, u32[]{:S(2)}, u32[]{:S(2)}) collective-permute-start(bf16[2,128,1024]{2,1,0:T(8,128)(2,1)} %get-tuple-element.35), channel_id=1, source_target_pairs={{0,16},{1,17},{2,18},{3,19},{4,20},{5,21},{6,22},{7,23},{8,24},{9,... | collective-permute-start | bytes 1572872 | tf_op jit(solution)/shard_map/ppermute | solution.py:29
  71.9 67.6 %collective-permute-start.10 = (bf16[2,6,128,256]{3,2,1,0:T(8,128)(2,1)S(1)}, bf16[2,6,128,256]{3,2,1,0:T(8,128)(2,1)S(1)}, u32[]{:S(2)}, u32[]{:S(2)}) collective-permute-start(bf16[2,6,128,256]{3,2,1,0:T(8,128)(2,1)S(1)} %get-tuple-element.32.refs_0_), channel_id=1, source_target_pairs={{0,4},{1,5},{2,6},{3,7},{4,0},{5,1},{6,2},{7,3},{8,12},{9,13},{10,... | collective-permute-start | bytes 2359304 | tf_op jit(solution)/shard_map/ppermute | solution.py:29
  72.3 15.8 %collective-permute-start.13 = (bf16[2,2,128,256]{3,2,1,0:T(8,128)(2,1)S(1)}, bf16[2,2,128,256]{3,2,1,0:T(8,128)(2,1)S(1)}, u32[]{:S(2)}, u32[]{:S(2)}) collective-permute-start(bf16[2,2,128,256]{3,2,1,0:T(8,128)(2,1)S(1)} %get-tuple-element.34), channel_id=1, source_target_pairs={{0,16},{1,17},{2,18},{3,19},{4,20},{5,21},{6,22},{7,23},{8,24},{9,... | collective-permute-start | bytes 786440 | tf_op jit(solution)/shard_map/ppermute | solution.py:29
  72.3 21.6 %collective-permute-start.17 = (bf16[2,64,1024]{2,1,0:T(8,128)(2,1)S(1)}, bf16[2,64,1024]{2,1,0:T(8,128)(2,1)S(1)}, u32[]{:S(2)}, u32[]{:S(2)}) collective-permute-start(bf16[2,64,1024]{2,1,0:T(8,128)(2,1)S(1)} %slice.25), channel_id=1, source_target_pairs={{0,16},{1,17},{2,18},{3,19},{4,20},{5,21},{6,22},{7,23},{8,24},{9,... | collective-permute-start | bytes 786440 | tf_op jit(solution)/shard_map/ppermute | solution.py:29
  76.2 73.7 %collective-permute-start.12 = (bf16[2,6,128,256]{3,2,1,0:T(8,128)(2,1)S(1)}, bf16[2,6,128,256]{3,2,1,0:T(8,128)(2,1)}, u32[]{:S(2)}, u32[]{:S(2)}) collective-permute-start(bf16[2,6,128,256]{3,2,1,0:T(8,128)(2,1)S(1)} %get-tuple-element.32.refs_0_), channel_id=1, source_target_pairs={{0,12},{1,13},{2,14},{3,15},{4,8},{5,9},{6,10},{7,11},{8,4},{9,5},... | collective-permute-start | bytes 2359304 | tf_op jit(solution)/shard_map/ppermute | solution.py:29
  88.1 64.5 %collective-permute-start.11 = (bf16[2,6,128,256]{3,2,1,0:T(8,128)(2,1)S(1)}, bf16[2,6,128,256]{3,2,1,0:T(8,128)(2,1)}, u32[]{:S(2)}, u32[]{:S(2)}) collective-permute-start(bf16[2,6,128,256]{3,2,1,0:T(8,128)(2,1)S(1)} %get-tuple-element.32.refs_0_), channel_id=1, source_target_pairs={{0,8},{1,9},{2,10},{3,11},{4,12},{5,13},{6,14},{7,15},{8,0},{9,1},... | collective-permute-start | bytes 2359304 | tf_op jit(solution)/shard_map/ppermute | solution.py:29
  94.7 58.0 %collective-permute-start.19 = (bf16[2,192,1024]{2,1,0:T(8,128)(2,1)}, bf16[2,192,1024]{2,1,0:T(8,128)(2,1)}, u32[]{:S(2)}, u32[]{:S(2)}) collective-permute-start(bf16[2,192,1024]{2,1,0:T(8,128)(2,1)} %slice.27), channel_id=1, source_target_pairs={{0,16},{1,17},{2,18},{3,19},{4,20},{5,21},{6,22},{7,23},{8,24},{9,... | collective-permute-start | bytes 2359304 | tf_op jit(solution)/shard_map/ppermute | solution.py:29
  95.5 42.8 %collective-permute-start.16 = (bf16[2,2,128,256]{3,2,1,0:T(8,128)(2,1)S(1)}, bf16[2,2,128,256]{3,2,1,0:T(8,128)(2,1)S(1)}, u32[]{:S(2)}, u32[]{:S(2)}) collective-permute-start(bf16[2,2,128,256]{3,2,1,0:T(8,128)(2,1)S(1)} %add_convert_fusion.refs_4_), channel_id=1, source_target_pairs={{0,12},{1,13},{2,14},{3,15},{4,8},{5,9},{6,10},{7,11},{8,4},{9,5},... | collective-permute-start | bytes 786440 | tf_op jit(solution)/shard_map/ppermute | solution.py:29
  138.3 7.9 %collective-permute-start.15 = (bf16[2,2,128,256]{3,2,1,0:T(8,128)(2,1)S(1)}, bf16[2,2,128,256]{3,2,1,0:T(8,128)(2,1)}, u32[]{:S(2)}, u32[]{:S(2)}) collective-permute-start(bf16[2,2,128,256]{3,2,1,0:T(8,128)(2,1)S(1)} %add_convert_fusion.refs_4_), channel_id=1, source_target_pairs={{0,8},{1,9},{2,10},{3,11},{4,12},{5,13},{6,14},{7,15},{8,0},{9,1},... | collective-permute-start | bytes 786440 | tf_op jit(solution)/shard_map/ppermute | solution.py:29
  146.2 20.7 %collective-permute-start.7 = (bf16[2,128,256]{2,1,0:T(8,128)(2,1)}, bf16[2,128,256]{2,1,0:T(8,128)(2,1)S(1)}, u32[]{:S(2)}, u32[]{:S(2)}) collective-permute-start(bf16[2,128,256]{2,1,0:T(8,128)(2,1)} %copy-done.31), channel_id=1, source_target_pairs={{0,4},{1,5},{2,6},{3,7},{4,0},{5,1},{6,2},{7,3},{8,12},{9,13},{10,... | collective-permute-start | bytes 393224 | tf_op jit(solution)/shard_map/ppermute | solution.py:29
  147.9 20.0 %collective-permute-start.8 = (bf16[2,128,256]{2,1,0:T(8,128)(2,1)}, bf16[2,128,256]{2,1,0:T(8,128)(2,1)S(1)}, u32[]{:S(2)}, u32[]{:S(2)}) collective-permute-start(bf16[2,128,256]{2,1,0:T(8,128)(2,1)} %copy-done.30), channel_id=1, source_target_pairs={{0,8},{1,9},{2,10},{3,11},{4,12},{5,13},{6,14},{7,15},{8,0},{9,1},... | collective-permute-start | bytes 393224 | tf_op jit(solution)/shard_map/ppermute | solution.py:29
  149.9 35.1 %collective-permute-start.28 = (bf16[2,128,1024]{2,1,0:T(8,128)(2,1)}, bf16[2,128,1024]{2,1,0:T(8,128)(2,1)S(1)}, u32[]{:S(2)}, u32[]{:S(2)}) collective-permute-start(bf16[2,128,1024]{2,1,0:T(8,128)(2,1)} %get-tuple-element.45), channel_id=1, source_target_pairs={{0,16},{1,17},{2,18},{3,19},{4,20},{5,21},{6,22},{7,23},{8,24},{9,... | collective-permute-start | bytes 1572872 | tf_op jit(solution)/shard_map/ppermute | solution.py:29
  164.7 18.0 %collective-permute-start.20 = (bf16[256,384]{1,0:T(8,128)(2,1)S(1)}, bf16[256,384]{1,0:T(8,128)(2,1)S(1)}, u32[]{:S(2)}, u32[]{:S(2)}) collective-permute-start(bf16[256,384]{1,0:T(8,128)(2,1)S(1)} %get-tuple-element.37), channel_id=1, source_target_pairs={{0,0},{1,8},{2,2},{3,10},{4,4},{5,12},{6,6},{7,14},{8,1},{9,9},{10... | collective-permute-start | bytes 589832 | tf_op jit(solution)/shard_map/ppermute | solution.py:29
  165.4 17.4 %collective-permute-start.21 = (bf16[256,384]{1,0:T(8,128)(2,1)S(1)}, bf16[256,384]{1,0:T(8,128)(2,1)S(1)}, u32[]{:S(2)}, u32[]{:S(2)}) collective-permute-start(bf16[256,384]{1,0:T(8,128)(2,1)S(1)} %get-tuple-element.38), channel_id=1, source_target_pairs={{0,2},{1,10},{2,0},{3,8},{4,6},{5,14},{6,4},{7,12},{8,3},{9,11},{1... | collective-permute-start | bytes 589832 | tf_op jit(solution)/shard_map/ppermute | solution.py:29
  167.0 16.5 %collective-permute-start.22 = (bf16[256,384]{1,0:T(8,128)(2,1)S(1)}, bf16[256,384]{1,0:T(8,128)(2,1)S(1)}, u32[]{:S(2)}, u32[]{:S(2)}) collective-permute-start(bf16[256,384]{1,0:T(8,128)(2,1)S(1)} %get-tuple-element.39), channel_id=1, source_target_pairs={{0,4},{1,12},{2,6},{3,14},{4,0},{5,8},{6,2},{7,10},{8,5},{9,13},{1... | collective-permute-start | bytes 589832 | tf_op jit(solution)/shard_map/ppermute | solution.py:29
  167.9 12.5 %collective-permute-start.9 = (bf16[2,128,256]{2,1,0:T(8,128)(2,1)S(1)}, bf16[2,128,256]{2,1,0:T(8,128)(2,1)S(1)}, u32[]{:S(2)}, u32[]{:S(2)}) collective-permute-start(bf16[2,128,256]{2,1,0:T(8,128)(2,1)S(1)} %get-tuple-element.31), channel_id=1, source_target_pairs={{0,12},{1,13},{2,14},{3,15},{4,8},{5,9},{6,10},{7,11},{8,4},{9,5},... | collective-permute-start | bytes 393224 | tf_op jit(solution)/shard_map/ppermute | solution.py:29
  180.3 13.7 %collective-permute-start.23 = (bf16[256,384]{1,0:T(8,128)(2,1)S(1)}, bf16[256,384]{1,0:T(8,128)(2,1)S(1)}, u32[]{:S(2)}, u32[]{:S(2)}) collective-permute-start(bf16[256,384]{1,0:T(8,128)(2,1)S(1)} %get-tuple-element.40), channel_id=1, source_target_pairs={{0,6},{1,14},{2,4},{3,12},{4,2},{5,10},{6,0},{7,8},{8,7},{9,15},{1... | collective-permute-start | bytes 589832 | tf_op jit(solution)/shard_map/ppermute | solution.py:29
  182.7 12.6 %collective-permute-start.24 = (bf16[256,384]{1,0:T(8,128)(2,1)S(1)}, bf16[256,384]{1,0:T(8,128)(2,1)S(1)}, u32[]{:S(2)}, u32[]{:S(2)}) collective-permute-start(bf16[256,384]{1,0:T(8,128)(2,1)S(1)} %get-tuple-element.41), channel_id=1, source_target_pairs={{0,8},{1,0},{2,10},{3,2},{4,12},{5,4},{6,14},{7,6},{8,9},{9,1},{10... | collective-permute-start | bytes 589832 | tf_op jit(solution)/shard_map/ppermute | solution.py:29
  183.5 13.0 %collective-permute-start.25 = (bf16[256,384]{1,0:T(8,128)(2,1)S(1)}, bf16[256,384]{1,0:T(8,128)(2,1)S(1)}, u32[]{:S(2)}, u32[]{:S(2)}) collective-permute-start(bf16[256,384]{1,0:T(8,128)(2,1)S(1)} %get-tuple-element.42), channel_id=1, source_target_pairs={{0,10},{1,2},{2,8},{3,0},{4,14},{5,6},{6,12},{7,4},{8,11},{9,3},{1... | collective-permute-start | bytes 589832 | tf_op jit(solution)/shard_map/ppermute | solution.py:29
  184.2 13.7 %collective-permute-start.26 = (bf16[256,384]{1,0:T(8,128)(2,1)S(1)}, bf16[256,384]{1,0:T(8,128)(2,1)S(1)}, u32[]{:S(2)}, u32[]{:S(2)}) collective-permute-start(bf16[256,384]{1,0:T(8,128)(2,1)S(1)} %get-tuple-element.43), channel_id=1, source_target_pairs={{0,12},{1,4},{2,14},{3,6},{4,8},{5,0},{6,10},{7,2},{8,13},{9,5},{1... | collective-permute-start | bytes 589832 | tf_op jit(solution)/shard_map/ppermute | solution.py:29
  185.0 15.9 %collective-permute-start.27 = (bf16[256,384]{1,0:T(8,128)(2,1)S(1)}, bf16[256,384]{1,0:T(8,128)(2,1)S(1)}, u32[]{:S(2)}, u32[]{:S(2)}) collective-permute-start(bf16[256,384]{1,0:T(8,128)(2,1)S(1)} %get-tuple-element.44), channel_id=1, source_target_pairs={{0,14},{1,6},{2,12},{3,4},{4,10},{5,2},{6,8},{7,0},{8,15},{9,7},{1... | collective-permute-start | bytes 589832 | tf_op jit(solution)/shard_map/ppermute | solution.py:29
  194.7 10.2 %collective-permute-start.29 = (bf16[256,128]{1,0:T(8,128)(2,1)S(1)}, bf16[256,128]{1,0:T(8,128)(2,1)S(1)}, u32[]{:S(2)}, u32[]{:S(2)}) collective-permute-start(bf16[256,128]{1,0:T(8,128)(2,1)S(1)} %get-tuple-element.46), channel_id=1, source_target_pairs={{0,0},{1,8},{2,2},{3,10},{4,4},{5,12},{6,6},{7,14},{8,1},{9,9},{10... | collective-permute-start | bytes 196616 | tf_op jit(solution)/shard_map/ppermute | solution.py:29
  196.1 8.8 %collective-permute-start.30 = (bf16[256,128]{1,0:T(8,128)(2,1)S(1)}, bf16[256,128]{1,0:T(8,128)(2,1)S(1)}, u32[]{:S(2)}, u32[]{:S(2)}) collective-permute-start(bf16[256,128]{1,0:T(8,128)(2,1)S(1)} %get-tuple-element.47), channel_id=1, source_target_pairs={{0,2},{1,10},{2,0},{3,8},{4,6},{5,14},{6,4},{7,12},{8,3},{9,11},{1... | collective-permute-start | bytes 196616 | tf_op jit(solution)/shard_map/ppermute | solution.py:29
  197.2 8.5 %collective-permute-start.31 = (bf16[256,128]{1,0:T(8,128)(2,1)S(1)}, bf16[256,128]{1,0:T(8,128)(2,1)S(1)}, u32[]{:S(2)}, u32[]{:S(2)}) collective-permute-start(bf16[256,128]{1,0:T(8,128)(2,1)S(1)} %get-tuple-element.48), channel_id=1, source_target_pairs={{0,4},{1,12},{2,6},{3,14},{4,0},{5,8},{6,2},{7,10},{8,5},{9,13},{1... | collective-permute-start | bytes 196616 | tf_op jit(solution)/shard_map/ppermute | solution.py:29
  198.5 10.4 %collective-permute-start.32 = (bf16[256,128]{1,0:T(8,128)(2,1)}, bf16[256,128]{1,0:T(8,128)(2,1)S(1)}, u32[]{:S(2)}, u32[]{:S(2)}) collective-permute-start(bf16[256,128]{1,0:T(8,128)(2,1)} %get-tuple-element.49), channel_id=1, source_target_pairs={{0,6},{1,14},{2,4},{3,12},{4,2},{5,10},{6,0},{7,8},{8,7},{9,15},{1... | collective-permute-start | bytes 196616 | tf_op jit(solution)/shard_map/ppermute | solution.py:29
  (42 other events, 359.3 us)

commit v2 on v1

v2 whole, which is shorter than its diff:
```python
import functools
import math

import jax
import jax.numpy as jnp
from jax import lax
from jax.experimental import pallas as pl
from jax.experimental.pallas import tpu as pltpu
from jax.sharding import PartitionSpec as P

HEAD_DIM = 64
BLOCK = 128
SLOTS = 4
GROUP = 4
AXES = ("tgt", "sec")
SCALE = 0.125
NT = (((1,), (1,)), ((), ()))
TN = (((0,), (0,)), ((), ()))


def send(block, route):
    rows, secs = lax.axis_size("tgt"), lax.axis_size("sec")
    pairs = []
    for t in range(rows):
        for s in range(secs):
            target = route(t, s)
            if target is not None and 0 <= target[0] < rows:
                pairs.append((t * secs + s, target[0] * secs + target[1]))
    return lax.ppermute(block, AXES, pairs)


def swap(block, a):
    return send(block, lambda t, s: (t ^ a, s))


def pack_kernel(pos, queries, grad_out, key_values, listed, *outs):
    width = outs[0].shape[1]
    size = queries.shape[0]
    for a, out in enumerate(outs):
        columns = pl.ds(pl.multiple_of((pos[0] ^ a) * width, width), width)
        out[0:size] = queries[:, columns]
        out[size : 2 * size] = grad_out[:, columns]
        out[2 * size : 3 * size] = key_values[0, :, columns]
        out[3 * size : 4 * size] = key_values[1, :, columns]
        out[4 * size :] = listed[...]


def pack(pos, queries, grad_out, key_values, listed):
    width = listed.shape[1]
    shape = jax.ShapeDtypeStruct((4 * queries.shape[0] + listed.shape[0], width), queries.dtype)
    whole = pl.BlockSpec(memory_space=pltpu.VMEM)
    return pl.pallas_call(
        pack_kernel,
        out_shape=[shape] * GROUP,
        in_specs=[pl.BlockSpec(memory_space=pltpu.SMEM)] + [whole] * 4,
        out_specs=[whole] * GROUP,
        name="pack",
    )(pos, queries, grad_out, key_values, listed)


def attend_kernel(span, n_halo, with_halos, with_state, last, meta, pos, *refs):
    packs, refs = refs[:GROUP], refs[GROUP:]
    n_read = n_halo if with_halos else 0
    halos, refs = refs[:n_read], refs[n_read:]
    state, refs = refs[: 2 * with_state], refs[2 * with_state :]
    outs, (keys, values, rows, ups, kg, vg, qm, om) = refs[:-8], refs[-8:]
    acc, dq_all = outs[:2]
    own, width = dq_all.shape[0], dq_all.shape[2]
    per_dev = own // GROUP
    total = own + n_halo * per_dev
    size = per_dev * BLOCK
    heads = width // HEAD_DIM
    here, start = pos[0], pos[1]
    block = (per_dev, BLOCK, width)
    for a in range(GROUP):
        place = pl.ds((here ^ a) * per_dev, per_dev)
        for n, held in enumerate((rows, ups, keys, values)):
            held[place] = packs[a][n * size : (n + 1) * size].reshape(block)
    for n, halo in enumerate(halos):
        part = slice(own + n * per_dev, own + (n + 1) * per_dev)
        keys[part] = halo[:size].reshape(block)
        values[part] = halo[size:].reshape(block)
    if with_state:
        acc[...] = state[0][...]
        dq_all[...] = state[1][...]
    else:
        acc[...] = jnp.zeros_like(acc)
        dq_all[...] = jnp.zeros_like(dq_all)
    lane_head = lax.broadcasted_iota(jnp.int32, (BLOCK, width), 1) // HEAD_DIM
    key_row = lax.broadcasted_iota(jnp.int32, (SLOTS * BLOCK, heads * BLOCK), 0)

    def step(turn, carry):
        member = lax.rem(start + 1 + turn // per_dev, GROUP)
        a = here ^ member
        r = lax.rem(turn, per_dev)
        i = member * per_dev + r
        count = meta[a, r, SLOTS]
        ids = [jnp.clip(meta[a, r, s], 0, total - 1) for s in range(SLOTS)]
        for s in range(SLOTS):
            kg[s * BLOCK : (s + 1) * BLOCK] = keys[ids[s]]
            vg[s * BLOCK : (s + 1) * BLOCK] = values[ids[s]]
        q, o = rows[i], ups[i]
        for h in range(heads):
            qm[h * BLOCK : (h + 1) * BLOCK] = jnp.where(lane_head == h, q, 0)
            om[h * BLOCK : (h + 1) * BLOCK] = jnp.where(lane_head == h, o, 0)
        scores = lax.dot_general(kg[...], qm[...], NT, preferred_element_type=jnp.float32)
        scores = jnp.where(key_row < count * BLOCK, scores, -jnp.inf)
        top = jnp.max(scores, axis=0, keepdims=True)
        expo = jnp.exp2((scores - top) * (SCALE * math.log2(math.e)))
        probs = expo * (1.0 / jnp.sum(expo, axis=0, keepdims=True))
        probs_half = probs.astype(jnp.bfloat16)
        grad_probs = lax.dot_general(vg[...], om[...], NT, preferred_element_type=jnp.float32)
        delta = jnp.sum(probs_half.astype(jnp.float32) * grad_probs, axis=0, keepdims=True)
        grad_half = (probs * (grad_probs - delta)).astype(jnp.bfloat16)
        grad_value = jnp.dot(probs_half, om[...], preferred_element_type=jnp.float32)
        grad_key = SCALE * jnp.dot(grad_half, qm[...], preferred_element_type=jnp.float32)
        for s in range(SLOTS):
            part = slice(s * BLOCK, (s + 1) * BLOCK)
            acc[0, ids[s]] += grad_key[part]
            acc[1, ids[s]] += grad_value[part]
        flipped = lax.dot_general(kg[...], grad_half, TN, preferred_element_type=jnp.float32)
        flipped = jnp.concatenate(
            [
                flipped[h * HEAD_DIM : (h + 1) * HEAD_DIM, h * BLOCK : (h + 1) * BLOCK]
                for h in range(heads)
            ],
            axis=0,
        )
        dq_all[i] = (SCALE * flipped.T).astype(jnp.bfloat16)
        return carry

    lax.fori_loop(span[0], span[1], step, 0)
    half = jnp.bfloat16
    if last:
        dq_outs, (inner, edge) = outs[2 : 2 + GROUP], outs[2 + GROUP :]
        for a in range(GROUP):
            dq_outs[a][...] = dq_all[pl.ds((here ^ a) * per_dev, per_dev)]
        for p in range(GROUP):
            member = lax.rem(start + 1 + p, GROUP)
            taken = acc[:, pl.ds(member * per_dev, per_dev)]
            if p < GROUP - n_halo:
                inner[:, p * per_dev : (p + 1) * per_dev] = taken.astype(half)
            else:
                p -= GROUP - n_halo
                edge[:, p * per_dev : (p + 1) * per_dev] = taken
    elif with_halos:
        for n, back in enumerate(outs[2:]):
            part = slice(own + n * per_dev, own + (n + 1) * per_dev)
            back[...] = acc[:, part].astype(half)


def attend(span, n_halo, meta, pos, packs, halos=(), state=(), last=False):
    per_dev, width = meta.shape[1], packs[0].shape[1]
    own = GROUP * per_dev
    total = own + n_halo * per_dev
    heads = width // HEAD_DIM
    half = jnp.bfloat16
    block = (BLOCK, width)
    shapes = [
        jax.ShapeDtypeStruct((2, total) + block, jnp.float32),
        jax.ShapeDtypeStruct((own,) + block, half),
    ]
    if last:
        shapes += [jax.ShapeDtypeStruct((per_dev,) + block, half)] * GROUP
        shapes.append(jax.ShapeDtypeStruct((2, own - n_halo * per_dev) + block, half))
        shapes.append(jax.ShapeDtypeStruct((2, n_halo * per_dev) + block, jnp.float32))
    elif halos:
        shapes += [jax.ShapeDtypeStruct((2, per_dev) + block, half)] * n_halo
    scratch = (
        [pltpu.VMEM((total,) + block, half)] * 2
        + [pltpu.VMEM((own,) + block, half)] * 2
        + [pltpu.VMEM((SLOTS * BLOCK, width), half)] * 2
        + [pltpu.VMEM((heads * BLOCK, width), half)] * 2
    )
    whole = pl.BlockSpec(memory_space=pltpu.VMEM)
    scalars = pl.BlockSpec(memory_space=pltpu.SMEM)
    turns = span[1] - span[0]
    results = pl.pallas_call(
        functools.partial(attend_kernel, span, n_halo, bool(halos), bool(state), last),
        out_shape=shapes,
        in_specs=[scalars] * 2 + [whole] * (GROUP + len(halos) + len(state)),
        out_specs=[whole] * len(shapes),
        scratch_shapes=scratch,
        compiler_params=pltpu.CompilerParams(vmem_limit_bytes=20 * 2**20),
        cost_estimate=pl.CostEstimate(
            flops=turns * 10 * SLOTS * BLOCK * heads * BLOCK * width,
            bytes_accessed=4 * 2**20,
            transcendentals=turns * SLOTS * heads * BLOCK * BLOCK,
        ),
        name="attend",
    )(meta, pos, *packs, *halos, *state)
    return results[:2], results[2:]


def project_kernel(parts, pos, *refs):
    grads, sources, refs = refs[:GROUP], refs[GROUP : GROUP + len(parts)], refs[GROUP + len(parts) :]
    outs, (left, weights, sems) = refs[:-3], refs[-3:]
    width = grads[0].shape[1]
    rows = grads[0].shape[0] // (2 * GROUP)
    depth = GROUP * width
    per_out = outs[0].shape[0]
    here, start, in_middle = pos[0], pos[1], pos[2]

    def transfer(finish):
        for n, (source, (where, first, size, column)) in enumerate(zip(sources, parts)):

            def move():
                for c in range(2):
                    target = weights.at[c, pl.ds(column, size)]
                    sem = sems.at[n, c]
                    copy = pltpu.make_async_copy(source.at[c, pl.ds(first, size)], target, sem)
                    copy.wait() if finish else copy.start()

            if where is None:
                move()
            else:
                pl.when(in_middle == where)(move)

    transfer(False)
    for j in range(per_out * len(outs)):
        p = lax.rem(pos[3 + j] + (GROUP - 1) - start, GROUP)
        for a in range(GROUP):
            column = (here ^ a) * width
            for c in range(2):
                first = pl.multiple_of((c * GROUP + p) * rows, rows)
                piece = grads[a][pl.ds(first, rows)]
                place = pl.ds(pl.multiple_of(c * depth + column, width), width)
                left[j * rows : (j + 1) * rows, place] = piece
    transfer(True)
    total = None
    for c in range(2):
        term = lax.dot_general(
            left[:, c * depth : (c + 1) * depth],
            weights[c],
            NT,
            preferred_element_type=jnp.float32,
        )
        total = term if total is None else total + term
    total = total.astype(left.dtype)
    for n, out in enumerate(outs):
        for j in range(per_out):
            place = n * per_out + j
            out[j] = total[place * rows : (place + 1) * rows]


def project(pos, rows_at, n_out, grads, parts):
    rows = grads[0].shape[0] // (2 * GROUP)
    depth = GROUP * grads[0].shape[1]
    columns = max(column + size for _, (_, _, size, column) in parts)
    half = jnp.bfloat16
    whole = pl.BlockSpec(memory_space=pltpu.VMEM)
    anywhere = pl.BlockSpec(memory_space=pl.ANY)
    count = len(rows_at)
    pos = jnp.stack(list(pos) + list(rows_at)).astype(jnp.int32)
    return pl.pallas_call(
        functools.partial(project_kernel, [part for _, part in parts]),
        out_shape=[jax.ShapeDtypeStruct((count // n_out, rows, columns), half)] * n_out,
        in_specs=[pl.BlockSpec(memory_space=pltpu.SMEM)]
        + [whole] * GROUP
        + [anywhere] * len(parts),
        out_specs=[whole] * n_out,
        scratch_shapes=[
            pltpu.VMEM((count * rows, 2 * depth), half),
            pltpu.VMEM((2, columns, depth), half),
            pltpu.SemaphoreType.DMA((len(parts), 2)),
        ],
        compiler_params=pltpu.CompilerParams(vmem_limit_bytes=20 * 2**20),
        cost_estimate=pl.CostEstimate(
            flops=4 * count * rows * columns * depth,
            bytes_accessed=6 * 2**20,
            transcendentals=0,
        ),
        name="project",
    )(pos, *grads, *[weight for weight, _ in parts])


def merge_kernel(flip, kept_own, kept_other, given_own, given_other, *outs):
    sums = ((kept_own, given_own), (kept_other, given_other))
    for order in range(2):

        @pl.when(flip[0] == order)
        def _():
            for n, out in enumerate(outs):
                kept, given = sums[(n % 2) ^ order]
                total = kept[n // 2].astype(jnp.float32) + given[n // 2].astype(jnp.float32)
                out[...] = total.astype(out.dtype)


def merge(flip, *parts):
    whole = pl.BlockSpec(memory_space=pltpu.VMEM)
    n_out = 2 * parts[0].shape[0]
    return pl.pallas_call(
        merge_kernel,
        out_shape=[jax.ShapeDtypeStruct(parts[0].shape[1:], parts[0].dtype)] * n_out,
        in_specs=[pl.BlockSpec(memory_space=pltpu.SMEM)] + [whole] * 4,
        out_specs=[whole] * n_out,
        name="merge",
    )(flip, *parts)


def collect_kernel(pos, *refs):
    parts, out = refs[:-1], refs[-1]
    wide = out.shape[1] // 2
    for a in range(2):
        total = parts[2 * a][...].astype(jnp.float32) + parts[2 * a + 1][...].astype(jnp.float32)
        out[:, pl.ds(pl.multiple_of((pos[0] ^ a) * wide, wide), wide)] = total.astype(out.dtype)


def collect(pos, parts):
    rows, wide = parts[0].shape
    whole = pl.BlockSpec(memory_space=pltpu.VMEM)
    return pl.pallas_call(
        collect_kernel,
        out_shape=jax.ShapeDtypeStruct((rows, 2 * wide), parts[0].dtype),
        in_specs=[pl.BlockSpec(memory_space=pltpu.SMEM)] + [whole] * 4,
        out_specs=whole,
        name="collect",
    )(pos, *parts)


def place_kernel(starts, pos, *refs):
    parts, (out, held, sems) = refs[:GROUP], refs[GROUP:]
    rows, width = held.shape[1:]
    copies = [
        pltpu.make_async_copy(part.at[pl.ds(start, rows)], held.at[a], sems.at[a])
        for a, (part, start) in enumerate(zip(parts, starts))
    ]
    for copy in copies:
        copy.start()
    for a, copy in enumerate(copies):
        copy.wait()
        out[:, pl.ds(pl.multiple_of((pos[0] ^ a) * width, width), width)] = held[a]


def place_columns(pos, rows, parts, starts):
    width = parts[0].shape[1]
    half = parts[0].dtype
    anywhere = pl.BlockSpec(memory_space=pl.ANY)
    return pl.pallas_call(
        functools.partial(place_kernel, starts),
        out_shape=jax.ShapeDtypeStruct((rows, GROUP * width), half),
        in_specs=[pl.BlockSpec(memory_space=pltpu.SMEM)] + [anywhere] * GROUP,
        out_specs=pl.BlockSpec(memory_space=pltpu.VMEM),
        scratch_shapes=[pltpu.VMEM((GROUP, rows, width), half), pltpu.SemaphoreType.DMA((GROUP,))],
        name="place_columns",
    )(pos, *parts)


def other_core(block):
    return send(block, lambda t, s: (t, s ^ 1))


def deliver(parts):
    arrived = []
    for n, part in enumerate(parts):
        a1, a2 = n // 2, n % 2

        def route(t, s):
            g, z, x = t // GROUP, (t // 2) % 2, t % 2
            y, core = s // 2, s % 2
            return (g * GROUP + 2 * core + (x ^ a1), 2 * (y ^ a2) + (z ^ y ^ a2 ^ g))

        arrived.append(send(part, route))
    return arrived


def deliver_any(parts, group):
    groups = len(parts)
    secs = lax.axis_size("sec")
    rows, wide = parts[0].shape[1:]
    stacked = jnp.roll(jnp.stack(parts[::-1]), group + 1, axis=0)
    shape = (secs, groups // secs, GROUP, rows, wide)
    mine = lax.psum_scatter(stacked.reshape(shape), "sec", scatter_dimension=0, tiled=False)
    mine = jnp.moveaxis(mine, 1, 0)
    n_tgt = lax.axis_size("tgt")
    lists = [list(range(g, g + GROUP)) for g in range(0, n_tgt, GROUP)]
    mine = lax.all_to_all(mine, "tgt", 0, 0, axis_index_groups=lists)
    return jnp.transpose(mine, (2, 1, 0, 3)).reshape(rows, -1)


def after(block, *earlier):
    return lax.optimization_barrier((block, *earlier))[0]


def per_device(queries, key_values, grad_out, block_ids, block_count, kv_weight):
    rows_here, width_here = queries.shape
    blocks_here = rows_here // BLOCK
    width = width_here // GROUP
    n_tgt = lax.axis_size("tgt")
    groups = n_tgt // GROUP
    paired = groups == 2
    n_halo = 1 if paired else 2
    t, s = lax.axis_index("tgt"), lax.axis_index("sec")
    group, here = t // GROUP, t % GROUP
    start = jnp.where(group == 0, GROUP - 1, 0) if paired else 0
    pos = jnp.stack([here, start]).astype(jnp.int32)

    def other_group(block):
        return send(block, lambda t, s: (t ^ GROUP, s))

    def middle(block):
        return send(block, lambda t, s: (t ^ 6, s) if t // 2 in (1, 2) else None)

    def ends(block):
        return send(block, lambda t, s: (t ^ 6, s) if t // 2 in (0, 3) else None)

    def shifted(block, k):
        return send(block, lambda t, s: (t + GROUP * k, s))

    wide = kv_weight.shape[1]
    unit = wide // 16
    middle_cuts, end_cuts = (0, 8, 16), (0, 16)

    def rows_of(cuts, n):
        return kv_weight[:, cuts[n] * unit : cuts[n + 1] * unit]

    total = (GROUP + n_halo) * blocks_here
    slots = (block_ids - group * GROUP * blocks_here) % total
    listed = jnp.concatenate([slots, block_count[:, None]], axis=1).astype(jnp.bfloat16)
    listed = jnp.pad(listed, ((0, 16 - blocks_here), (0, width - SLOTS - 1)))
    packs = pack(pos, queries, grad_out, key_values, listed)
    if paired:
        middles = [middle(after(rows_of(middle_cuts, 0), packs[0]))]
    packs = [packs[0]] + [swap(packs[a], a) for a in range(1, GROUP)]
    pairs = [p[2 * rows_here : 4 * rows_here] for p in packs]

    def member(m):
        chosen = pairs[0]
        for a in range(1, GROUP):
            chosen = jnp.where(here ^ a == m, pairs[a], chosen)
        return chosen

    if paired:
        halos = [other_group(after(member(start), middles[0]))]
    else:
        halos = [shifted(member(0), -1), shifted(member(GROUP - 1), 1)]

    meta = jnp.stack([p[4 * rows_here : 4 * rows_here + blocks_here, : SLOTS + 1] for p in packs])
    meta = meta.astype(jnp.int32)
    own = GROUP * blocks_here
    n_inner = own - n_halo * blocks_here
    state, _ = attend((0, n_inner // 2), n_halo, meta, pos, packs)
    state, backs = attend((n_inner, own), n_halo, meta, pos, packs, halos, state)
    if paired:
        returned = other_group(backs[0])
    else:
        returned = jnp.concatenate([shifted(backs[1], -1), shifted(backs[0], 1)], axis=1)
    _, results = attend((n_inner // 2, n_inner), n_halo, meta, pos, packs, (), state, True)
    dq, (inner, edge) = results[:GROUP], results[GROUP:]
    edge = (edge + returned.astype(jnp.float32)).astype(jnp.bfloat16)
    grads = jnp.concatenate([inner, edge], axis=1).reshape(-1, width)
    dq = [block.reshape(rows_here, width) for block in dq]
    if paired:
        middles.append(middle(after(rows_of(middle_cuts, 1), returned)))
    near = swap(jnp.concatenate([grads, dq[1]]), 1)
    beside = swap(jnp.concatenate([grads, dq[2], dq[3]]), 2)
    if paired:
        far = [ends(after(rows_of(end_cuts, 0), beside, middles[1]))]
        beside = after(beside, near, middles[1])
    across = swap(beside, 1)
    done = grads.shape[0]
    dq = [dq[0], near, beside, across]
    starts = (0, done, done, done + rows_here)
    grads = [grads, near, beside, across]

    if paired:
        in_middle = ((t // 2 == 1) | (t // 2 == 2)).astype(jnp.int32)
        core, y, x = s % 2, s // 2, t % 2
        pos = [here, start, in_middle]
        order = [2 * z + (x ^ a) for z in (core ^ 1, core) for a in range(2)]
        give_own, keep_own = project(pos, order, 2, grads, [(kv_weight, (None, 0, wide, 0))])
        given_own = other_core(give_own)
        parts = []
        for where, weights, cuts in ((1, middles, middle_cuts), (0, far, end_cuts)):
            for weight, lo, hi in zip(weights, cuts, cuts[1:]):
                parts.append((weight, (where, 0, (hi - lo) * unit, lo * unit)))
        give_other, keep_other = project(pos, order, 2, grads, parts)
        given_other = other_core(give_other)
        flip = (y ^ group).astype(jnp.int32).reshape(1)
        arrived = deliver(merge(flip, keep_own, keep_other, given_own, given_other))
        grad_memory = collect(x.astype(jnp.int32).reshape(1), arrived)
    else:
        weights = [kv_weight] + [
            send(kv_weight, lambda t, s, k=k: ((t + GROUP * k) % n_tgt, s))
            for k in range(1, groups)
        ]
        pos, rows_at = [here, start, 0], list(range(GROUP))
        parts = [project(pos, rows_at, 1, grads, [(w, (None, 0, wide, 0))])[0] for w in weights]
        grad_memory = deliver_any(parts, group)

    here = here.astype(jnp.int32).reshape(1)
    return place_columns(here, rows_here, dq, starts), grad_memory


def solution(mesh):
    return jax.shard_map(
        per_device,
        mesh=mesh,
        in_specs=(
            P("tgt", "sec"),
            P(None, "tgt", "sec"),
            P("tgt", "sec"),
            P("tgt", None),
            P("tgt"),
            P(None, "tgt", "sec"),
        ),
        out_specs=(P("tgt", "sec"), P("tgt", "sec")),
        check_vma=False,
    )
```

time: 221 us -> 188 us (0.85)
  starting transfers between devices: 50.6 us -> 28.7 us
  local copies, waits for them, and re-layouts: 27.2 us -> 7.59 us
  Pallas kernels: 30.5 us -> 38.4 us
    ppermute x37 -> x17, starting transfers between devices: 50.6 us -> 28.7 us  [send(): return lax.ppermute(block, AXES, pairs)]
    unnamed x74 -> x34, local copies, waits for them, and re-layouts: 21.2 us -> 4.28 us
    pallas_call x5 -> x9, Pallas kernels: 30.5 us -> 38.4 us  [the longest x3 16.1 us: attend(): pl.pallas_call(functools.partial(attend_kernel, span, n_halo, bool(halos)...]
    dynamic_slice x2 -> x0, local copies, waits for them, and re-layouts: 2.38 us -> none  [the longest x1 1.45 us: per_device(): lax.dynamic_slice_in_dim(part, first, width, axis=1)]
    ppermute x37 -> x17, waiting for transfers between devices: 109 us -> 109 us  [send(): return lax.ppermute(block, AXES, pairs)]
  transfers between devices with their start and end apart: 37 -> 17, of which waited for: 9 -> 12; matrix products, arithmetic and copies ran while one was open for 2% -> 2% of each run, Pallas kernels for 13% -> 14%
where the time goes in v2:
time: 188 us; the launch traced here: 187 us
  waiting for transfers between devices  109 us (58%)
  Pallas kernels  38.4 us (20%)
  starting transfers between devices  28.7 us (15%)
  local copies, waits for them, and re-layouts  7.59 us (4%)
  other arithmetic  3.06 us (2%)
    ppermute x17, waiting for transfers between devices, send(): return lax.ppermute(block, AXES, pairs)  109 us
    ppermute x17, starting transfers between devices, send(): return lax.ppermute(block, AXES, pairs)  28.7 us
    pallas_call x3, Pallas kernels, attend(): pl.pallas_call(functools.partial(attend_kernel, span, n_halo, bool(halos)...  16.1 us
    pallas_call x2, Pallas kernels, project(): pl.pallas_call(functools.partial(project_kernel, [part for _, part in par...  12.4 us
    unnamed x34, local copies, waits for them, and re-layouts  4.28 us
  transfers between devices with their start and end apart: 17, of which 12 were waited for; matrix products, arithmetic and copies ran while one was open for 2% of the time, Pallas kernels for 14%

profile of v2, /device:TPU:0, one launch (start us, length us, event | category | flops | bytes accessed | tf_op | source)
XLA Modules:
  0.0 187.3 jit_solution(5403261540215111835)
XLA Ops:
  3.4 3.2 %pack.1 = (bf16[1040,256]{1,0:T(8,128)(2,1)}, bf16[1040,256]{1,0:T(8,128)(2,1)}, bf16[1040,256]{1,0:T(8,128)(2,1)}, bf16[1040,256]{1,0:T(8,128)(2,1)}) custom-call(s32[2]{0:T(128)} %pad_add_fusion.pos, bf16[256,1024]{1,0:T(8,128)(2,1)} %queries.1, bf16[256,1024]{1,0:T(8,128)(2,1)} %grad_out.1, bf16[2,256,1024]{2,1,0:T(8,128)(2,1)} %key_values.1, ...), custom_call_target="tpu_custom_call" | custom-call | tf_op jit(solution)/shard_map/pack/pallas_call | solution.py:52
  6.6 2.9 %collective-permute-start = (bf16[1040,256]{1,0:T(8,128)(2,1)}, bf16[1040,256]{1,0:T(8,128)(2,1)S(1)}, u32[]{:S(2)}, u32[]{:S(2)}) collective-permute-start(bf16[1040,256]{1,0:T(8,128)(2,1)} %get-tuple-element.31), channel_id=1, source_target_pairs={{0,4},{1,5},{2,6},{3,7},{4,0},{5,1},{6,2},{7,3},{8,12},{9,13},{10,... | collective-permute-start | bytes 1597448 | tf_op jit(solution)/shard_map/ppermute | solution.py:29
  9.5 1.6 collective-permute-start.1
  11.1 3.1 %fusion.9 = (bf16[2,256,1024]{2,1,0:T(8,128)(2,1)}, bf16[2,256,1024]{2,1,0:T(8,128)(2,1)}) fusion(bf16[2,512,1024]{2,1,0:T(8,128)(2,1)} %refs_4_.1), kind=kLoop, calls=%fused_computation.24 | loop fusion | bytes 4194304 | tf_op jit(solution)/shard_map/slice | solution.py:415
  15.0 6.9 %collective-permute-done.refs_1_ = bf16[1040,256]{1,0:T(8,128)(2,1)S(1)} collective-permute-done((bf16[1040,256]{1,0:T(8,128)(2,1)}, bf16[1040,256]{1,0:T(8,128)(2,1)S(1)}, u32[]{:S(2)}, u32[]{:S(2)}) %collective-permute-start) | collective-permute-done | bytes 532512 | tf_op jit(solution)/shard_map/ppermute | solution.py:29
  21.9 2.9 %collective-permute-done.1.refs_2_ = bf16[1040,256]{1,0:T(8,128)(2,1)S(1)} collective-permute-done((bf16[1040,256]{1,0:T(8,128)(2,1)}, bf16[1040,256]{1,0:T(8,128)(2,1)S(1)}, u32[]{:S(2)}, u32[]{:S(2)}) %collective-permute-start.1) | collective-permute-done | bytes 532512 | tf_op jit(solution)/shard_map/ppermute | solution.py:29
  24.8 9.7 %collective-permute-done.2.refs_3_ = bf16[1040,256]{1,0:T(8,128)(2,1)S(1)} collective-permute-done((bf16[1040,256]{1,0:T(8,128)(2,1)}, bf16[1040,256]{1,0:T(8,128)(2,1)S(1)}, u32[]{:S(2)}, u32[]{:S(2)}) %collective-permute-start.2) | collective-permute-done | bytes 532512 | tf_op jit(solution)/shard_map/ppermute | solution.py:29
  34.6 9.3 %collective-permute-start.4 = (bf16[512,256]{1,0:T(8,128)(2,1)S(1)}, bf16[512,256]{1,0:T(8,128)(2,1)S(1)}, u32[]{:S(2)}, u32[]{:S(2)}) collective-permute-start(bf16[512,256]{1,0:T(8,128)(2,1)S(1)} %fusion.1), channel_id=1, source_target_pairs={{0,16},{1,17},{2,18},{3,19},{4,20},{5,21},{6,22},{7,23},{8,24},{9,... | collective-permute-start | bytes 786440 | tf_op jit(solution)/shard_map/ppermute | solution.py:29
  44.0 5.2 %attend.3 = (f32[2,10,128,256]{3,2,1,0:T(8,128)S(1)}, bf16[8,128,256]{2,1,0:T(8,128)(2,1)S(1)}) custom-call(s32[4,2,5]{2,1,0:T(2,128)S(1)} %maximum_convert_fusion.meta, s32[2]{0:T(128)S(1)} %copy-done.10, bf16[1040,256]{1,0:T(8,128)(2,1)S(1)} %copy-done.2, bf16[1040,256]{1,0:T(8,128)(2,1)S(1)} %collective-permute-done.refs_1_, ...), custom_call_target="tpu_custom_call" | custom-call | flops 2013265920 | bytes 4194304 | tf_op jit(solution)/shard_map/attend/pallas_call | solution.py:178
  49.2 4.3 %collective-permute-done.4.refs_4_ = bf16[512,256]{1,0:T(8,128)(2,1)S(1)} collective-permute-done((bf16[512,256]{1,0:T(8,128)(2,1)S(1)}, bf16[512,256]{1,0:T(8,128)(2,1)S(1)}, u32[]{:S(2)}, u32[]{:S(2)}) %collective-permute-start.4) | collective-permute-done | bytes 262176 | tf_op jit(solution)/shard_map/ppermute | solution.py:29
  53.6 3.8 %attend.4 = (f32[2,10,128,256]{3,2,1,0:T(8,128)S(1)}, bf16[8,128,256]{2,1,0:T(8,128)(2,1)S(1)}, bf16[2,2,128,256]{3,2,1,0:T(8,128)(2,1)S(1)}) custom-call(s32[4,2,5]{2,1,0:T(2,128)S(1)} %maximum_convert_fusion.meta, s32[2]{0:T(128)S(1)} %copy-done.10, bf16[1040,256]{1,0:T(8,128)(2,1)S(1)} %copy-done.2, bf16[1040,256]{1,0:T(8,128)(2,1)S(1)} %collective-permute-done.refs_1_, ...), custom_call_target="tpu_custom_call" | custom-call | flops 1342177280 | bytes 4194304 | tf_op jit(solution)/shard_map/attend/pallas_call | solution.py:178
  57.5 7.0 %attend.5 = (f32[2,10,128,256]{3,2,1,0:T(8,128)}, bf16[8,128,256]{2,1,0:T(8,128)(2,1)}, bf16[2,128,256]{2,1,0:T(8,128)(2,1)S(1)}, bf16[2,128,256]{2,1,0:T(8,128)...) custom-call(s32[4,2,5]{2,1,0:T(2,128)S(1)} %maximum_convert_fusion.m, ...), custom_call_target="tpu_custom_call" | custom-call | flops 2013265920 | bytes 4194304 | tf_op jit(solution)/shard_map/attend/pallas_call | solution.py:178
  64.5 5.4 %collective-permute-done.5 = bf16[2,2,128,256]{3,2,1,0:T(8,128)(2,1)S(1)} collective-permute-done((bf16[2,2,128,256]{3,2,1,0:T(8,128)(2,1)S(1)}, bf16[2,2,128,256]{3,2,1,0:T(8,128)(2,1)S(1)}, u32[]{:S(2)}, u32[]{:S(2)}) %collective-permute-start.5) | collective-permute-done | bytes 262176 | tf_op jit(solution)/shard_map/ppermute | solution.py:29
  71.9 1.6 collective-permute-start.6
  73.5 1.0 copy-done.5
  74.5 26.3 %collective-permute-done.7.refs_2_ = bf16[2560,256]{1,0:T(8,128)(2,1)S(1)} collective-permute-done((bf16[2560,256]{1,0:T(8,128)(2,1)S(1)}, bf16[2560,256]{1,0:T(8,128)(2,1)S(1)}, u32[]{:S(2)}, u32[]{:S(2)}) %collective-permute-start.7) | collective-permute-done | bytes 1310752 | tf_op jit(solution)/shard_map/ppermute | solution.py:29
  100.9 4.4 %collective-permute-start.10 = (bf16[2,512,1024]{2,1,0:T(8,128)(2,1)}, bf16[2,512,1024]{2,1,0:T(8,128)(2,1)}, u32[]{:S(2)}, u32[]{:S(2)}) collective-permute-start(bf16[2,512,1024]{2,1,0:T(8,128)(2,1)} %refs_4_.1), channel_id=1, source_target_pairs={{0,24},{1,25},{2,26},{3,27},{4,28},{5,29},{6,30},{7,31},{24,0},{25... | collective-permute-start | bytes 6291464 | tf_op jit(solution)/shard_map/ppermute | solution.py:29
  105.3 1.4 collective-permute-start.9
  106.8 28.2 %collective-permute-done.9.refs_3_ = bf16[2560,256]{1,0:T(8,128)(2,1)} collective-permute-done((bf16[2560,256]{1,0:T(8,128)(2,1)S(1)}, bf16[2560,256]{1,0:T(8,128)(2,1)}, u32[]{:S(2)}, u32[]{:S(2)}) %collective-permute-start.9) | collective-permute-done | bytes 1310752 | tf_op jit(solution)/shard_map/ppermute | solution.py:29
  135.0 6.1 %project.2 = (bf16[2,256,512]{2,1,0:T(8,128)(2,1)}, bf16[2,256,512]{2,1,0:T(8,128)(2,1)S(1)}) custom-call(s32[7]{0:T(128)S(1)} %stack.66.pos, bf16[2048,256]{1,0:T(8,128)(2,1)S(1)} %bitcast.26, bf16[2304,256]{1,0:T(8,128)(2,1)S(1)} %collective-permute-done.6.refs_1_, bf16[2560,256]{1,0:T(8,128)(2,1)S(1)} %collective-permute-done.7.refs_2_, ...), custom_call_target="tpu_custom_call" | custom-call | flops 2147483648 | bytes 6291456 | tf_op jit(solution)/shard_map/project/pallas_call | solution.py:255
  141.3 10.3 %collective-permute-done.10.refs_6_ = bf16[2,512,1024]{2,1,0:T(8,128)(2,1)} collective-permute-done((bf16[2,512,1024]{2,1,0:T(8,128)(2,1)}, bf16[2,512,1024]{2,1,0:T(8,128)(2,1)}, u32[]{:S(2)}, u32[]{:S(2)}) %collective-permute-start.10) | collective-permute-done | bytes 2097184 | tf_op jit(solution)/shard_map/ppermute | solution.py:29
  151.6 6.2 %project.3 = (bf16[2,256,512]{2,1,0:T(8,128)(2,1)}, bf16[2,256,512]{2,1,0:T(8,128)(2,1)S(1)}) custom-call(s32[7]{0:T(128)S(1)} %stack.66.pos, bf16[2048,256]{1,0:T(8,128)(2,1)S(1)} %bitcast.27, bf16[2304,256]{1,0:T(8,128)(2,1)S(1)} %collective-permute-done.6.refs_1_, bf16[2560,256]{1,0:T(8,128)(2,1)S(1)} %collective-permute-done.7.refs_2_, ...), custom_call_target="tpu_custom_call" | custom-call | flops 2147483648 | bytes 6291456 | tf_op jit(solution)/shard_map/project/pallas_call | solution.py:255
  158.7 2.1 %collective-permute-done.12.given_other = bf16[2,256,512]{2,1,0:T(8,128)(2,1)S(1)} collective-permute-done((bf16[2,256,512]{2,1,0:T(8,128)(2,1)}, bf16[2,256,512]{2,1,0:T(8,128)(2,1)S(1)}, u32[]{:S(2)}, u32[]{:S(2)}) %collective-permute-start.12) | collective-permute-done | bytes 524320 | tf_op jit(solution)/shard_map/ppermute | solution.py:29
  161.6 2.8 %merge.1 = (bf16[256,512]{1,0:T(8,128)(2,1)}, bf16[256,512]{1,0:T(8,128)(2,1)}, bf16[256,512]{1,0:T(8,128)(2,1)}, bf16[256,512]{1,0:T(8,128)(2,1)}) custom-call(s32[1]{0:T(128)} %bitcast.13.flip, bf16[2,256,512]{2,1,0:T(8,128)(2,1)} %copy-done.7, bf16[2,256,512]{2,1,0:T(8,128)(2,1)} %copy-done.8, bf16[2,256,512]{2,1,0:T(8,128)(2,1)} %collective-permute-done.11.given_own, ...), custom_call_target="tpu_custom_call" | custom-call | tf_op jit(solution)/shard_map/merge/pallas_call | solution.py:292
  164.4 1.6 collective-permute-start.13
  165.9 1.6 collective-permute-start.14
  167.6 1.5 collective-permute-start.15
  169.1 1.1 collective-permute-start.16
  170.2 1.9 %place_columns.1 = bf16[256,1024]{1,0:T(8,128)(2,1)} custom-call(s32[1]{0:T(128)} %bitcast.pos, bf16[256,256]{1,0:T(8,128)(2,1)} %bitcast.28, bf16[2304,256]{1,0:T(8,128)(2,1)} %copy-done.1, bf16[2560,256]{1,0:T(8,128)(2,1)} %copy-done, bf16[2560,256]{1,0:T(8,128)(2,1)} %collective-permute-done.9.refs_3_), custom_call_target="tpu_custom_call" | custom-call | tf_op jit(solution)/shard_map/place_columns/pallas_call | solution.py:339
  172.5 1.6 collective-permute-done.15.refs_2_
  174.2 10.3 %collective-permute-done.16.refs_3_ = bf16[256,512]{1,0:T(8,128)(2,1)S(1)} collective-permute-done((bf16[256,512]{1,0:T(8,128)(2,1)}, bf16[256,512]{1,0:T(8,128)(2,1)S(1)}, u32[]{:S(2)}, u32[]{:S(2)}) %collective-permute-start.16) | collective-permute-done | bytes 262176 | tf_op jit(solution)/shard_map/ppermute | solution.py:29
  185.2 2.1 %collect.1 = bf16[256,1024]{1,0:T(8,128)(2,1)} custom-call(s32[1]{0:T(128)} %bitcast.12.pos, bf16[256,512]{1,0:T(8,128)(2,1)} %copy-done.13, bf16[256,512]{1,0:T(8,128)(2,1)} %copy-done.14, bf16[256,512]{1,0:T(8,128)(2,1)} %copy-done.15, bf16[256,512]{1,0:T(8,128)(2,1)} %copy-done.16), custom_call_target="tpu_custom_call" | custom-call | tf_op jit(solution)/shard_map/collect/pallas_call | solution.py:312
  (62 shorter events, 8.5 us)
Async XLA Ops:
  6.6 15.2 %collective-permute-start = (bf16[1040,256]{1,0:T(8,128)(2,1)}, bf16[1040,256]{1,0:T(8,128)(2,1)S(1)}, u32[]{:S(2)}, u32[]{:S(2)}) collective-permute-start(bf16[1040,256]{1,0:T(8,128)(2,1)} %get-tuple-element.31), channel_id=1, source_target_pairs={{0,4},{1,5},{2,6},{3,7},{4,0},{5,1},{6,2},{7,3},{8,12},{9,13},{10,... | collective-permute-start | bytes 1597448 | tf_op jit(solution)/shard_map/ppermute | solution.py:29
  9.5 15.2 %collective-permute-start.1 = (bf16[1040,256]{1,0:T(8,128)(2,1)}, bf16[1040,256]{1,0:T(8,128)(2,1)S(1)}, u32[]{:S(2)}, u32[]{:S(2)}) collective-permute-start(bf16[1040,256]{1,0:T(8,128)(2,1)} %get-tuple-element.32), channel_id=1, source_target_pairs={{0,8},{1,9},{2,10},{3,11},{4,12},{5,13},{6,14},{7,15},{8,0},{9,1},... | collective-permute-start | bytes 1597448 | tf_op jit(solution)/shard_map/ppermute | solution.py:29
  11.1 3.8 %copy-start.2 = (bf16[1040,256]{1,0:T(8,128)(2,1)S(1)}, bf16[1040,256]{1,0:T(8,128)(2,1)}, u32[]{:S(2)}) copy-start(bf16[1040,256]{1,0:T(8,128)(2,1)} %get-tuple-element.30.refs_0_) | copy-start | bytes 1597444
  11.1 32.9 %copy-start.10 = (s32[2]{0:T(128)S(1)}, s32[2]{0:T(128)}, u32[]{:S(2)}) copy-start(s32[2]{0:T(128)} %pad_add_fusion.pos) | copy-start | bytes 28
  11.1 23.4 %collective-permute-start.2 = (bf16[1040,256]{1,0:T(8,128)(2,1)}, bf16[1040,256]{1,0:T(8,128)(2,1)S(1)}, u32[]{:S(2)}, u32[]{:S(2)}) collective-permute-start(bf16[1040,256]{1,0:T(8,128)(2,1)} %get-tuple-element.33), channel_id=1, source_target_pairs={{0,12},{1,13},{2,14},{3,15},{4,8},{5,9},{6,10},{7,11},{8,4},{9,5},... | collective-permute-start | bytes 1597448 | tf_op jit(solution)/shard_map/ppermute | solution.py:29
  14.2 20.4 %collective-permute-start.3 = (bf16[2,256,1024]{2,1,0:T(8,128)(2,1)}, bf16[2,256,1024]{2,1,0:T(8,128)(2,1)S(1)}, u32[]{:S(2)}, u32[]{:S(2)}) collective-permute-start(bf16[2,256,1024]{2,1,0:T(8,128)(2,1)} %get-tuple-element.34), channel_id=1, source_target_pairs={{8,16},{9,17},{10,18},{11,19},{12,20},{13,21},{14,22},{15,23},{16,... | collective-permute-start | bytes 3145736 | tf_op jit(solution)/shard_map/ppermute | solution.py:29
  34.6 14.6 %copy-start.3 = (bf16[2,256,1024]{2,1,0:T(8,128)(2,1)}, bf16[2,256,1024]{2,1,0:T(8,128)(2,1)S(1)}, u32[]{:S(2)}) copy-start(bf16[2,256,1024]{2,1,0:T(8,128)(2,1)S(1)} %collective-permute-done.3.refs_4_) | copy-start | bytes 3145732
  34.6 18.9 %collective-permute-start.4 = (bf16[512,256]{1,0:T(8,128)(2,1)S(1)}, bf16[512,256]{1,0:T(8,128)(2,1)S(1)}, u32[]{:S(2)}, u32[]{:S(2)}) collective-permute-start(bf16[512,256]{1,0:T(8,128)(2,1)S(1)} %fusion.1), channel_id=1, source_target_pairs={{0,16},{1,17},{2,18},{3,19},{4,20},{5,21},{6,22},{7,23},{8,24},{9,... | collective-permute-start | bytes 786440 | tf_op jit(solution)/shard_map/ppermute | solution.py:29
  57.4 12.4 %collective-permute-start.5 = (bf16[2,2,128,256]{3,2,1,0:T(8,128)(2,1)S(1)}, bf16[2,2,128,256]{3,2,1,0:T(8,128)(2,1)S(1)}, u32[]{:S(2)}, u32[]{:S(2)}) collective-permute-start(bf16[2,2,128,256]{3,2,1,0:T(8,128)(2,1)S(1)} %get-tuple-element.43), channel_id=1, source_target_pairs={{0,16},{1,17},{2,18},{3,19},{4,20},{5,21},{6,22},{7,23},{8,24},{9,... | collective-permute-start | bytes 786440 | tf_op jit(solution)/shard_map/ppermute | solution.py:29
  64.5 5.7 %copy-start.9 = (bf16[2,128,256]{2,1,0:T(8,128)(2,1)}, bf16[2,128,256]{2,1,0:T(8,128)(2,1)S(1)}, u32[]{:S(2)}) copy-start(bf16[2,128,256]{2,1,0:T(8,128)(2,1)S(1)} %get-tuple-element.40) | copy-start | bytes 393220
  69.9 1.2 copy-start.11
  70.1 30.8 %collective-permute-start.7 = (bf16[2560,256]{1,0:T(8,128)(2,1)S(1)}, bf16[2560,256]{1,0:T(8,128)(2,1)S(1)}, u32[]{:S(2)}, u32[]{:S(2)}) collective-permute-start(bf16[2560,256]{1,0:T(8,128)(2,1)S(1)} %pad_maximum_fusion), channel_id=1, source_target_pairs={{0,8},{1,9},{2,10},{3,11},{4,12},{5,13},{6,14},{7,15},{8,0},{9,1},... | collective-permute-start | bytes 3932168 | tf_op jit(solution)/shard_map/ppermute | solution.py:29
  71.1 2.4 %collective-permute-start.8 = (bf16[2,256,1024]{2,1,0:T(8,128)(2,1)S(1)}, bf16[2,256,1024]{2,1,0:T(8,128)(2,1)S(1)}, u32[]{:S(2)}, u32[]{:S(2)}) collective-permute-start(bf16[2,256,1024]{2,1,0:T(8,128)(2,1)S(1)} %copy-done.11), channel_id=1, source_target_pairs={{8,16},{9,17},{10,18},{11,19},{12,20},{13,21},{14,22},{15,23},{16,... | collective-permute-start | bytes 3145736 | tf_op jit(solution)/shard_map/ppermute | solution.py:29
  71.9 33.3 %collective-permute-start.6 = (bf16[2304,256]{1,0:T(8,128)(2,1)S(1)}, bf16[2304,256]{1,0:T(8,128)(2,1)S(1)}, u32[]{:S(2)}, u32[]{:S(2)}) collective-permute-start(bf16[2304,256]{1,0:T(8,128)(2,1)S(1)} %pad_maximum_fusion.1), channel_id=1, source_target_pairs={{0,4},{1,5},{2,6},{3,7},{4,0},{5,1},{6,2},{7,3},{8,12},{9,13},{10,... | collective-permute-start | bytes 3538952 | tf_op jit(solution)/shard_map/ppermute | solution.py:29
  73.5 1.0 copy-start.5
  100.9 50.7 %copy-start = (bf16[2560,256]{1,0:T(8,128)(2,1)}, bf16[2560,256]{1,0:T(8,128)(2,1)S(1)}, u32[]{:S(2)}) copy-start(bf16[2560,256]{1,0:T(8,128)(2,1)S(1)} %collective-permute-done.7.refs_2_) | copy-start | bytes 3932164
  100.9 50.7 %collective-permute-start.10 = (bf16[2,512,1024]{2,1,0:T(8,128)(2,1)}, bf16[2,512,1024]{2,1,0:T(8,128)(2,1)}, u32[]{:S(2)}, u32[]{:S(2)}) collective-permute-start(bf16[2,512,1024]{2,1,0:T(8,128)(2,1)} %refs_4_.1), channel_id=1, source_target_pairs={{0,24},{1,25},{2,26},{3,27},{4,28},{5,29},{6,30},{7,31},{24,0},{25... | collective-permute-start | bytes 6291464 | tf_op jit(solution)/shard_map/ppermute | solution.py:29
  105.3 46.3 %copy-start.1 = (bf16[2304,256]{1,0:T(8,128)(2,1)}, bf16[2304,256]{1,0:T(8,128)(2,1)S(1)}, u32[]{:S(2)}) copy-start(bf16[2304,256]{1,0:T(8,128)(2,1)S(1)} %collective-permute-done.6.refs_1_) | copy-start | bytes 3538948
  105.3 29.7 %collective-permute-start.9 = (bf16[2560,256]{1,0:T(8,128)(2,1)S(1)}, bf16[2560,256]{1,0:T(8,128)(2,1)}, u32[]{:S(2)}, u32[]{:S(2)}) collective-permute-start(bf16[2560,256]{1,0:T(8,128)(2,1)S(1)} %collective-permute-done.7.refs_2_), channel_id=1, source_target_pairs={{0,4},{1,5},{2,6},{3,7},{4,0},{5,1},{6,2},{7,3},{8,12},{9,13},{10,... | collective-permute-start | bytes 3932168 | tf_op jit(solution)/shard_map/ppermute | solution.py:29
  106.8 44.8 %copy-start.4 = (bf16[2,256,1024]{2,1,0:T(8,128)(2,1)S(1)}, bf16[2,256,1024]{2,1,0:T(8,128)(2,1)}, u32[]{:S(2)}) copy-start(bf16[2,256,1024]{2,1,0:T(8,128)(2,1)} %copy-done.3) | copy-start | bytes 3145732
  106.8 44.8 %copy-start.6 = (bf16[2,256,1024]{2,1,0:T(8,128)(2,1)S(1)}, bf16[2,256,1024]{2,1,0:T(8,128)(2,1)}, u32[]{:S(2)}) copy-start(bf16[2,256,1024]{2,1,0:T(8,128)(2,1)} %copy-done.5) | copy-start | bytes 3145732
  141.2 16.7 %copy-start.7 = (bf16[2,256,512]{2,1,0:T(8,128)(2,1)}, bf16[2,256,512]{2,1,0:T(8,128)(2,1)S(1)}, u32[]{:S(2)}) copy-start(bf16[2,256,512]{2,1,0:T(8,128)(2,1)S(1)} %get-tuple-element.49.kept_own) | copy-start | bytes 1572868
  141.2 17.5 %collective-permute-start.11 = (bf16[2,256,512]{2,1,0:T(8,128)(2,1)}, bf16[2,256,512]{2,1,0:T(8,128)(2,1)}, u32[]{:S(2)}, u32[]{:S(2)}) collective-permute-start(bf16[2,256,512]{2,1,0:T(8,128)(2,1)} %get-tuple-element.52), channel_id=1, source_target_pairs={{0,1},{1,0},{2,3},{3,2},{4,5},{5,4},{6,7},{7,6},{8,9},{9,8},{10,11... | collective-permute-start | bytes 1572872 | tf_op jit(solution)/shard_map/ppermute | solution.py:29
  158.7 2.1 %collective-permute-start.12 = (bf16[2,256,512]{2,1,0:T(8,128)(2,1)}, bf16[2,256,512]{2,1,0:T(8,128)(2,1)S(1)}, u32[]{:S(2)}, u32[]{:S(2)}) collective-permute-start(bf16[2,256,512]{2,1,0:T(8,128)(2,1)} %get-tuple-element.53), channel_id=1, source_target_pairs={{0,1},{1,0},{2,3},{3,2},{4,5},{5,4},{6,7},{7,6},{8,9},{9,8},{10,11... | collective-permute-start | bytes 1572872 | tf_op jit(solution)/shard_map/ppermute | solution.py:29
  160.8 0.8 copy-start.12
  164.4 7.8 %collective-permute-start.13 = (bf16[256,512]{1,0:T(8,128)(2,1)}, bf16[256,512]{1,0:T(8,128)(2,1)S(1)}, u32[]{:S(2)}, u32[]{:S(2)}) collective-permute-start(bf16[256,512]{1,0:T(8,128)(2,1)} %get-tuple-element.54), channel_id=1, source_target_pairs={{0,0},{1,8},{2,3},{3,11},{4,4},{5,12},{6,7},{7,15},{8,1},{9,9},{10... | collective-permute-start | bytes 786440 | tf_op jit(solution)/shard_map/ppermute | solution.py:29
  165.9 6.6 %collective-permute-start.14 = (bf16[256,512]{1,0:T(8,128)(2,1)}, bf16[256,512]{1,0:T(8,128)(2,1)S(1)}, u32[]{:S(2)}, u32[]{:S(2)}) collective-permute-start(bf16[256,512]{1,0:T(8,128)(2,1)} %get-tuple-element.55), channel_id=1, source_target_pairs={{0,3},{1,11},{2,0},{3,8},{4,7},{5,15},{6,4},{7,12},{8,2},{9,10},{1... | collective-permute-start | bytes 786440 | tf_op jit(solution)/shard_map/ppermute | solution.py:29
  167.6 6.6 %collective-permute-start.15 = (bf16[256,512]{1,0:T(8,128)(2,1)}, bf16[256,512]{1,0:T(8,128)(2,1)S(1)}, u32[]{:S(2)}, u32[]{:S(2)}) collective-permute-start(bf16[256,512]{1,0:T(8,128)(2,1)} %get-tuple-element.56), channel_id=1, source_target_pairs={{0,4},{1,12},{2,7},{3,15},{4,0},{5,8},{6,3},{7,11},{8,5},{9,13},{1... | collective-permute-start | bytes 786440 | tf_op jit(solution)/shard_map/ppermute | solution.py:29
  169.1 15.4 %collective-permute-start.16 = (bf16[256,512]{1,0:T(8,128)(2,1)}, bf16[256,512]{1,0:T(8,128)(2,1)S(1)}, u32[]{:S(2)}, u32[]{:S(2)}) collective-permute-start(bf16[256,512]{1,0:T(8,128)(2,1)} %get-tuple-element.57), channel_id=1, source_target_pairs={{0,7},{1,15},{2,4},{3,12},{4,3},{5,11},{6,0},{7,8},{8,6},{9,14},{1... | collective-permute-start | bytes 786440 | tf_op jit(solution)/shard_map/ppermute | solution.py:29
  172.1 12.3 %copy-start.13 = (bf16[256,512]{1,0:T(8,128)(2,1)}, bf16[256,512]{1,0:T(8,128)(2,1)S(1)}, u32[]{:S(2)}) copy-start(bf16[256,512]{1,0:T(8,128)(2,1)S(1)} %collective-permute-done.13.refs_0_) | copy-start | bytes 786436
  172.5 11.9 %copy-start.14 = (bf16[256,512]{1,0:T(8,128)(2,1)}, bf16[256,512]{1,0:T(8,128)(2,1)S(1)}, u32[]{:S(2)}) copy-start(bf16[256,512]{1,0:T(8,128)(2,1)S(1)} %collective-permute-done.14.refs_1_) | copy-start | bytes 786436
  174.2 10.3 %copy-start.15 = (bf16[256,512]{1,0:T(8,128)(2,1)}, bf16[256,512]{1,0:T(8,128)(2,1)S(1)}, u32[]{:S(2)}) copy-start(bf16[256,512]{1,0:T(8,128)(2,1)S(1)} %collective-permute-done.15.refs_2_) | copy-start | bytes 786436
  (2 other events, 1.5 us)

commit v3 on v2

--- a/solution.py
+++ b/solution.py
@@ -33,29 +33,43 @@
     return send(block, lambda t, s: (t ^ a, s))
 
 
-def pack_kernel(pos, queries, grad_out, key_values, listed, *outs):
+def pack_kernel(total, block_ids, block_count, queries, grad_out, key_values, *outs):
     width = outs[0].shape[1]
     size = queries.shape[0]
+    position = lax.axis_index("tgt")
+    here, group = lax.rem(position, GROUP), lax.div(position, GROUP)
+    blocks_here, slots = block_ids.shape
+    shape = (outs[0].shape[0] - 4 * size, width)
+    row = lax.broadcasted_iota(jnp.int32, shape, 0)
+    column = lax.broadcasted_iota(jnp.int32, shape, 1)
+    lists = jnp.zeros(shape, jnp.int32)
+    for r in range(blocks_here):
+        for n in range(slots):
+            slot = lax.rem(block_ids[r, n] - group * GROUP * blocks_here + total, total)
+            lists = jnp.where((row == r) & (column == n), slot, lists)
+        lists = jnp.where((row == r) & (column == slots), block_count[r], lists)
+    lists = lists.astype(jnp.float32).astype(outs[0].dtype)
     for a, out in enumerate(outs):
-        columns = pl.ds(pl.multiple_of((pos[0] ^ a) * width, width), width)
+        columns = pl.ds(pl.multiple_of((here ^ a) * width, width), width)
         out[0:size] = queries[:, columns]
         out[size : 2 * size] = grad_out[:, columns]
         out[2 * size : 3 * size] = key_values[0, :, columns]
         out[3 * size : 4 * size] = key_values[1, :, columns]
-        out[4 * size :] = listed[...]
-
-
-def pack(pos, queries, grad_out, key_values, listed):
-    width = listed.shape[1]
-    shape = jax.ShapeDtypeStruct((4 * queries.shape[0] + listed.shape[0], width), queries.dtype)
+        out[4 * size :] = lists
+
+
+def pack(total, block_ids, block_count, queries, grad_out, key_values):
+    width = queries.shape[1] // GROUP
+    shape = jax.ShapeDtypeStruct((4 * queries.shape[0] + 16, width), queries.dtype)
     whole = pl.BlockSpec(memory_space=pltpu.VMEM)
+    scalars = pl.BlockSpec(memory_space=pltpu.SMEM)
     return pl.pallas_call(
-        pack_kernel,
+        functools.partial(pack_kernel, total),
         out_shape=[shape] * GROUP,
-        in_specs=[pl.BlockSpec(memory_space=pltpu.SMEM)] + [whole] * 4,
+        in_specs=[scalars] * 2 + [whole] * 3,
         out_specs=[whole] * GROUP,
         name="pack",
-    )(pos, queries, grad_out, key_values, listed)
+    )(block_ids, block_count, queries, grad_out, key_values)
 
 
 def attend_kernel(span, n_halo, with_halos, with_state, last, meta, pos, *refs):
@@ -274,28 +288,36 @@
     )(pos, *grads, *[weight for weight, _ in parts])
 
 
-def merge_kernel(flip, kept_own, kept_other, given_own, given_other, *outs):
-    sums = ((kept_own, given_own), (kept_other, given_other))
+def merge_kernel(flip, *refs):
+    kept_own, given_own = refs[:2]
+    n_parts = (len(refs) - 2 - 4) // 2
+    kept, given, outs = refs[2 : 2 + n_parts], refs[2 + n_parts : 2 + 2 * n_parts], refs[-4:]
     for order in range(2):
 
         @pl.when(flip[0] == order)
         def _():
             for n, out in enumerate(outs):
-                kept, given = sums[(n % 2) ^ order]
-                total = kept[n // 2].astype(jnp.float32) + given[n // 2].astype(jnp.float32)
-                out[...] = total.astype(out.dtype)
-
-
-def merge(flip, *parts):
+                if (n % 2) ^ order == 0:
+                    terms = [(kept_own, given_own)]
+                else:
+                    terms = list(zip(kept, given))
+                column = 0
+                for left, right in terms:
+                    size = left.shape[2]
+                    total = left[n // 2].astype(jnp.float32) + right[n // 2].astype(jnp.float32)
+                    out[:, column : column + size] = total.astype(out.dtype)
+                    column += size
+
+
+def merge(flip, kept_own, given_own, kept, given):
     whole = pl.BlockSpec(memory_space=pltpu.VMEM)
-    n_out = 2 * parts[0].shape[0]
     return pl.pallas_call(
         merge_kernel,
-        out_shape=[jax.ShapeDtypeStruct(parts[0].shape[1:], parts[0].dtype)] * n_out,
-        in_specs=[pl.BlockSpec(memory_space=pltpu.SMEM)] + [whole] * 4,
-        out_specs=[whole] * n_out,
+        out_shape=[jax.ShapeDtypeStruct(kept_own.shape[1:], kept_own.dtype)] * 4,
+        in_specs=[pl.BlockSpec(memory_space=pltpu.SMEM)] + [whole] * (2 + 2 * len(kept)),
+        out_specs=[whole] * 4,
         name="merge",
-    )(flip, *parts)
+    )(flip, kept_own, given_own, *kept, *given)
 
 
 def collect_kernel(pos, *refs):
@@ -318,30 +340,22 @@
     )(pos, *parts)
 
 
-def place_kernel(starts, pos, *refs):
-    parts, (out, held, sems) = refs[:GROUP], refs[GROUP:]
-    rows, width = held.shape[1:]
-    copies = [
-        pltpu.make_async_copy(part.at[pl.ds(start, rows)], held.at[a], sems.at[a])
-        for a, (part, start) in enumerate(zip(parts, starts))
-    ]
-    for copy in copies:
-        copy.start()
-    for a, copy in enumerate(copies):
-        copy.wait()
-        out[:, pl.ds(pl.multiple_of((pos[0] ^ a) * width, width), width)] = held[a]
-
-
-def place_columns(pos, rows, parts, starts):
-    width = parts[0].shape[1]
-    half = parts[0].dtype
-    anywhere = pl.BlockSpec(memory_space=pl.ANY)
+def place_kernel(pos, *refs):
+    out = refs[-1]
+    for a, part in enumerate(refs[:-1]):
+        width = part.shape[1]
+        start = pl.multiple_of((pos[0] ^ a) * width, width)
+        out[:, pl.ds(start, width)] = part[...]
+
+
+def place_columns(pos, parts):
+    rows, width = parts[0].shape
+    whole = pl.BlockSpec(memory_space=pltpu.VMEM)
     return pl.pallas_call(
-        functools.partial(place_kernel, starts),
-        out_shape=jax.ShapeDtypeStruct((rows, GROUP * width), half),
-        in_specs=[pl.BlockSpec(memory_space=pltpu.SMEM)] + [anywhere] * GROUP,
-        out_specs=pl.BlockSpec(memory_space=pltpu.VMEM),
-        scratch_shapes=[pltpu.VMEM((GROUP, rows, width), half), pltpu.SemaphoreType.DMA((GROUP,))],
+        place_kernel,
+        out_shape=jax.ShapeDtypeStruct((rows, GROUP * width), parts[0].dtype),
+        in_specs=[pl.BlockSpec(memory_space=pltpu.SMEM)] + [whole] * len(parts),
+        out_specs=whole,
         name="place_columns",
     )(pos, *parts)
 
@@ -409,16 +423,13 @@
 
     wide = kv_weight.shape[1]
     unit = wide // 16
-    middle_cuts, end_cuts = (0, 8, 16), (0, 16)
+    middle_cuts, end_cuts = (0, 8, 16), (0, 12, 16)
 
     def rows_of(cuts, n):
         return kv_weight[:, cuts[n] * unit : cuts[n + 1] * unit]
 
     total = (GROUP + n_halo) * blocks_here
-    slots = (block_ids - group * GROUP * blocks_here) % total
-    listed = jnp.concatenate([slots, block_count[:, None]], axis=1).astype(jnp.bfloat16)
-    listed = jnp.pad(listed, ((0, 16 - blocks_here), (0, width - SLOTS - 1)))
-    packs = pack(pos, queries, grad_out, key_values, listed)
+    packs = pack(total, block_ids, block_count, queries, grad_out, key_values)
     if paired:
         middles = [middle(after(rows_of(middle_cuts, 0), packs[0]))]
     packs = [packs[0]] + [swap(packs[a], a) for a in range(1, GROUP)]
@@ -452,16 +463,12 @@
     dq = [block.reshape(rows_here, width) for block in dq]
     if paired:
         middles.append(middle(after(rows_of(middle_cuts, 1), returned)))
-    near = swap(jnp.concatenate([grads, dq[1]]), 1)
-    beside = swap(jnp.concatenate([grads, dq[2], dq[3]]), 2)
+    near, beside = swap(grads, 1), swap(grads, 2)
     if paired:
         far = [ends(after(rows_of(end_cuts, 0), beside, middles[1]))]
         beside = after(beside, near, middles[1])
-    across = swap(beside, 1)
-    done = grads.shape[0]
-    dq = [dq[0], near, beside, across]
-    starts = (0, done, done, done + rows_here)
-    grads = [grads, near, beside, across]
+    grads = [grads, near, beside, swap(beside, 1)]
+    dq = [dq[0]] + [swap(after(dq[a], grads[3]), a) for a in range(1, GROUP)]
 
     if paired:
         in_middle = ((t // 2 == 1) | (t // 2 == 2)).astype(jnp.int32)
@@ -470,14 +477,22 @@
         order = [2 * z + (x ^ a) for z in (core ^ 1, core) for a in range(2)]
         give_own, keep_own = project(pos, order, 2, grads, [(kv_weight, (None, 0, wide, 0))])
         given_own = other_core(give_own)
-        parts = []
-        for where, weights, cuts in ((1, middles, middle_cuts), (0, far, end_cuts)):
-            for weight, lo, hi in zip(weights, cuts, cuts[1:]):
-                parts.append((weight, (where, 0, (hi - lo) * unit, lo * unit)))
-        give_other, keep_other = project(pos, order, 2, grads, parts)
-        given_other = other_core(give_other)
+        far.append(ends(after(rows_of(end_cuts, 1), grads[3])))
+        kept, given = [], []
+        for lo, hi in zip(end_cuts, end_cuts[1:]):
+            parts = []
+            for where, weights, cuts in ((1, middles, middle_cuts), (0, far, end_cuts)):
+                for weight, first, last in zip(weights, cuts, cuts[1:]):
+                    begin, end = max(first, lo), min(last, hi)
+                    if begin < end:
+                        span = ((begin - first) * unit, (end - begin) * unit, (begin - lo) * unit)
+                        parts.append((weight, (where,) + span))
+            give_other, keep_other = project(pos, order, 2, grads, parts)
+            kept.append(keep_other)
+            given.append(other_core(give_other))
+        kept[-1] = after(kept[-1], *dq[1:])
         flip = (y ^ group).astype(jnp.int32).reshape(1)
-        arrived = deliver(merge(flip, keep_own, keep_other, given_own, given_other))
+        arrived = deliver(merge(flip, keep_own, given_own, kept, given))
         grad_memory = collect(x.astype(jnp.int32).reshape(1), arrived)
     else:
         weights = [kv_weight] + [
@@ -489,7 +504,7 @@
         grad_memory = deliver_any(parts, group)
 
     here = here.astype(jnp.int32).reshape(1)
-    return place_columns(here, rows_here, dq, starts), grad_memory
+    return place_columns(here, dq), grad_memory
 
 
 def solution(mesh):

time: 188 us -> 179 us (0.952)
  waiting for transfers between devices: 109 us -> 88.7 us
  local copies, waits for them, and re-layouts: 7.59 us -> 12.5 us
  Pallas kernels: 38.4 us -> 43 us
  starting transfers between devices: 28.7 us -> 31.5 us
    ppermute x17 -> x22, waiting for transfers between devices: 109 us -> 88.7 us  [send(): return lax.ppermute(block, AXES, pairs)]
    ppermute x17 -> x22, starting transfers between devices: 28.7 us -> 31.5 us  [send(): return lax.ppermute(block, AXES, pairs)]
    unnamed x34 -> x38, local copies, waits for them, and re-layouts: 4.28 us -> 6.8 us
    pallas_call x3, Pallas kernels: 16.1 us -> 18.4 us  [attend(): pl.pallas_call(functools.partial(attend_kernel, span, n_halo, bool(halos)...]
    pallas_call x2 -> x3, Pallas kernels: 12.4 us -> 14.5 us  [project(): pl.pallas_call(functools.partial(project_kernel, [part for _, part in par...]
    another operation x4, local copies, waits for them, and re-layouts: 0.01 us -> 2.01 us  [per_device(): jnp.stack([p[4 * rows_here:4 * rows_here + blocks_here, :SLOTS + 1] for p...]
  transfers between devices with their start and end apart: 17 -> 22, of which waited for: 12 -> 12; matrix products, arithmetic and copies ran while one was open for 2% -> 4% of each run, Pallas kernels for 14% -> 17%
where the time goes in v3:
time: 179 us; the launch traced here: 178 us
  waiting for transfers between devices  88.7 us (50%)
  Pallas kernels  43 us (24%)
  starting transfers between devices  31.5 us (18%)
  local copies, waits for them, and re-layouts  12.5 us (7%)
    ppermute x22, waiting for transfers between devices, send(): return lax.ppermute(block, AXES, pairs)  88.7 us
    ppermute x22, starting transfers between devices, send(): return lax.ppermute(block, AXES, pairs)  31.5 us
    pallas_call x3, Pallas kernels, attend(): pl.pallas_call(functools.partial(attend_kernel, span, n_halo, bool(halos)...  18.4 us
    pallas_call x3, Pallas kernels, project(): pl.pallas_call(functools.partial(project_kernel, [part for _, part in par...  14.5 us
    unnamed x38, local copies, waits for them, and re-layouts  6.8 us
    slice x3, local copies, waits for them, and re-layouts, rows_of(): return kv_weight[:, cuts[n] * unit:cuts[n + 1] * unit]  3.65 us
  transfers between devices with their start and end apart: 22, of which 12 were waited for; matrix products, arithmetic and copies ran while one was open for 4% of the time, Pallas kernels for 17%

profile of v3, /device:TPU:0, one launch (start us, length us, event | category | flops | bytes accessed | tf_op | source)
XLA Modules:
  0.0 178.1 jit_solution(12219920054921368465)
XLA Ops:
  0.6 3.3 %pack.1 = (bf16[1040,256]{1,0:T(8,128)(2,1)}, bf16[1040,256]{1,0:T(8,128)(2,1)}, bf16[1040,256]{1,0:T(8,128)(2,1)}, bf16[1040,256]{1,0:T(8,128)(2,1)}) custom-call(s32[2,4]{1,0:T(2,128)} %block_ids.1, s32[2]{0:T(128)} %block_count.1, bf16[256,1024]{1,0:T(8,128)(2,1)} %queries.1, bf16[256,1024]{1,0:T(8,128)(2,1)} %grad_out.1, bf16[2,256,1024]{2,1,0:T(8,128)(2,1)} %key_values.1), custom_call_target="tpu_custom_call" | custom-call | tf_op jit(solution)/shard_map/pack/pallas_call | solution.py:66
  4.0 4.0 %collective-permute-start.2 = (bf16[1040,256]{1,0:T(8,128)(2,1)}, bf16[1040,256]{1,0:T(8,128)(2,1)}, u32[]{:S(2)}, u32[]{:S(2)}) collective-permute-start(bf16[1040,256]{1,0:T(8,128)(2,1)} %get-tuple-element.40), channel_id=1, source_target_pairs={{0,12},{1,13},{2,14},{3,15},{4,8},{5,9},{6,10},{7,11},{8,4},{9,5},... | collective-permute-start | bytes 1597448 | tf_op jit(solution)/shard_map/ppermute | solution.py:29
  8.5 1.5 fusion.2
  10.0 1.6 collective-permute-start.3
  11.8 9.5 %collective-permute-done.2.refs_3_ = bf16[1040,256]{1,0:T(8,128)(2,1)} collective-permute-done((bf16[1040,256]{1,0:T(8,128)(2,1)}, bf16[1040,256]{1,0:T(8,128)(2,1)}, u32[]{:S(2)}, u32[]{:S(2)}) %collective-permute-start.2) | collective-permute-done | bytes 532512 | tf_op jit(solution)/shard_map/ppermute | solution.py:29
  21.9 10.1 %collective-permute-done.1.refs_2_ = bf16[1040,256]{1,0:T(8,128)(2,1)} collective-permute-done((bf16[1040,256]{1,0:T(8,128)(2,1)}, bf16[1040,256]{1,0:T(8,128)(2,1)}, u32[]{:S(2)}, u32[]{:S(2)}) %collective-permute-start.1) | collective-permute-done | bytes 532512 | tf_op jit(solution)/shard_map/ppermute | solution.py:29
  34.5 4.8 %collective-permute-start.4 = (bf16[512,256]{1,0:T(8,128)(2,1)S(1)}, bf16[512,256]{1,0:T(8,128)(2,1)S(1)}, u32[]{:S(2)}, u32[]{:S(2)}) collective-permute-start(bf16[512,256]{1,0:T(8,128)(2,1)S(1)} %fusion.1), channel_id=1, source_target_pairs={{0,16},{1,17},{2,18},{3,19},{4,20},{5,21},{6,22},{7,23},{8,24},{9,... | collective-permute-start | bytes 786440 | tf_op jit(solution)/shard_map/ppermute | solution.py:29
  39.3 6.0 %attend.3 = (f32[2,10,128,256]{3,2,1,0:T(8,128)S(1)}, bf16[8,128,256]{2,1,0:T(8,128)(2,1)S(1)}) custom-call(s32[4,2,5]{2,1,0:T(2,128)S(1)} %maximum_convert_fusion.meta, s32[2]{0:T(128)S(1)} %pad_add_fusion.pos, bf16[1040,256]{1,0:T(8,128)(2,1)S(1)} %copy-done.5, bf16[1040,256]{1,0:T(8,128)(2,1)} %collective-permute-done.refs_1_, ...), custom_call_target="tpu_custom_call" | custom-call | flops 2013265920 | bytes 4194304 | tf_op jit(solution)/shard_map/attend/pallas_call | solution.py:192
  45.3 4.1 %collective-permute-done.4.refs_4_ = bf16[512,256]{1,0:T(8,128)(2,1)S(1)} collective-permute-done((bf16[512,256]{1,0:T(8,128)(2,1)S(1)}, bf16[512,256]{1,0:T(8,128)(2,1)S(1)}, u32[]{:S(2)}, u32[]{:S(2)}) %collective-permute-start.4) | collective-permute-done | bytes 262176 | tf_op jit(solution)/shard_map/ppermute | solution.py:29
  49.5 4.6 %attend.4 = (f32[2,10,128,256]{3,2,1,0:T(8,128)S(1)}, bf16[8,128,256]{2,1,0:T(8,128)(2,1)S(1)}, bf16[2,2,128,256]{3,2,1,0:T(8,128)(2,1)S(1)}) custom-call(s32[4,2,5]{2,1,0:T(2,128)S(1)} %maximum_convert_fusion.meta, s32[2]{0:T(128)S(1)} %pad_add_fusion.pos, bf16[1040,256]{1,0:T(8,128)(2,1)S(1)} %copy-done.5, bf16[1040,256]{1,0:T(8,128)(2,1)} %collective-permute-done.refs_1_, ...), custom_call_target="tpu_custom_call" | custom-call | flops 1342177280 | bytes 4194304 | tf_op jit(solution)/shard_map/attend/pallas_call | solution.py:192
  54.1 7.8 %attend.5 = (f32[2,10,128,256]{3,2,1,0:T(8,128)}, bf16[8,128,256]{2,1,0:T(8,128)(2,1)}, bf16[2,128,256]{2,1,0:T(8,128)(2,1)S(1)}, bf16[2,128,256]{2,1,0:T(8,128)...) custom-call(s32[4,2,5]{2,1,0:T(2,128)S(1)} %maximum_convert_fusion.m, ...), custom_call_target="tpu_custom_call" | custom-call | flops 2013265920 | bytes 4194304 | tf_op jit(solution)/shard_map/attend/pallas_call | solution.py:192
  62.0 5.8 %collective-permute-done.5 = bf16[2,2,128,256]{3,2,1,0:T(8,128)(2,1)S(1)} collective-permute-done((bf16[2,2,128,256]{3,2,1,0:T(8,128)(2,1)S(1)}, bf16[2,2,128,256]{3,2,1,0:T(8,128)(2,1)S(1)}, u32[]{:S(2)}, u32[]{:S(2)}) %collective-permute-start.5) | collective-permute-done | bytes 262176 | tf_op jit(solution)/shard_map/ppermute | solution.py:29
  68.7 1.6 collective-permute-start.7
  71.6 21.3 %collective-permute-done.6.refs_2_ = bf16[2048,256]{1,0:T(8,128)(2,1)} collective-permute-done((bf16[2048,256]{1,0:T(8,128)(2,1)S(1)}, bf16[2048,256]{1,0:T(8,128)(2,1)}, u32[]{:S(2)}, u32[]{:S(2)}) %collective-permute-start.6) | collective-permute-done | bytes 1048608 | tf_op jit(solution)/shard_map/ppermute | solution.py:29
  93.8 3.4 %collective-permute-start.14 = (bf16[2,384,1024]{2,1,0:T(8,128)(2,1)}, bf16[2,384,1024]{2,1,0:T(8,128)(2,1)}, u32[]{:S(2)}, u32[]{:S(2)}) collective-permute-start(bf16[2,384,1024]{2,1,0:T(8,128)(2,1)} %slice.46), channel_id=1, source_target_pairs={{0,24},{1,25},{2,26},{3,27},{4,28},{5,29},{6,30},{7,31},{24,0},{25... | collective-permute-start | bytes 4718600 | tf_op jit(solution)/shard_map/ppermute | solution.py:29
  98.3 1.5 collective-permute-start.9
  100.7 21.9 %collective-permute-done.9.refs_3_ = bf16[2048,256]{1,0:T(8,128)(2,1)} collective-permute-done((bf16[2048,256]{1,0:T(8,128)(2,1)}, bf16[2048,256]{1,0:T(8,128)(2,1)}, u32[]{:S(2)}, u32[]{:S(2)}) %collective-permute-start.9) | collective-permute-done | bytes 1048608 | tf_op jit(solution)/shard_map/ppermute | solution.py:29
  122.5 3.9 %collective-permute-start.15 = (bf16[2,128,1024]{2,1,0:T(8,128)(2,1)}, bf16[2,128,1024]{2,1,0:T(8,128)(2,1)S(1)}, u32[]{:S(2)}, u32[]{:S(2)}) collective-permute-start(bf16[2,128,1024]{2,1,0:T(8,128)(2,1)} %slice.47), channel_id=1, source_target_pairs={{0,24},{1,25},{2,26},{3,27},{4,28},{5,29},{6,30},{7,31},{24,0},{25... | collective-permute-start | bytes 1572872 | tf_op jit(solution)/shard_map/ppermute | solution.py:29
  127.6 5.3 %project.3 = (bf16[2,256,512]{2,1,0:T(8,128)(2,1)}, bf16[2,256,512]{2,1,0:T(8,128)(2,1)S(1)}) custom-call(s32[7]{0:T(128)S(1)} %stack.74.pos, bf16[2048,256]{1,0:T(8,128)(2,1)S(1)} %bitcast.24, bf16[2048,256]{1,0:T(8,128)(2,1)S(1)} %copy-done.4, bf16[2048,256]{1,0:T(8,128)(2,1)} %collective-permute-done.6.refs_2_, ...), custom_call_target="tpu_custom_call" | custom-call | flops 2147483648 | bytes 6291456 | tf_op jit(solution)/shard_map/project/pallas_call | solution.py:269
  133.7 1.4 collective-permute-done.14.refs_6_
  135.1 5.5 %project.4 = (bf16[2,256,384]{2,1,0:T(8,128)(2,1)S(1)}, bf16[2,256,384]{2,1,0:T(8,128)(2,1)S(1)}) custom-call(s32[7]{0:T(128)S(1)} %stack.74.pos, bf16[2048,256]{1,0:T(8,128)(2,1)S(1)} %bitcast.25, bf16[2048,256]{1,0:T(8,128)(2,1)S(1)} %copy-done.4, bf16[2048,256]{1,0:T(8,128)(2,1)} %collective-permute-done.6.refs_2_, ...), custom_call_target="tpu_custom_call" | custom-call | flops 1610612736 | bytes 6291456 | tf_op jit(solution)/shard_map/project/pallas_call | solution.py:269
  140.9 2.9 %collective-permute-start.11 = (bf16[256,256]{1,0:T(8,128)(2,1)S(1)}, bf16[256,256]{1,0:T(8,128)(2,1)}, u32[]{:S(2)}, u32[]{:S(2)}) collective-permute-start(bf16[256,256]{1,0:T(8,128)(2,1)S(1)} %bitcast.29), channel_id=1, source_target_pairs={{0,8},{1,9},{2,10},{3,11},{4,12},{5,13},{6,14},{7,15},{8,0},{9,1},... | collective-permute-start | bytes 393224 | tf_op jit(solution)/shard_map/ppermute | solution.py:29
  144.4 1.3 collective-permute-start.10
  145.7 3.6 %project.5 = (bf16[2,256,128]{2,1,0:T(8,128)(2,1)S(1)}, bf16[2,256,128]{2,1,0:T(8,128)(2,1)S(1)}) custom-call(s32[7]{0:T(128)S(1)} %stack.74.pos, bf16[2048,256]{1,0:T(8,128)(2,1)S(1)} %bitcast.26, bf16[2048,256]{1,0:T(8,128)(2,1)S(1)} %copy-done.4, bf16[2048,256]{1,0:T(8,128)(2,1)} %collective-permute-done.6.refs_2_, ...), custom_call_target="tpu_custom_call" | custom-call | flops 536870912 | bytes 6291456 | tf_op jit(solution)/shard_map/project/pallas_call | solution.py:269
  150.7 1.3 collective-permute-done.17.refs_5_
  152.8 2.8 %merge.1 = (bf16[256,512]{1,0:T(8,128)(2,1)}, bf16[256,512]{1,0:T(8,128)(2,1)}, bf16[256,512]{1,0:T(8,128)(2,1)}, bf16[256,512]{1,0:T(8,128)(2,1)}) custom-call(s32[1]{0:T(128)} %bitcast.12.flip, bf16[2,256,512]{2,1,0:T(8,128)(2,1)} %copy-done.6, bf16[2,256,512]{2,1,0:T(8,128)(2,1)} %copy-done.11, bf16[2,256,384]{2,1,0:T(8,128)(2,1)} %copy-done.7, ...), custom_call_target="tpu_custom_call" | custom-call | tf_op jit(solution)/shard_map/merge/pallas_call | solution.py:314
  155.6 1.6 collective-permute-start.18
  157.2 1.6 collective-permute-start.19
  160.6 2.0 %place_columns.1 = bf16[256,1024]{1,0:T(8,128)(2,1)} custom-call(s32[1]{0:T(128)} %bitcast.pos, bf16[256,256]{1,0:T(8,128)(2,1)} %bitcast.27, bf16[256,256]{1,0:T(8,128)(2,1)} %collective-permute-done.10.refs_1_, bf16[256,256]{1,0:T(8,128)(2,1)} %collective-permute-done.11.refs_2_, bf16[256,256]{1,0:T(8,128)(2,1)} %copy-done.18), custom_call_target="tpu_custom_call" | custom-call | tf_op jit(solution)/shard_map/place_columns/pallas_call | solution.py:354
  163.7 1.6 collective-permute-done.20.refs_2_
  165.4 9.9 %collective-permute-done.21.refs_3_ = bf16[256,512]{1,0:T(8,128)(2,1)S(1)} collective-permute-done((bf16[256,512]{1,0:T(8,128)(2,1)}, bf16[256,512]{1,0:T(8,128)(2,1)S(1)}, u32[]{:S(2)}, u32[]{:S(2)}) %collective-permute-start.21) | collective-permute-done | bytes 262176 | tf_op jit(solution)/shard_map/ppermute | solution.py:29
  176.0 2.1 %collect.1 = bf16[256,1024]{1,0:T(8,128)(2,1)} custom-call(s32[1]{0:T(128)} %bitcast.11.pos, bf16[256,512]{1,0:T(8,128)(2,1)} %copy-done.13, bf16[256,512]{1,0:T(8,128)(2,1)} %copy-done.14, bf16[256,512]{1,0:T(8,128)(2,1)} %copy-done.15, bf16[256,512]{1,0:T(8,128)(2,1)} %copy-done.16), custom_call_target="tpu_custom_call" | custom-call | tf_op jit(solution)/shard_map/collect/pallas_call | solution.py:334
  (73 shorter events, 17.7 us)
Async XLA Ops:
  0.6 7.9 %copy-start = (bf16[2,512,1024]{2,1,0:T(8,128)(2,1)S(1)}, bf16[2,512,1024]{2,1,0:T(8,128)(2,1)}, u32[]{:S(2)}) copy-start(bf16[2,512,1024]{2,1,0:T(8,128)(2,1)} %refs_4_.1) | copy-start | bytes 6291460
  4.0 17.2 %collective-permute-start.2 = (bf16[1040,256]{1,0:T(8,128)(2,1)}, bf16[1040,256]{1,0:T(8,128)(2,1)}, u32[]{:S(2)}, u32[]{:S(2)}) collective-permute-start(bf16[1040,256]{1,0:T(8,128)(2,1)} %get-tuple-element.40), channel_id=1, source_target_pairs={{0,12},{1,13},{2,14},{3,15},{4,8},{5,9},{6,10},{7,11},{8,4},{9,5},... | collective-permute-start | bytes 1597448 | tf_op jit(solution)/shard_map/ppermute | solution.py:29
  7.9 24.0 %collective-permute-start.1 = (bf16[1040,256]{1,0:T(8,128)(2,1)}, bf16[1040,256]{1,0:T(8,128)(2,1)}, u32[]{:S(2)}, u32[]{:S(2)}) collective-permute-start(bf16[1040,256]{1,0:T(8,128)(2,1)} %get-tuple-element.39), channel_id=1, source_target_pairs={{0,8},{1,9},{2,10},{3,11},{4,12},{5,13},{6,14},{7,15},{8,0},{9,1},... | collective-permute-start | bytes 1597448 | tf_op jit(solution)/shard_map/ppermute | solution.py:29
  8.4 3.3 %copy-start.5 = (bf16[1040,256]{1,0:T(8,128)(2,1)S(1)}, bf16[1040,256]{1,0:T(8,128)(2,1)}, u32[]{:S(2)}) copy-start(bf16[1040,256]{1,0:T(8,128)(2,1)} %get-tuple-element.37.refs_0_) | copy-start | bytes 1597444
  8.4 24.3 %collective-permute-start = (bf16[1040,256]{1,0:T(8,128)(2,1)}, bf16[1040,256]{1,0:T(8,128)(2,1)}, u32[]{:S(2)}, u32[]{:S(2)}) collective-permute-start(bf16[1040,256]{1,0:T(8,128)(2,1)} %get-tuple-element.38), channel_id=1, source_target_pairs={{0,4},{1,5},{2,6},{3,7},{4,0},{5,1},{6,2},{7,3},{8,12},{9,13},{10,... | collective-permute-start | bytes 1597448 | tf_op jit(solution)/shard_map/ppermute | solution.py:29
  10.0 24.4 %collective-permute-start.3 = (bf16[2,256,1024]{2,1,0:T(8,128)(2,1)}, bf16[2,256,1024]{2,1,0:T(8,128)(2,1)}, u32[]{:S(2)}, u32[]{:S(2)}) collective-permute-start(bf16[2,256,1024]{2,1,0:T(8,128)(2,1)} %get-tuple-element.41), channel_id=1, source_target_pairs={{8,16},{9,17},{10,18},{11,19},{12,20},{13,21},{14,22},{15,23},{16,... | collective-permute-start | bytes 3145736 | tf_op jit(solution)/shard_map/ppermute | solution.py:29
  34.5 15.0 %collective-permute-start.4 = (bf16[512,256]{1,0:T(8,128)(2,1)S(1)}, bf16[512,256]{1,0:T(8,128)(2,1)S(1)}, u32[]{:S(2)}, u32[]{:S(2)}) collective-permute-start(bf16[512,256]{1,0:T(8,128)(2,1)S(1)} %fusion.1), channel_id=1, source_target_pairs={{0,16},{1,17},{2,18},{3,19},{4,20},{5,21},{6,22},{7,23},{8,24},{9,... | collective-permute-start | bytes 786440 | tf_op jit(solution)/shard_map/ppermute | solution.py:29
  54.1 13.7 %collective-permute-start.5 = (bf16[2,2,128,256]{3,2,1,0:T(8,128)(2,1)S(1)}, bf16[2,2,128,256]{3,2,1,0:T(8,128)(2,1)S(1)}, u32[]{:S(2)}, u32[]{:S(2)}) collective-permute-start(bf16[2,2,128,256]{3,2,1,0:T(8,128)(2,1)S(1)} %get-tuple-element.51), channel_id=1, source_target_pairs={{0,16},{1,17},{2,18},{3,19},{4,20},{5,21},{6,22},{7,23},{8,24},{9,... | collective-permute-start | bytes 786440 | tf_op jit(solution)/shard_map/ppermute | solution.py:29
  62.0 9.6 %copy-start.9 = (bf16[2,128,256]{2,1,0:T(8,128)(2,1)}, bf16[2,128,256]{2,1,0:T(8,128)(2,1)S(1)}, u32[]{:S(2)}) copy-start(bf16[2,128,256]{2,1,0:T(8,128)(2,1)S(1)} %get-tuple-element.47) | copy-start | bytes 393220
  62.0 6.0 %copy-start.10 = (bf16[2,256,1024]{2,1,0:T(8,128)(2,1)S(1)}, bf16[2,256,1024]{2,1,0:T(8,128)(2,1)}, u32[]{:S(2)}) copy-start(bf16[2,256,1024]{2,1,0:T(8,128)(2,1)} %get-tuple-element.52) | copy-start | bytes 3145732
  67.9 24.9 %collective-permute-start.6 = (bf16[2048,256]{1,0:T(8,128)(2,1)S(1)}, bf16[2048,256]{1,0:T(8,128)(2,1)}, u32[]{:S(2)}, u32[]{:S(2)}) collective-permute-start(bf16[2048,256]{1,0:T(8,128)(2,1)S(1)} %bitcast.22), channel_id=1, source_target_pairs={{0,8},{1,9},{2,10},{3,11},{4,12},{5,13},{6,14},{7,15},{8,0},{9,1},... | collective-permute-start | bytes 3145736 | tf_op jit(solution)/shard_map/ppermute | solution.py:29
  68.0 24.8 %collective-permute-start.8 = (bf16[2,256,1024]{2,1,0:T(8,128)(2,1)S(1)}, bf16[2,256,1024]{2,1,0:T(8,128)(2,1)S(1)}, u32[]{:S(2)}, u32[]{:S(2)}) collective-permute-start(bf16[2,256,1024]{2,1,0:T(8,128)(2,1)S(1)} %copy-done.10), channel_id=1, source_target_pairs={{8,16},{9,17},{10,18},{11,19},{12,20},{13,21},{14,22},{15,23},{16,... | collective-permute-start | bytes 3145736 | tf_op jit(solution)/shard_map/ppermute | solution.py:29
  68.7 28.5 %collective-permute-start.7 = (bf16[2048,256]{1,0:T(8,128)(2,1)S(1)}, bf16[2048,256]{1,0:T(8,128)(2,1)S(1)}, u32[]{:S(2)}, u32[]{:S(2)}) collective-permute-start(bf16[2048,256]{1,0:T(8,128)(2,1)S(1)} %bitcast.23), channel_id=1, source_target_pairs={{0,4},{1,5},{2,6},{3,7},{4,0},{5,1},{6,2},{7,3},{8,12},{9,13},{10,... | collective-permute-start | bytes 3145736 | tf_op jit(solution)/shard_map/ppermute | solution.py:29
  93.8 41.3 %collective-permute-start.14 = (bf16[2,384,1024]{2,1,0:T(8,128)(2,1)}, bf16[2,384,1024]{2,1,0:T(8,128)(2,1)}, u32[]{:S(2)}, u32[]{:S(2)}) collective-permute-start(bf16[2,384,1024]{2,1,0:T(8,128)(2,1)} %slice.46), channel_id=1, source_target_pairs={{0,24},{1,25},{2,26},{3,27},{4,28},{5,29},{6,30},{7,31},{24,0},{25... | collective-permute-start | bytes 4718600 | tf_op jit(solution)/shard_map/ppermute | solution.py:29
  98.3 24.3 %collective-permute-start.9 = (bf16[2048,256]{1,0:T(8,128)(2,1)}, bf16[2048,256]{1,0:T(8,128)(2,1)}, u32[]{:S(2)}, u32[]{:S(2)}) collective-permute-start(bf16[2048,256]{1,0:T(8,128)(2,1)} %collective-permute-done.6.refs_2_), channel_id=1, source_target_pairs={{0,4},{1,5},{2,6},{3,7},{4,0},{5,1},{6,2},{7,3},{8,12},{9,13},{10,... | collective-permute-start | bytes 3145736 | tf_op jit(solution)/shard_map/ppermute | solution.py:29
  100.7 34.5 %copy-start.2 = (bf16[2,256,1024]{2,1,0:T(8,128)(2,1)S(1)}, bf16[2,256,1024]{2,1,0:T(8,128)(2,1)}, u32[]{:S(2)}) copy-start(bf16[2,256,1024]{2,1,0:T(8,128)(2,1)} %copy-done.1) | copy-start | bytes 3145732
  122.5 21.9 %collective-permute-start.15 = (bf16[2,128,1024]{2,1,0:T(8,128)(2,1)}, bf16[2,128,1024]{2,1,0:T(8,128)(2,1)S(1)}, u32[]{:S(2)}, u32[]{:S(2)}) collective-permute-start(bf16[2,128,1024]{2,1,0:T(8,128)(2,1)} %slice.47), channel_id=1, source_target_pairs={{0,24},{1,25},{2,26},{3,27},{4,28},{5,29},{6,30},{7,31},{24,0},{25... | collective-permute-start | bytes 1572872 | tf_op jit(solution)/shard_map/ppermute | solution.py:29
  133.7 17.0 %collective-permute-start.13 = (bf16[2,256,512]{2,1,0:T(8,128)(2,1)}, bf16[2,256,512]{2,1,0:T(8,128)(2,1)S(1)}, u32[]{:S(2)}, u32[]{:S(2)}) collective-permute-start(bf16[2,256,512]{2,1,0:T(8,128)(2,1)} %get-tuple-element.60), channel_id=1, source_target_pairs={{0,1},{1,0},{2,3},{3,2},{4,5},{5,4},{6,7},{7,6},{8,9},{9,8},{10,11... | collective-permute-start | bytes 1572872 | tf_op jit(solution)/shard_map/ppermute | solution.py:29
  140.7 8.7 %copy-start.7 = (bf16[2,256,384]{2,1,0:T(8,128)(2,1)}, bf16[2,256,384]{2,1,0:T(8,128)(2,1)S(1)}, u32[]{:S(2)}) copy-start(bf16[2,256,384]{2,1,0:T(8,128)(2,1)S(1)} %get-tuple-element.62.refs_2_) | copy-start | bytes 1179652
  140.7 11.3 %collective-permute-start.16 = (bf16[2,256,384]{2,1,0:T(8,128)(2,1)S(1)}, bf16[2,256,384]{2,1,0:T(8,128)(2,1)S(1)}, u32[]{:S(2)}, u32[]{:S(2)}) collective-permute-start(bf16[2,256,384]{2,1,0:T(8,128)(2,1)S(1)} %get-tuple-element.66), channel_id=1, source_target_pairs={{0,1},{1,0},{2,3},{3,2},{4,5},{5,4},{6,7},{7,6},{8,9},{9,8},{10,11... | collective-permute-start | bytes 1179656 | tf_op jit(solution)/shard_map/ppermute | solution.py:29
  140.8 9.2 %collective-permute-start.12 = (bf16[256,256]{1,0:T(8,128)(2,1)S(1)}, bf16[256,256]{1,0:T(8,128)(2,1)S(1)}, u32[]{:S(2)}, u32[]{:S(2)}) collective-permute-start(bf16[256,256]{1,0:T(8,128)(2,1)S(1)} %bitcast.30), channel_id=1, source_target_pairs={{0,12},{1,13},{2,14},{3,15},{4,8},{5,9},{6,10},{7,11},{8,4},{9,5},... | collective-permute-start | bytes 393224 | tf_op jit(solution)/shard_map/ppermute | solution.py:29
  140.9 9.8 %collective-permute-start.11 = (bf16[256,256]{1,0:T(8,128)(2,1)S(1)}, bf16[256,256]{1,0:T(8,128)(2,1)}, u32[]{:S(2)}, u32[]{:S(2)}) collective-permute-start(bf16[256,256]{1,0:T(8,128)(2,1)S(1)} %bitcast.29), channel_id=1, source_target_pairs={{0,8},{1,9},{2,10},{3,11},{4,12},{5,13},{6,14},{7,15},{8,0},{9,1},... | collective-permute-start | bytes 393224 | tf_op jit(solution)/shard_map/ppermute | solution.py:29
  144.4 6.3 %collective-permute-start.10 = (bf16[256,256]{1,0:T(8,128)(2,1)S(1)}, bf16[256,256]{1,0:T(8,128)(2,1)}, u32[]{:S(2)}, u32[]{:S(2)}) collective-permute-start(bf16[256,256]{1,0:T(8,128)(2,1)S(1)} %bitcast.28), channel_id=1, source_target_pairs={{0,4},{1,5},{2,6},{3,7},{4,0},{5,1},{6,2},{7,3},{8,12},{9,13},{10,... | collective-permute-start | bytes 393224 | tf_op jit(solution)/shard_map/ppermute | solution.py:29
  150.7 1.3 collective-permute-start.17
  150.7 1.3 copy-start.11
  155.6 7.0 %collective-permute-start.18 = (bf16[256,512]{1,0:T(8,128)(2,1)}, bf16[256,512]{1,0:T(8,128)(2,1)S(1)}, u32[]{:S(2)}, u32[]{:S(2)}) collective-permute-start(bf16[256,512]{1,0:T(8,128)(2,1)} %get-tuple-element.68), channel_id=1, source_target_pairs={{0,0},{1,8},{2,3},{3,11},{4,4},{5,12},{6,7},{7,15},{8,1},{9,9},{10... | collective-permute-start | bytes 786440 | tf_op jit(solution)/shard_map/ppermute | solution.py:29
  157.2 6.6 %collective-permute-start.19 = (bf16[256,512]{1,0:T(8,128)(2,1)}, bf16[256,512]{1,0:T(8,128)(2,1)S(1)}, u32[]{:S(2)}, u32[]{:S(2)}) collective-permute-start(bf16[256,512]{1,0:T(8,128)(2,1)} %get-tuple-element.69), channel_id=1, source_target_pairs={{0,3},{1,11},{2,0},{3,8},{4,7},{5,15},{6,4},{7,12},{8,2},{9,10},{1... | collective-permute-start | bytes 786440 | tf_op jit(solution)/shard_map/ppermute | solution.py:29
  158.8 6.6 %collective-permute-start.20 = (bf16[256,512]{1,0:T(8,128)(2,1)}, bf16[256,512]{1,0:T(8,128)(2,1)S(1)}, u32[]{:S(2)}, u32[]{:S(2)}) collective-permute-start(bf16[256,512]{1,0:T(8,128)(2,1)} %get-tuple-element.70), channel_id=1, source_target_pairs={{0,4},{1,12},{2,7},{3,15},{4,0},{5,8},{6,3},{7,11},{8,5},{9,13},{1... | collective-permute-start | bytes 786440 | tf_op jit(solution)/shard_map/ppermute | solution.py:29
  159.5 15.8 %collective-permute-start.21 = (bf16[256,512]{1,0:T(8,128)(2,1)}, bf16[256,512]{1,0:T(8,128)(2,1)S(1)}, u32[]{:S(2)}, u32[]{:S(2)}) collective-permute-start(bf16[256,512]{1,0:T(8,128)(2,1)} %get-tuple-element.71), channel_id=1, source_target_pairs={{0,7},{1,15},{2,4},{3,12},{4,3},{5,11},{6,0},{7,8},{8,6},{9,14},{1... | collective-permute-start | bytes 786440 | tf_op jit(solution)/shard_map/ppermute | solution.py:29
  162.6 12.7 %copy-start.13 = (bf16[256,512]{1,0:T(8,128)(2,1)}, bf16[256,512]{1,0:T(8,128)(2,1)S(1)}, u32[]{:S(2)}) copy-start(bf16[256,512]{1,0:T(8,128)(2,1)S(1)} %collective-permute-done.18.refs_0_) | copy-start | bytes 786436
  163.7 11.5 %copy-start.14 = (bf16[256,512]{1,0:T(8,128)(2,1)}, bf16[256,512]{1,0:T(8,128)(2,1)S(1)}, u32[]{:S(2)}) copy-start(bf16[256,512]{1,0:T(8,128)(2,1)S(1)} %collective-permute-done.19.refs_1_) | copy-start | bytes 786436
  165.4 9.9 %copy-start.15 = (bf16[256,512]{1,0:T(8,128)(2,1)}, bf16[256,512]{1,0:T(8,128)(2,1)S(1)}, u32[]{:S(2)}) copy-start(bf16[256,512]{1,0:T(8,128)(2,1)S(1)} %collective-permute-done.20.refs_2_) | copy-start | bytes 786436
  (9 other events, 7.5 us)

commit v4 on v3

--- a/solution.py
+++ b/solution.py
@@ -94,10 +94,7 @@
         part = slice(own + n * per_dev, own + (n + 1) * per_dev)
         keys[part] = halo[:size].reshape(block)
         values[part] = halo[size:].reshape(block)
-    if with_state:
-        acc[...] = state[0][...]
-        dq_all[...] = state[1][...]
-    else:
+    if not with_state:
         acc[...] = jnp.zeros_like(acc)
         dq_all[...] = jnp.zeros_like(dq_all)
     lane_head = lax.broadcasted_iota(jnp.int32, (BLOCK, width), 1) // HEAD_DIM
@@ -195,6 +192,7 @@
         in_specs=[scalars] * 2 + [whole] * (GROUP + len(halos) + len(state)),
         out_specs=[whole] * len(shapes),
         scratch_shapes=scratch,
+        input_output_aliases={2 + GROUP + len(halos) + n: n for n in range(len(state))},
         compiler_params=pltpu.CompilerParams(vmem_limit_bytes=20 * 2**20),
         cost_estimate=pl.CostEstimate(
             flops=turns * 10 * SLOTS * BLOCK * heads * BLOCK * width,
@@ -208,7 +206,7 @@
 
 def project_kernel(parts, pos, *refs):
     grads, sources, refs = refs[:GROUP], refs[GROUP : GROUP + len(parts)], refs[GROUP + len(parts) :]
-    outs, (left, weights, sems) = refs[:-3], refs[-3:]
+    outs, (total, weights, sems) = refs[:-3], refs[-3:]
     width = grads[0].shape[1]
     rows = grads[0].shape[0] // (2 * GROUP)
     depth = GROUP * width
@@ -231,30 +229,22 @@
                 pl.when(in_middle == where)(move)
 
     transfer(False)
-    for j in range(per_out * len(outs)):
-        p = lax.rem(pos[3 + j] + (GROUP - 1) - start, GROUP)
+    transfer(True)
+    for c in range(2):
         for a in range(GROUP):
-            column = (here ^ a) * width
-            for c in range(2):
-                first = pl.multiple_of((c * GROUP + p) * rows, rows)
-                piece = grads[a][pl.ds(first, rows)]
-                place = pl.ds(pl.multiple_of(c * depth + column, width), width)
-                left[j * rows : (j + 1) * rows, place] = piece
-    transfer(True)
-    total = None
-    for c in range(2):
-        term = lax.dot_general(
-            left[:, c * depth : (c + 1) * depth],
-            weights[c],
-            NT,
-            preferred_element_type=jnp.float32,
-        )
-        total = term if total is None else total + term
-    total = total.astype(left.dtype)
+            column = pl.multiple_of((here ^ a) * width, width)
+            term = lax.dot_general(
+                grads[a][c * GROUP * rows : (c + 1) * GROUP * rows],
+                weights[c, :, pl.ds(column, width)],
+                NT,
+                preferred_element_type=jnp.float32,
+            )
+            total[...] = term if c + a == 0 else total[...] + term
     for n, out in enumerate(outs):
         for j in range(per_out):
-            place = n * per_out + j
-            out[j] = total[place * rows : (place + 1) * rows]
+            p = lax.rem(pos[3 + n * per_out + j] + (GROUP - 1) - start, GROUP)
+            place = pl.ds(pl.multiple_of(p * rows, rows), rows)
+            out[j] = total[place].astype(out.dtype)
 
 
 def project(pos, rows_at, n_out, grads, parts):
@@ -274,7 +264,7 @@
         + [anywhere] * len(parts),
         out_specs=[whole] * n_out,
         scratch_shapes=[
-            pltpu.VMEM((count * rows, 2 * depth), half),
+            pltpu.VMEM((GROUP * rows, columns), jnp.float32),
             pltpu.VMEM((2, columns, depth), half),
             pltpu.SemaphoreType.DMA((len(parts), 2)),
         ],
@@ -423,7 +413,7 @@
 
     wide = kv_weight.shape[1]
     unit = wide // 16
-    middle_cuts, end_cuts = (0, 8, 16), (0, 12, 16)
+    middle_cuts, end_cuts = (0, 7, 16), (0, 12, 16)
 
     def rows_of(cuts, n):
         return kv_weight[:, cuts[n] * unit : cuts[n + 1] * unit]

time: 179 us -> 177 us (0.989)
  Pallas kernels: 43 us -> 40.1 us
    pallas_call x3, Pallas kernels: 18.4 us -> 16.3 us  [attend(): pl.pallas_call(functools.partial(attend_kernel, span, n_halo, bool(halos)...]
    slice x3 -> x4, local copies, waits for them, and re-layouts: 3.65 us -> 3.21 us  [rows_of(): return kv_weight[:, cuts[n] * unit:cuts[n + 1] * unit]]
  transfers between devices with their start and end apart: 22 -> 22, of which waited for: 12 -> 12; matrix products, arithmetic and copies ran while one was open for 4% -> 4% of each run, Pallas kernels for 17% -> 16%
where the time goes in v4:
time: 177 us; the launch traced here: 176 us
  waiting for transfers between devices  88.4 us (50%)
  Pallas kernels  40.1 us (23%)
  starting transfers between devices  32.7 us (18%)
  local copies, waits for them, and re-layouts  12.8 us (7%)
    ppermute x22, waiting for transfers between devices, send(): return lax.ppermute(block, AXES, pairs)  88.4 us
    ppermute x22, starting transfers between devices, send(): return lax.ppermute(block, AXES, pairs)  32.7 us
    pallas_call x3, Pallas kernels, attend(): pl.pallas_call(functools.partial(attend_kernel, span, n_halo, bool(halos)...  16.3 us
    pallas_call x3, Pallas kernels, project(): pl.pallas_call(functools.partial(project_kernel, [part for _, part in par...  13.6 us
    unnamed x38, local copies, waits for them, and re-layouts  6.82 us
  transfers between devices with their start and end apart: 22, of which 12 were waited for; matrix products, arithmetic and copies ran while one was open for 4% of the time, Pallas kernels for 16%

profile of v4, /device:TPU:0, one launch (start us, length us, event | category | flops | bytes accessed | tf_op | source)
XLA Modules:
  0.0 176.3 jit_solution(9737161420780765867)
XLA Ops:
  0.6 3.4 %pack.1 = (bf16[1040,256]{1,0:T(8,128)(2,1)}, bf16[1040,256]{1,0:T(8,128)(2,1)}, bf16[1040,256]{1,0:T(8,128)(2,1)}, bf16[1040,256]{1,0:T(8,128)(2,1)}) custom-call(s32[2,4]{1,0:T(2,128)} %block_ids.1, s32[2]{0:T(128)} %block_count.1, bf16[256,1024]{1,0:T(8,128)(2,1)} %queries.1, bf16[256,1024]{1,0:T(8,128)(2,1)} %grad_out.1, bf16[2,256,1024]{2,1,0:T(8,128)(2,1)} %key_values.1), custom_call_target="tpu_custom_call" | custom-call | tf_op jit(solution)/shard_map/pack/pallas_call | solution.py:66
  4.0 4.0 %collective-permute-start.2 = (bf16[1040,256]{1,0:T(8,128)(2,1)}, bf16[1040,256]{1,0:T(8,128)(2,1)}, u32[]{:S(2)}, u32[]{:S(2)}) collective-permute-start(bf16[1040,256]{1,0:T(8,128)(2,1)} %get-tuple-element.40), channel_id=1, source_target_pairs={{0,12},{1,13},{2,14},{3,15},{4,8},{5,9},{6,10},{7,11},{8,4},{9,5},... | collective-permute-start | bytes 1597448 | tf_op jit(solution)/shard_map/ppermute | solution.py:29
  9.6 1.6 collective-permute-start.3
  12.0 9.3 %collective-permute-done.2.refs_3_ = bf16[1040,256]{1,0:T(8,128)(2,1)} collective-permute-done((bf16[1040,256]{1,0:T(8,128)(2,1)}, bf16[1040,256]{1,0:T(8,128)(2,1)}, u32[]{:S(2)}, u32[]{:S(2)}) %collective-permute-start.2) | collective-permute-done | bytes 532512 | tf_op jit(solution)/shard_map/ppermute | solution.py:29
  21.9 10.1 %collective-permute-done.1.refs_2_ = bf16[1040,256]{1,0:T(8,128)(2,1)} collective-permute-done((bf16[1040,256]{1,0:T(8,128)(2,1)}, bf16[1040,256]{1,0:T(8,128)(2,1)}, u32[]{:S(2)}, u32[]{:S(2)}) %collective-permute-start.1) | collective-permute-done | bytes 532512 | tf_op jit(solution)/shard_map/ppermute | solution.py:29
  34.6 2.7 %collective-permute-start.4 = (bf16[512,256]{1,0:T(8,128)(2,1)S(1)}, bf16[512,256]{1,0:T(8,128)(2,1)S(1)}, u32[]{:S(2)}, u32[]{:S(2)}) collective-permute-start(bf16[512,256]{1,0:T(8,128)(2,1)S(1)} %fusion.1), channel_id=1, source_target_pairs={{0,16},{1,17},{2,18},{3,19},{4,20},{5,21},{6,22},{7,23},{8,24},{9,... | collective-permute-start | bytes 786440 | tf_op jit(solution)/shard_map/ppermute | solution.py:29
  37.2 6.0 %attend.3 = (f32[2,10,128,256]{3,2,1,0:T(8,128)S(1)}, bf16[8,128,256]{2,1,0:T(8,128)(2,1)S(1)}) custom-call(s32[4,2,5]{2,1,0:T(2,128)S(1)} %maximum_convert_fusion.meta, s32[2]{0:T(128)S(1)} %pad_add_fusion.pos, bf16[1040,256]{1,0:T(8,128)(2,1)S(1)} %copy-done.6, bf16[1040,256]{1,0:T(8,128)(2,1)} %collective-permute-done.refs_1_, ...), custom_call_target="tpu_custom_call" | custom-call | flops 2013265920 | bytes 4194304 | tf_op jit(solution)/shard_map/attend/pallas_call | solution.py:189
  43.2 5.3 %collective-permute-done.4.refs_4_ = bf16[512,256]{1,0:T(8,128)(2,1)S(1)} collective-permute-done((bf16[512,256]{1,0:T(8,128)(2,1)S(1)}, bf16[512,256]{1,0:T(8,128)(2,1)S(1)}, u32[]{:S(2)}, u32[]{:S(2)}) %collective-permute-start.4) | collective-permute-done | bytes 262176 | tf_op jit(solution)/shard_map/ppermute | solution.py:29
  48.6 4.4 %attend.4 = (f32[2,10,128,256]{3,2,1,0:T(8,128)S(1)}, bf16[8,128,256]{2,1,0:T(8,128)(2,1)S(1)}, bf16[2,2,128,256]{3,2,1,0:T(8,128)(2,1)S(1)}) custom-call(s32[4,2,5]{2,1,0:T(2,128)S(1)} %maximum_convert_fusion.meta, s32[2]{0:T(128)S(1)} %pad_add_fusion.pos, bf16[1040,256]{1,0:T(8,128)(2,1)S(1)} %copy-done.6, ...), custom_call_target="tpu_custom_call", output_to_operand_aliasing={{0}: (7, {}), {1}: (8, {})} | custom-call | flops 1342177280 | bytes 4194304 | tf_op jit(solution)/shard_map/attend/pallas_call | solution.py:189
  53.1 5.9 %attend.5 = (f32[2,10,128,256]{3,2,1,0:T(8,128)S(1)}, bf16[8,128,256]{2,1,0:T(8,128)(2,1)S(1)}, bf16[2,128,256]{2,1,0:T(8,128)(2,1)S(1)}, bf16[2,128,256]{2,1,0:...) custom-call(s32[4,2,5]{2,1,0:T(2,128)S(1)} %maximum_convert_fusion.m, ...), custom_call_target="tpu_custom_call", output_to_operand_aliasing={{0}: (6, {}), {1}: (7, {})} | custom-call | flops 2013265920 | bytes 4194304 | tf_op jit(solution)/shard_map/attend/pallas_call | solution.py:189
  59.1 7.6 %collective-permute-done.5 = bf16[2,2,128,256]{3,2,1,0:T(8,128)(2,1)S(1)} collective-permute-done((bf16[2,2,128,256]{3,2,1,0:T(8,128)(2,1)S(1)}, bf16[2,2,128,256]{3,2,1,0:T(8,128)(2,1)S(1)}, u32[]{:S(2)}, u32[]{:S(2)}) %collective-permute-start.5) | collective-permute-done | bytes 262176 | tf_op jit(solution)/shard_map/ppermute | solution.py:29
  67.6 1.3 collective-permute-start.6
  68.9 1.8 %collective-permute-start.7 = (bf16[2048,256]{1,0:T(8,128)(2,1)S(1)}, bf16[2048,256]{1,0:T(8,128)(2,1)S(1)}, u32[]{:S(2)}, u32[]{:S(2)}) collective-permute-start(bf16[2048,256]{1,0:T(8,128)(2,1)S(1)} %bitcast.23), channel_id=1, source_target_pairs={{0,4},{1,5},{2,6},{3,7},{4,0},{5,1},{6,2},{7,3},{8,12},{9,13},{10,... | collective-permute-start | bytes 3145736 | tf_op jit(solution)/shard_map/ppermute | solution.py:29
  70.7 1.3 slice.46
  72.0 18.8 %collective-permute-done.6.refs_2_ = bf16[2048,256]{1,0:T(8,128)(2,1)} collective-permute-done((bf16[2048,256]{1,0:T(8,128)(2,1)S(1)}, bf16[2048,256]{1,0:T(8,128)(2,1)}, u32[]{:S(2)}, u32[]{:S(2)}) %collective-permute-start.6) | collective-permute-done | bytes 1048608 | tf_op jit(solution)/shard_map/ppermute | solution.py:29
  91.8 5.1 %collective-permute-start.14 = (bf16[2,384,1024]{2,1,0:T(8,128)(2,1)}, bf16[2,384,1024]{2,1,0:T(8,128)(2,1)}, u32[]{:S(2)}, u32[]{:S(2)}) collective-permute-start(bf16[2,384,1024]{2,1,0:T(8,128)(2,1)} %slice.46), channel_id=1, source_target_pairs={{0,24},{1,25},{2,26},{3,27},{4,28},{5,29},{6,30},{7,31},{24,0},{25... | collective-permute-start | bytes 4718600 | tf_op jit(solution)/shard_map/ppermute | solution.py:29
  97.9 1.8 %collective-permute-start.9 = (bf16[2048,256]{1,0:T(8,128)(2,1)}, bf16[2048,256]{1,0:T(8,128)(2,1)}, u32[]{:S(2)}, u32[]{:S(2)}) collective-permute-start(bf16[2048,256]{1,0:T(8,128)(2,1)} %collective-permute-done.6.refs_2_), channel_id=1, source_target_pairs={{0,4},{1,5},{2,6},{3,7},{4,0},{5,1},{6,2},{7,3},{8,12},{9,13},{10,... | collective-permute-start | bytes 3145736 | tf_op jit(solution)/shard_map/ppermute | solution.py:29
  100.7 21.6 %collective-permute-done.9.refs_3_ = bf16[2048,256]{1,0:T(8,128)(2,1)} collective-permute-done((bf16[2048,256]{1,0:T(8,128)(2,1)}, bf16[2048,256]{1,0:T(8,128)(2,1)}, u32[]{:S(2)}, u32[]{:S(2)}) %collective-permute-start.9) | collective-permute-done | bytes 1048608 | tf_op jit(solution)/shard_map/ppermute | solution.py:29
  122.3 2.2 %collective-permute-start.15 = (bf16[2,128,1024]{2,1,0:T(8,128)(2,1)}, bf16[2,128,1024]{2,1,0:T(8,128)(2,1)S(1)}, u32[]{:S(2)}, u32[]{:S(2)}) collective-permute-start(bf16[2,128,1024]{2,1,0:T(8,128)(2,1)} %slice.47), channel_id=1, source_target_pairs={{0,24},{1,25},{2,26},{3,27},{4,28},{5,29},{6,30},{7,31},{24,0},{25... | collective-permute-start | bytes 1572872 | tf_op jit(solution)/shard_map/ppermute | solution.py:29
  125.7 5.1 %project.3 = (bf16[2,256,512]{2,1,0:T(8,128)(2,1)}, bf16[2,256,512]{2,1,0:T(8,128)(2,1)S(1)}) custom-call(s32[7]{0:T(128)S(1)} %stack.74.pos, bf16[2048,256]{1,0:T(8,128)(2,1)S(1)} %bitcast.24, bf16[2048,256]{1,0:T(8,128)(2,1)S(1)} %copy-done.4, bf16[2048,256]{1,0:T(8,128)(2,1)} %collective-permute-done.6.refs_2_, ...), custom_call_target="tpu_custom_call" | custom-call | flops 2147483648 | bytes 6291456 | tf_op jit(solution)/shard_map/project/pallas_call | solution.py:259
  131.7 1.5 collective-permute-done.14.refs_6_
  133.1 5.5 %project.4 = (bf16[2,256,384]{2,1,0:T(8,128)(2,1)S(1)}, bf16[2,256,384]{2,1,0:T(8,128)(2,1)S(1)}) custom-call(s32[7]{0:T(128)S(1)} %stack.74.pos, bf16[2048,256]{1,0:T(8,128)(2,1)S(1)} %bitcast.25, bf16[2048,256]{1,0:T(8,128)(2,1)S(1)} %copy-done.5, bf16[2048,256]{1,0:T(8,128)(2,1)} %collective-permute-done.6.refs_2_, ...), custom_call_target="tpu_custom_call" | custom-call | flops 1610612736 | bytes 6291456 | tf_op jit(solution)/shard_map/project/pallas_call | solution.py:259
  138.8 3.6 %collective-permute-start.11 = (bf16[256,256]{1,0:T(8,128)(2,1)S(1)}, bf16[256,256]{1,0:T(8,128)(2,1)}, u32[]{:S(2)}, u32[]{:S(2)}) collective-permute-start(bf16[256,256]{1,0:T(8,128)(2,1)S(1)} %bitcast.29), channel_id=1, source_target_pairs={{0,8},{1,9},{2,10},{3,11},{4,12},{5,13},{6,14},{7,15},{8,0},{9,1},... | collective-permute-start | bytes 393224 | tf_op jit(solution)/shard_map/ppermute | solution.py:29
  142.9 1.8 collective-permute-start.10
  144.7 2.9 %project.5 = (bf16[2,256,128]{2,1,0:T(8,128)(2,1)S(1)}, bf16[2,256,128]{2,1,0:T(8,128)(2,1)S(1)}) custom-call(s32[7]{0:T(128)S(1)} %stack.74.pos, bf16[2048,256]{1,0:T(8,128)(2,1)S(1)} %bitcast.26, bf16[2048,256]{1,0:T(8,128)(2,1)S(1)} %copy-done.5, bf16[2048,256]{1,0:T(8,128)(2,1)} %collective-permute-done.6.refs_2_, ...), custom_call_target="tpu_custom_call" | custom-call | flops 536870912 | bytes 6291456 | tf_op jit(solution)/shard_map/project/pallas_call | solution.py:259
  151.1 2.8 %merge.1 = (bf16[256,512]{1,0:T(8,128)(2,1)}, bf16[256,512]{1,0:T(8,128)(2,1)}, bf16[256,512]{1,0:T(8,128)(2,1)}, bf16[256,512]{1,0:T(8,128)(2,1)}) custom-call(s32[1]{0:T(128)} %bitcast.12.flip, bf16[2,256,512]{2,1,0:T(8,128)(2,1)} %copy-done.7, bf16[2,256,512]{2,1,0:T(8,128)(2,1)} %copy-done.11, bf16[2,256,384]{2,1,0:T(8,128)(2,1)} %copy-done.8, ...), custom_call_target="tpu_custom_call" | custom-call | tf_op jit(solution)/shard_map/merge/pallas_call | solution.py:304
  153.8 1.6 collective-permute-start.18
  155.4 2.3 %collective-permute-start.19 = (bf16[256,512]{1,0:T(8,128)(2,1)}, bf16[256,512]{1,0:T(8,128)(2,1)S(1)}, u32[]{:S(2)}, u32[]{:S(2)}) collective-permute-start(bf16[256,512]{1,0:T(8,128)(2,1)} %get-tuple-element.69), channel_id=1, source_target_pairs={{0,3},{1,11},{2,0},{3,8},{4,7},{5,15},{6,4},{7,12},{8,2},{9,10},{1... | collective-permute-start | bytes 786440 | tf_op jit(solution)/shard_map/ppermute | solution.py:29
  159.1 2.0 %place_columns.1 = bf16[256,1024]{1,0:T(8,128)(2,1)} custom-call(s32[1]{0:T(128)} %bitcast.pos, bf16[256,256]{1,0:T(8,128)(2,1)} %bitcast.27, bf16[256,256]{1,0:T(8,128)(2,1)} %collective-permute-done.10.refs_1_, bf16[256,256]{1,0:T(8,128)(2,1)} %collective-permute-done.11.refs_2_, bf16[256,256]{1,0:T(8,128)(2,1)} %copy-done.18), custom_call_target="tpu_custom_call" | custom-call | tf_op jit(solution)/shard_map/place_columns/pallas_call | solution.py:344
  161.1 4.1 %collective-permute-done.19.refs_1_ = bf16[256,512]{1,0:T(8,128)(2,1)S(1)} collective-permute-done((bf16[256,512]{1,0:T(8,128)(2,1)}, bf16[256,512]{1,0:T(8,128)(2,1)S(1)}, u32[]{:S(2)}, u32[]{:S(2)}) %collective-permute-start.19) | collective-permute-done | bytes 262176 | tf_op jit(solution)/shard_map/ppermute | solution.py:29
  165.1 8.4 %collective-permute-done.21.refs_3_ = bf16[256,512]{1,0:T(8,128)(2,1)S(1)} collective-permute-done((bf16[256,512]{1,0:T(8,128)(2,1)}, bf16[256,512]{1,0:T(8,128)(2,1)S(1)}, u32[]{:S(2)}, u32[]{:S(2)}) %collective-permute-start.21) | collective-permute-done | bytes 262176 | tf_op jit(solution)/shard_map/ppermute | solution.py:29
  174.2 2.1 %collect.1 = bf16[256,1024]{1,0:T(8,128)(2,1)} custom-call(s32[1]{0:T(128)} %bitcast.11.pos, bf16[256,512]{1,0:T(8,128)(2,1)} %copy-done.13, bf16[256,512]{1,0:T(8,128)(2,1)} %copy-done.14, bf16[256,512]{1,0:T(8,128)(2,1)} %copy-done.15, bf16[256,512]{1,0:T(8,128)(2,1)} %copy-done.16), custom_call_target="tpu_custom_call" | custom-call | tf_op jit(solution)/shard_map/collect/pallas_call | solution.py:324
  (74 shorter events, 17.7 us)
Async XLA Ops:
  0.6 8.0 %copy-start = (bf16[2,512,1024]{2,1,0:T(8,128)(2,1)S(1)}, bf16[2,512,1024]{2,1,0:T(8,128)(2,1)}, u32[]{:S(2)}) copy-start(bf16[2,512,1024]{2,1,0:T(8,128)(2,1)} %refs_4_.1) | copy-start | bytes 6291460
  4.0 29.3 %copy-start.6 = (bf16[1040,256]{1,0:T(8,128)(2,1)S(1)}, bf16[1040,256]{1,0:T(8,128)(2,1)}, u32[]{:S(2)}) copy-start(bf16[1040,256]{1,0:T(8,128)(2,1)} %get-tuple-element.37.refs_0_) | copy-start | bytes 1597444
  4.0 17.2 %collective-permute-start.2 = (bf16[1040,256]{1,0:T(8,128)(2,1)}, bf16[1040,256]{1,0:T(8,128)(2,1)}, u32[]{:S(2)}, u32[]{:S(2)}) collective-permute-start(bf16[1040,256]{1,0:T(8,128)(2,1)} %get-tuple-element.40), channel_id=1, source_target_pairs={{0,12},{1,13},{2,14},{3,15},{4,8},{5,9},{6,10},{7,11},{8,4},{9,5},... | collective-permute-start | bytes 1597448 | tf_op jit(solution)/shard_map/ppermute | solution.py:29
  8.0 24.0 %collective-permute-start.1 = (bf16[1040,256]{1,0:T(8,128)(2,1)}, bf16[1040,256]{1,0:T(8,128)(2,1)}, u32[]{:S(2)}, u32[]{:S(2)}) collective-permute-start(bf16[1040,256]{1,0:T(8,128)(2,1)} %get-tuple-element.39), channel_id=1, source_target_pairs={{0,8},{1,9},{2,10},{3,11},{4,12},{5,13},{6,14},{7,15},{8,0},{9,1},... | collective-permute-start | bytes 1597448 | tf_op jit(solution)/shard_map/ppermute | solution.py:29
  8.4 24.3 %collective-permute-start = (bf16[1040,256]{1,0:T(8,128)(2,1)}, bf16[1040,256]{1,0:T(8,128)(2,1)}, u32[]{:S(2)}, u32[]{:S(2)}) collective-permute-start(bf16[1040,256]{1,0:T(8,128)(2,1)} %get-tuple-element.38), channel_id=1, source_target_pairs={{0,4},{1,5},{2,6},{3,7},{4,0},{5,1},{6,2},{7,3},{8,12},{9,13},{10,... | collective-permute-start | bytes 1597448 | tf_op jit(solution)/shard_map/ppermute | solution.py:29
  9.6 24.9 %collective-permute-start.3 = (bf16[2,224,1024]{2,1,0:T(8,128)(2,1)}, bf16[2,224,1024]{2,1,0:T(8,128)(2,1)}, u32[]{:S(2)}, u32[]{:S(2)}) collective-permute-start(bf16[2,224,1024]{2,1,0:T(8,128)(2,1)} %slice.44), channel_id=1, source_target_pairs={{8,16},{9,17},{10,18},{11,19},{12,20},{13,21},{14,22},{15,23},{16,... | collective-permute-start | bytes 2752520 | tf_op jit(solution)/shard_map/ppermute | solution.py:29
  34.6 14.0 %collective-permute-start.4 = (bf16[512,256]{1,0:T(8,128)(2,1)S(1)}, bf16[512,256]{1,0:T(8,128)(2,1)S(1)}, u32[]{:S(2)}, u32[]{:S(2)}) collective-permute-start(bf16[512,256]{1,0:T(8,128)(2,1)S(1)} %fusion.1), channel_id=1, source_target_pairs={{0,16},{1,17},{2,18},{3,19},{4,20},{5,21},{6,22},{7,23},{8,24},{9,... | collective-permute-start | bytes 786440 | tf_op jit(solution)/shard_map/ppermute | solution.py:29
  52.9 13.7 %collective-permute-start.5 = (bf16[2,2,128,256]{3,2,1,0:T(8,128)(2,1)S(1)}, bf16[2,2,128,256]{3,2,1,0:T(8,128)(2,1)S(1)}, u32[]{:S(2)}, u32[]{:S(2)}) collective-permute-start(bf16[2,2,128,256]{3,2,1,0:T(8,128)(2,1)S(1)} %get-tuple-element.51), channel_id=1, source_target_pairs={{0,16},{1,17},{2,18},{3,19},{4,20},{5,21},{6,22},{7,23},{8,24},{9,... | collective-permute-start | bytes 786440 | tf_op jit(solution)/shard_map/ppermute | solution.py:29
  59.1 8.4 %copy-start.10 = (bf16[2,128,256]{2,1,0:T(8,128)(2,1)}, bf16[2,128,256]{2,1,0:T(8,128)(2,1)S(1)}, u32[]{:S(2)}) copy-start(bf16[2,128,256]{2,1,0:T(8,128)(2,1)S(1)} %get-tuple-element.47) | copy-start | bytes 393220
  66.6 24.1 %collective-permute-start.8 = (bf16[2,288,1024]{2,1,0:T(8,128)(2,1)S(1)}, bf16[2,288,1024]{2,1,0:T(8,128)(2,1)S(1)}, u32[]{:S(2)}, u32[]{:S(2)}) collective-permute-start(bf16[2,288,1024]{2,1,0:T(8,128)(2,1)S(1)} %slice.45), channel_id=1, source_target_pairs={{8,16},{9,17},{10,18},{11,19},{12,20},{13,21},{14,22},{15,23},{16,... | collective-permute-start | bytes 3538952 | tf_op jit(solution)/shard_map/ppermute | solution.py:29
  67.6 23.2 %collective-permute-start.6 = (bf16[2048,256]{1,0:T(8,128)(2,1)S(1)}, bf16[2048,256]{1,0:T(8,128)(2,1)}, u32[]{:S(2)}, u32[]{:S(2)}) collective-permute-start(bf16[2048,256]{1,0:T(8,128)(2,1)S(1)} %bitcast.22), channel_id=1, source_target_pairs={{0,8},{1,9},{2,10},{3,11},{4,12},{5,13},{6,14},{7,15},{8,0},{9,1},... | collective-permute-start | bytes 3145736 | tf_op jit(solution)/shard_map/ppermute | solution.py:29
  68.9 28.0 %collective-permute-start.7 = (bf16[2048,256]{1,0:T(8,128)(2,1)S(1)}, bf16[2048,256]{1,0:T(8,128)(2,1)S(1)}, u32[]{:S(2)}, u32[]{:S(2)}) collective-permute-start(bf16[2048,256]{1,0:T(8,128)(2,1)S(1)} %bitcast.23), channel_id=1, source_target_pairs={{0,4},{1,5},{2,6},{3,7},{4,0},{5,1},{6,2},{7,3},{8,12},{9,13},{10,... | collective-permute-start | bytes 3145736 | tf_op jit(solution)/shard_map/ppermute | solution.py:29
  91.8 41.3 %collective-permute-start.14 = (bf16[2,384,1024]{2,1,0:T(8,128)(2,1)}, bf16[2,384,1024]{2,1,0:T(8,128)(2,1)}, u32[]{:S(2)}, u32[]{:S(2)}) collective-permute-start(bf16[2,384,1024]{2,1,0:T(8,128)(2,1)} %slice.46), channel_id=1, source_target_pairs={{0,24},{1,25},{2,26},{3,27},{4,28},{5,29},{6,30},{7,31},{24,0},{25... | collective-permute-start | bytes 4718600 | tf_op jit(solution)/shard_map/ppermute | solution.py:29
  97.9 24.4 %collective-permute-start.9 = (bf16[2048,256]{1,0:T(8,128)(2,1)}, bf16[2048,256]{1,0:T(8,128)(2,1)}, u32[]{:S(2)}, u32[]{:S(2)}) collective-permute-start(bf16[2048,256]{1,0:T(8,128)(2,1)} %collective-permute-done.6.refs_2_), channel_id=1, source_target_pairs={{0,4},{1,5},{2,6},{3,7},{4,0},{5,1},{6,2},{7,3},{8,12},{9,13},{10,... | collective-permute-start | bytes 3145736 | tf_op jit(solution)/shard_map/ppermute | solution.py:29
  100.7 32.4 %copy-start.2 = (bf16[2,288,1024]{2,1,0:T(8,128)(2,1)S(1)}, bf16[2,288,1024]{2,1,0:T(8,128)(2,1)}, u32[]{:S(2)}) copy-start(bf16[2,288,1024]{2,1,0:T(8,128)(2,1)} %copy-done.1) | copy-start | bytes 3538948
  122.3 20.6 %collective-permute-start.15 = (bf16[2,128,1024]{2,1,0:T(8,128)(2,1)}, bf16[2,128,1024]{2,1,0:T(8,128)(2,1)S(1)}, u32[]{:S(2)}, u32[]{:S(2)}) collective-permute-start(bf16[2,128,1024]{2,1,0:T(8,128)(2,1)} %slice.47), channel_id=1, source_target_pairs={{0,24},{1,25},{2,26},{3,27},{4,28},{5,29},{6,30},{7,31},{24,0},{25... | collective-permute-start | bytes 1572872 | tf_op jit(solution)/shard_map/ppermute | solution.py:29
  124.5 1.2 copy-start.4
  125.7 7.4 %copy-start.5 = (bf16[2048,256]{1,0:T(8,128)(2,1)S(1)}, bf16[2048,256]{1,0:T(8,128)(2,1)}, u32[]{:S(2)}) copy-start(bf16[2048,256]{1,0:T(8,128)(2,1)} %copy-done.3) | copy-start | bytes 3145732
  131.6 17.5 %collective-permute-start.13 = (bf16[2,256,512]{2,1,0:T(8,128)(2,1)}, bf16[2,256,512]{2,1,0:T(8,128)(2,1)S(1)}, u32[]{:S(2)}, u32[]{:S(2)}) collective-permute-start(bf16[2,256,512]{2,1,0:T(8,128)(2,1)} %get-tuple-element.60), channel_id=1, source_target_pairs={{0,1},{1,0},{2,3},{3,2},{4,5},{5,4},{6,7},{7,6},{8,9},{9,8},{10,11... | collective-permute-start | bytes 1572872 | tf_op jit(solution)/shard_map/ppermute | solution.py:29
  138.6 9.0 %copy-start.8 = (bf16[2,256,384]{2,1,0:T(8,128)(2,1)}, bf16[2,256,384]{2,1,0:T(8,128)(2,1)S(1)}, u32[]{:S(2)}) copy-start(bf16[2,256,384]{2,1,0:T(8,128)(2,1)S(1)} %get-tuple-element.62.refs_2_) | copy-start | bytes 1179652
  138.7 11.6 %collective-permute-start.16 = (bf16[2,256,384]{2,1,0:T(8,128)(2,1)S(1)}, bf16[2,256,384]{2,1,0:T(8,128)(2,1)S(1)}, u32[]{:S(2)}, u32[]{:S(2)}) collective-permute-start(bf16[2,256,384]{2,1,0:T(8,128)(2,1)S(1)} %get-tuple-element.66), channel_id=1, source_target_pairs={{0,1},{1,0},{2,3},{3,2},{4,5},{5,4},{6,7},{7,6},{8,9},{9,8},{10,11... | collective-permute-start | bytes 1179656 | tf_op jit(solution)/shard_map/ppermute | solution.py:29
  138.7 9.5 %collective-permute-start.12 = (bf16[256,256]{1,0:T(8,128)(2,1)S(1)}, bf16[256,256]{1,0:T(8,128)(2,1)S(1)}, u32[]{:S(2)}, u32[]{:S(2)}) collective-permute-start(bf16[256,256]{1,0:T(8,128)(2,1)S(1)} %bitcast.30), channel_id=1, source_target_pairs={{0,12},{1,13},{2,14},{3,15},{4,8},{5,9},{6,10},{7,11},{8,4},{9,5},... | collective-permute-start | bytes 393224 | tf_op jit(solution)/shard_map/ppermute | solution.py:29
  138.8 10.3 %collective-permute-start.11 = (bf16[256,256]{1,0:T(8,128)(2,1)S(1)}, bf16[256,256]{1,0:T(8,128)(2,1)}, u32[]{:S(2)}, u32[]{:S(2)}) collective-permute-start(bf16[256,256]{1,0:T(8,128)(2,1)S(1)} %bitcast.29), channel_id=1, source_target_pairs={{0,8},{1,9},{2,10},{3,11},{4,12},{5,13},{6,14},{7,15},{8,0},{9,1},... | collective-permute-start | bytes 393224 | tf_op jit(solution)/shard_map/ppermute | solution.py:29
  142.9 6.3 %collective-permute-start.10 = (bf16[256,256]{1,0:T(8,128)(2,1)S(1)}, bf16[256,256]{1,0:T(8,128)(2,1)}, u32[]{:S(2)}, u32[]{:S(2)}) collective-permute-start(bf16[256,256]{1,0:T(8,128)(2,1)S(1)} %bitcast.28), channel_id=1, source_target_pairs={{0,4},{1,5},{2,6},{3,7},{4,0},{5,1},{6,2},{7,3},{8,12},{9,13},{10,... | collective-permute-start | bytes 393224 | tf_op jit(solution)/shard_map/ppermute | solution.py:29
  148.9 1.3 collective-permute-start.17
  153.8 7.2 %collective-permute-start.18 = (bf16[256,512]{1,0:T(8,128)(2,1)}, bf16[256,512]{1,0:T(8,128)(2,1)S(1)}, u32[]{:S(2)}, u32[]{:S(2)}) collective-permute-start(bf16[256,512]{1,0:T(8,128)(2,1)} %get-tuple-element.68), channel_id=1, source_target_pairs={{0,0},{1,8},{2,3},{3,11},{4,4},{5,12},{6,7},{7,15},{8,1},{9,9},{10... | collective-permute-start | bytes 786440 | tf_op jit(solution)/shard_map/ppermute | solution.py:29
  155.4 9.7 %collective-permute-start.19 = (bf16[256,512]{1,0:T(8,128)(2,1)}, bf16[256,512]{1,0:T(8,128)(2,1)S(1)}, u32[]{:S(2)}, u32[]{:S(2)}) collective-permute-start(bf16[256,512]{1,0:T(8,128)(2,1)} %get-tuple-element.69), channel_id=1, source_target_pairs={{0,3},{1,11},{2,0},{3,8},{4,7},{5,15},{6,4},{7,12},{8,2},{9,10},{1... | collective-permute-start | bytes 786440 | tf_op jit(solution)/shard_map/ppermute | solution.py:29
  157.8 7.4 %collective-permute-start.20 = (bf16[256,512]{1,0:T(8,128)(2,1)}, bf16[256,512]{1,0:T(8,128)(2,1)S(1)}, u32[]{:S(2)}, u32[]{:S(2)}) collective-permute-start(bf16[256,512]{1,0:T(8,128)(2,1)} %get-tuple-element.70), channel_id=1, source_target_pairs={{0,4},{1,12},{2,7},{3,15},{4,0},{5,8},{6,3},{7,11},{8,5},{9,13},{1... | collective-permute-start | bytes 786440 | tf_op jit(solution)/shard_map/ppermute | solution.py:29
  158.2 15.3 %collective-permute-start.21 = (bf16[256,512]{1,0:T(8,128)(2,1)}, bf16[256,512]{1,0:T(8,128)(2,1)S(1)}, u32[]{:S(2)}, u32[]{:S(2)}) collective-permute-start(bf16[256,512]{1,0:T(8,128)(2,1)} %get-tuple-element.71), channel_id=1, source_target_pairs={{0,7},{1,15},{2,4},{3,12},{4,3},{5,11},{6,0},{7,8},{8,6},{9,14},{1... | collective-permute-start | bytes 786440 | tf_op jit(solution)/shard_map/ppermute | solution.py:29
  161.1 12.5 %copy-start.13 = (bf16[256,512]{1,0:T(8,128)(2,1)}, bf16[256,512]{1,0:T(8,128)(2,1)S(1)}, u32[]{:S(2)}) copy-start(bf16[256,512]{1,0:T(8,128)(2,1)S(1)} %collective-permute-done.18.refs_0_) | copy-start | bytes 786436
  165.1 8.4 %copy-start.14 = (bf16[256,512]{1,0:T(8,128)(2,1)}, bf16[256,512]{1,0:T(8,128)(2,1)S(1)}, u32[]{:S(2)}) copy-start(bf16[256,512]{1,0:T(8,128)(2,1)S(1)} %collective-permute-done.19.refs_1_) | copy-start | bytes 786436
  165.1 8.4 %copy-start.15 = (bf16[256,512]{1,0:T(8,128)(2,1)}, bf16[256,512]{1,0:T(8,128)(2,1)S(1)}, u32[]{:S(2)}) copy-start(bf16[256,512]{1,0:T(8,128)(2,1)S(1)} %collective-permute-done.20.refs_2_) | copy-start | bytes 786436
  (9 other events, 7.4 us)

commit v5 on v4

--- a/solution.py
+++ b/solution.py
@@ -452,8 +452,9 @@
     grads = jnp.concatenate([inner, edge], axis=1).reshape(-1, width)
     dq = [block.reshape(rows_here, width) for block in dq]
     if paired:
-        middles.append(middle(after(rows_of(middle_cuts, 1), returned)))
-    near, beside = swap(grads, 1), swap(grads, 2)
+        middles.append(middle(after(rows_of(middle_cuts, 1), inner)))
+    near = swap(grads, 1)
+    beside = jnp.concatenate([swap(inner, 2), swap(edge, 2)], axis=1).reshape(-1, width)
     if paired:
         far = [ends(after(rows_of(end_cuts, 0), beside, middles[1]))]
         beside = after(beside, near, middles[1])

time: 177 us -> 175 us (0.989)
  waiting for transfers between devices: 88.4 us -> 82.3 us
  local copies, waits for them, and re-layouts: 12.8 us -> 16 us
  starting transfers between devices: 32.7 us -> 35.8 us
  Pallas kernels: 40.1 us -> 38.2 us
    ppermute x22 -> x23, waiting for transfers between devices: 88.4 us -> 82.3 us  [send(): return lax.ppermute(block, AXES, pairs)]
    ppermute x22 -> x23, starting transfers between devices: 32.7 us -> 35.8 us  [send(): return lax.ppermute(block, AXES, pairs)]
    pallas_call x3, Pallas kernels: 13.6 us -> 11.1 us  [project(): pl.pallas_call(functools.partial(project_kernel, [part for _, part in par...]
    unnamed x38 -> x40, local copies, waits for them, and re-layouts: 6.82 us -> 8.94 us
  transfers between devices with their start and end apart: 22 -> 23, of which waited for: 12 -> 13; matrix products, arithmetic and copies ran while one was open for 4% -> 5% of each run, Pallas kernels for 16% -> 15%
where the time goes in v5:
time: 175 us
  waiting for transfers between devices  82.3 us (47%)
  Pallas kernels  38.2 us (22%)
  starting transfers between devices  35.8 us (20%)
  local copies, waits for them, and re-layouts  16 us (9%)
    ppermute x23, waiting for transfers between devices, send(): return lax.ppermute(block, AXES, pairs)  82.3 us
    ppermute x23, starting transfers between devices, send(): return lax.ppermute(block, AXES, pairs)  35.8 us
    pallas_call x3, Pallas kernels, attend(): pl.pallas_call(functools.partial(attend_kernel, span, n_halo, bool(halos)...  17 us
    pallas_call x3, Pallas kernels, project(): pl.pallas_call(functools.partial(project_kernel, [part for _, part in par...  11.1 us
    unnamed x40, local copies, waits for them, and re-layouts  8.94 us
    slice x4, local copies, waits for them, and re-layouts, rows_of(): return kv_weight[:, cuts[n] * unit:cuts[n + 1] * unit]  4.25 us
  transfers between devices with their start and end apart: 23, of which 13 were waited for; matrix products, arithmetic and copies ran while one was open for 5% of the time, Pallas kernels for 15%

profile of v5, /device:TPU:0, one launch (start us, length us, event | category | flops | bytes accessed | tf_op | source)
XLA Modules:
  0.0 174.6 jit_solution(11183679495569340575)
XLA Ops:
  0.6 3.3 %pack.1 = (bf16[1040,256]{1,0:T(8,128)(2,1)}, bf16[1040,256]{1,0:T(8,128)(2,1)}, bf16[1040,256]{1,0:T(8,128)(2,1)}, bf16[1040,256]{1,0:T(8,128)(2,1)}) custom-call(s32[2,4]{1,0:T(2,128)} %block_ids.1, s32[2]{0:T(128)} %block_count.1, bf16[256,1024]{1,0:T(8,128)(2,1)} %queries.1, bf16[256,1024]{1,0:T(8,128)(2,1)} %grad_out.1, bf16[2,256,1024]{2,1,0:T(8,128)(2,1)} %key_values.1), custom_call_target="tpu_custom_call" | custom-call | tf_op jit(solution)/shard_map/pack/pallas_call | solution.py:66
  4.0 4.0 %collective-permute-start.2 = (bf16[1040,256]{1,0:T(8,128)(2,1)}, bf16[1040,256]{1,0:T(8,128)(2,1)}, u32[]{:S(2)}, u32[]{:S(2)}) collective-permute-start(bf16[1040,256]{1,0:T(8,128)(2,1)} %get-tuple-element.40), channel_id=1, source_target_pairs={{0,12},{1,13},{2,14},{3,15},{4,8},{5,9},{6,10},{7,11},{8,4},{9,5},... | collective-permute-start | bytes 1597448 | tf_op jit(solution)/shard_map/ppermute | solution.py:29
  9.6 1.6 collective-permute-start.3
  11.9 9.3 %collective-permute-done.2.refs_3_ = bf16[1040,256]{1,0:T(8,128)(2,1)} collective-permute-done((bf16[1040,256]{1,0:T(8,128)(2,1)}, bf16[1040,256]{1,0:T(8,128)(2,1)}, u32[]{:S(2)}, u32[]{:S(2)}) %collective-permute-start.2) | collective-permute-done | bytes 532512 | tf_op jit(solution)/shard_map/ppermute | solution.py:29
  21.9 10.1 %collective-permute-done.1.refs_2_ = bf16[1040,256]{1,0:T(8,128)(2,1)} collective-permute-done((bf16[1040,256]{1,0:T(8,128)(2,1)}, bf16[1040,256]{1,0:T(8,128)(2,1)}, u32[]{:S(2)}, u32[]{:S(2)}) %collective-permute-start.1) | collective-permute-done | bytes 532512 | tf_op jit(solution)/shard_map/ppermute | solution.py:29
  34.5 2.7 %collective-permute-start.4 = (bf16[512,256]{1,0:T(8,128)(2,1)S(1)}, bf16[512,256]{1,0:T(8,128)(2,1)S(1)}, u32[]{:S(2)}, u32[]{:S(2)}) collective-permute-start(bf16[512,256]{1,0:T(8,128)(2,1)S(1)} %fusion.1), channel_id=1, source_target_pairs={{0,16},{1,17},{2,18},{3,19},{4,20},{5,21},{6,22},{7,23},{8,24},{9,... | collective-permute-start | bytes 786440 | tf_op jit(solution)/shard_map/ppermute | solution.py:29
  37.2 6.0 %attend.3 = (f32[2,10,128,256]{3,2,1,0:T(8,128)S(1)}, bf16[8,128,256]{2,1,0:T(8,128)(2,1)S(1)}) custom-call(s32[4,2,5]{2,1,0:T(2,128)S(1)} %maximum_convert_fusion.meta, s32[2]{0:T(128)S(1)} %pad_add_fusion.pos, bf16[1040,256]{1,0:T(8,128)(2,1)S(1)} %copy-done.7, bf16[1040,256]{1,0:T(8,128)(2,1)} %collective-permute-done.refs_1_, ...), custom_call_target="tpu_custom_call" | custom-call | flops 2013265920 | bytes 4194304 | tf_op jit(solution)/shard_map/attend/pallas_call | solution.py:189
  43.1 5.4 %collective-permute-done.4.refs_4_ = bf16[512,256]{1,0:T(8,128)(2,1)S(1)} collective-permute-done((bf16[512,256]{1,0:T(8,128)(2,1)S(1)}, bf16[512,256]{1,0:T(8,128)(2,1)S(1)}, u32[]{:S(2)}, u32[]{:S(2)}) %collective-permute-start.4) | collective-permute-done | bytes 262176 | tf_op jit(solution)/shard_map/ppermute | solution.py:29
  48.5 4.4 %attend.4 = (f32[2,10,128,256]{3,2,1,0:T(8,128)S(1)}, bf16[8,128,256]{2,1,0:T(8,128)(2,1)S(1)}, bf16[2,2,128,256]{3,2,1,0:T(8,128)(2,1)S(1)}) custom-call(s32[4,2,5]{2,1,0:T(2,128)S(1)} %maximum_convert_fusion.meta, s32[2]{0:T(128)S(1)} %pad_add_fusion.pos, bf16[1040,256]{1,0:T(8,128)(2,1)S(1)} %copy-done.7, ...), custom_call_target="tpu_custom_call", output_to_operand_aliasing={{0}: (7, {}), {1}: (8, {})} | custom-call | flops 1342177280 | bytes 4194304 | tf_op jit(solution)/shard_map/attend/pallas_call | solution.py:189
  53.1 6.7 %attend.5 = (f32[2,10,128,256]{3,2,1,0:T(8,128)S(1)}, bf16[8,128,256]{2,1,0:T(8,128)(2,1)S(1)}, bf16[2,128,256]{2,1,0:T(8,128)(2,1)S(1)}, bf16[2,128,256]{2,1,0:...) custom-call(s32[4,2,5]{2,1,0:T(2,128)S(1)} %maximum_convert_fusion.m, ...), custom_call_target="tpu_custom_call", output_to_operand_aliasing={{0}: (6, {}), {1}: (7, {})} | custom-call | flops 2013265920 | bytes 4194304 | tf_op jit(solution)/shard_map/attend/pallas_call | solution.py:189
  61.1 5.3 %collective-permute-start.5 = (bf16[2,6,128,256]{3,2,1,0:T(8,128)(2,1)S(1)}, bf16[2,6,128,256]{3,2,1,0:T(8,128)(2,1)S(1)}, u32[]{:S(2)}, u32[]{:S(2)}) collective-permute-start(bf16[2,6,128,256]{3,2,1,0:T(8,128)(2,1)S(1)} %get-tuple-element.49), channel_id=1, source_target_pairs={{0,8},{1,9},{2,10},{3,11},{4,12},{5,13},{6,14},{7,15},{8,0},{9,1},... | collective-permute-start | bytes 2359304 | tf_op jit(solution)/shard_map/ppermute | solution.py:29
  66.7 1.9 %collective-permute-start.8 = (bf16[2048,256]{1,0:T(8,128)(2,1)S(1)}, bf16[2048,256]{1,0:T(8,128)(2,1)S(1)}, u32[]{:S(2)}, u32[]{:S(2)}) collective-permute-start(bf16[2048,256]{1,0:T(8,128)(2,1)S(1)} %bitcast.23), channel_id=1, source_target_pairs={{0,4},{1,5},{2,6},{3,7},{4,0},{5,1},{6,2},{7,3},{8,12},{9,13},{10,... | collective-permute-start | bytes 3145736 | tf_op jit(solution)/shard_map/ppermute | solution.py:29
  69.9 19.6 %collective-permute-done.7 = bf16[2,2,128,256]{3,2,1,0:T(8,128)(2,1)S(1)} collective-permute-done((bf16[2,2,128,256]{3,2,1,0:T(8,128)(2,1)S(1)}, bf16[2,2,128,256]{3,2,1,0:T(8,128)(2,1)S(1)}, u32[]{:S(2)}, u32[]{:S(2)}) %collective-permute-start.7) | collective-permute-done | bytes 262176 | tf_op jit(solution)/shard_map/ppermute | solution.py:29
  90.6 4.5 %collective-permute-start.15 = (bf16[2,384,1024]{2,1,0:T(8,128)(2,1)}, bf16[2,384,1024]{2,1,0:T(8,128)(2,1)}, u32[]{:S(2)}, u32[]{:S(2)}) collective-permute-start(bf16[2,384,1024]{2,1,0:T(8,128)(2,1)} %slice.46), channel_id=1, source_target_pairs={{0,24},{1,25},{2,26},{3,27},{4,28},{5,29},{6,30},{7,31},{24,0},{25... | collective-permute-start | bytes 4718600 | tf_op jit(solution)/shard_map/ppermute | solution.py:29
  96.2 1.5 collective-permute-start.10
  97.7 1.9 %slice.47 = bf16[2,128,1024]{2,1,0:T(8,128)(2,1)} slice(bf16[2,512,1024]{2,1,0:T(8,128)(2,1)} %refs_4_.1), slice={[0:2], [384:512], [0:1024]} | slice | bytes 1048576 | tf_op jit(solution)/shard_map/slice | solution.py:419
  99.6 20.2 %collective-permute-done.10.refs_3_ = bf16[2048,256]{1,0:T(8,128)(2,1)S(1)} collective-permute-done((bf16[2048,256]{1,0:T(8,128)(2,1)S(1)}, bf16[2048,256]{1,0:T(8,128)(2,1)S(1)}, u32[]{:S(2)}, u32[]{:S(2)}) %collective-permute-start.10) | collective-permute-done | bytes 1048608 | tf_op jit(solution)/shard_map/ppermute | solution.py:29
  119.8 3.4 %collective-permute-start.16 = (bf16[2,128,1024]{2,1,0:T(8,128)(2,1)}, bf16[2,128,1024]{2,1,0:T(8,128)(2,1)S(1)}, u32[]{:S(2)}, u32[]{:S(2)}) collective-permute-start(bf16[2,128,1024]{2,1,0:T(8,128)(2,1)} %slice.47), channel_id=1, source_target_pairs={{0,24},{1,25},{2,26},{3,27},{4,28},{5,29},{6,30},{7,31},{24,0},{25... | collective-permute-start | bytes 1572872 | tf_op jit(solution)/shard_map/ppermute | solution.py:29
  123.2 1.6 copy-done.1
  126.1 4.0 %project.3 = (bf16[2,256,512]{2,1,0:T(8,128)(2,1)}, bf16[2,256,512]{2,1,0:T(8,128)(2,1)S(1)}) custom-call(s32[7]{0:T(128)S(1)} %stack.74.pos, bf16[2048,256]{1,0:T(8,128)(2,1)S(1)} %bitcast.24, bf16[2048,256]{1,0:T(8,128)(2,1)S(1)} %copy-done.5, bf16[2048,256]{1,0:T(8,128)(2,1)S(1)} %bitcast.28, bf16[2048,256]{1,0:T(8,128)(2,1)S(1)} %collective-permute-done.10.refs_3_, ...), custom_call_target="tpu_custom_call" | custom-call | flops 2147483648 | bytes 6291456 | tf_op jit(solution)/shard_map/project/pallas_call | solution.py:259
  132.0 4.5 %project.4 = (bf16[2,256,384]{2,1,0:T(8,128)(2,1)S(1)}, bf16[2,256,384]{2,1,0:T(8,128)(2,1)S(1)}) custom-call(s32[7]{0:T(128)S(1)} %stack.74.pos, bf16[2048,256]{1,0:T(8,128)(2,1)S(1)} %bitcast.25, bf16[2048,256]{1,0:T(8,128)(2,1)S(1)} %copy-done.6, bf16[2048,256]{1,0:T(8,128)(2,1)S(1)} %bitcast.29, bf16[2048,256]{1,0:T(8,128)(2,1)S(1)} %collective-permute-done.10.refs_3_, ...), custom_call_target="tpu_custom_call" | custom-call | flops 1610612736 | bytes 6291456 | tf_op jit(solution)/shard_map/project/pallas_call | solution.py:259
  136.7 2.9 %collective-permute-start.12 = (bf16[256,256]{1,0:T(8,128)(2,1)}, bf16[256,256]{1,0:T(8,128)(2,1)}, u32[]{:S(2)}, u32[]{:S(2)}) collective-permute-start(bf16[256,256]{1,0:T(8,128)(2,1)} %bitcast.10), channel_id=1, source_target_pairs={{0,8},{1,9},{2,10},{3,11},{4,12},{5,13},{6,14},{7,15},{8,0},{9,1},... | collective-permute-start | bytes 393224 | tf_op jit(solution)/shard_map/ppermute | solution.py:29
  139.6 2.2 %collective-permute-done.16.refs_5_ = bf16[2,128,1024]{2,1,0:T(8,128)(2,1)S(1)} collective-permute-done((bf16[2,128,1024]{2,1,0:T(8,128)(2,1)}, bf16[2,128,1024]{2,1,0:T(8,128)(2,1)S(1)}, u32[]{:S(2)}, u32[]{:S(2)}) %collective-permute-start.16) | collective-permute-done | bytes 524320 | tf_op jit(solution)/shard_map/ppermute | solution.py:29
  141.8 1.5 collective-permute-start.11
  143.3 2.6 %project.5 = (bf16[2,256,128]{2,1,0:T(8,128)(2,1)}, bf16[2,256,128]{2,1,0:T(8,128)(2,1)S(1)}) custom-call(s32[7]{0:T(128)S(1)} %stack.74.pos, bf16[2048,256]{1,0:T(8,128)(2,1)S(1)} %bitcast.26, bf16[2048,256]{1,0:T(8,128)(2,1)S(1)} %copy-done.6, bf16[2048,256]{1,0:T(8,128)(2,1)S(1)} %bitcast.30, bf16[2048,256]{1,0:T(8,128)(2,1)S(1)} %collective-permute-done.10.refs_3_, ...), custom_call_target="tpu_custom_call" | custom-call | flops 536870912 | bytes 6291456 | tf_op jit(solution)/shard_map/project/pallas_call | solution.py:259
  149.5 2.7 %merge.1 = (bf16[256,512]{1,0:T(8,128)(2,1)}, bf16[256,512]{1,0:T(8,128)(2,1)}, bf16[256,512]{1,0:T(8,128)(2,1)}, bf16[256,512]{1,0:T(8,128)(2,1)}) custom-call(s32[1]{0:T(128)} %bitcast.13.flip, bf16[2,256,512]{2,1,0:T(8,128)(2,1)} %copy-done.8, bf16[2,256,512]{2,1,0:T(8,128)(2,1)} %collective-permute-done.14.refs_1_, bf16[2,256,384]{2,1,0:T(8,128)(2,1)} %copy-done.9, ...), custom_call_target="tpu_custom_call" | custom-call | tf_op jit(solution)/shard_map/merge/pallas_call | solution.py:304
  152.2 1.6 collective-permute-start.19
  153.8 1.8 %collective-permute-start.20 = (bf16[256,512]{1,0:T(8,128)(2,1)}, bf16[256,512]{1,0:T(8,128)(2,1)S(1)}, u32[]{:S(2)}, u32[]{:S(2)}) collective-permute-start(bf16[256,512]{1,0:T(8,128)(2,1)} %get-tuple-element.69), channel_id=1, source_target_pairs={{0,3},{1,11},{2,0},{3,8},{4,7},{5,15},{6,4},{7,12},{8,2},{9,10},{1... | collective-permute-start | bytes 786440 | tf_op jit(solution)/shard_map/ppermute | solution.py:29
  157.1 2.0 %place_columns.1 = bf16[256,1024]{1,0:T(8,128)(2,1)} custom-call(s32[1]{0:T(128)} %bitcast.pos, bf16[256,256]{1,0:T(8,128)(2,1)} %bitcast.31, bf16[256,256]{1,0:T(8,128)(2,1)} %collective-permute-done.11.refs_1_, bf16[256,256]{1,0:T(8,128)(2,1)} %collective-permute-done.12.refs_2_, bf16[256,256]{1,0:T(8,128)(2,1)} %copy-done.19), custom_call_target="tpu_custom_call" | custom-call | tf_op jit(solution)/shard_map/place_columns/pallas_call | solution.py:344
  160.4 1.7 collective-permute-done.21.refs_2_
  162.1 9.7 %collective-permute-done.22.refs_3_ = bf16[256,512]{1,0:T(8,128)(2,1)S(1)} collective-permute-done((bf16[256,512]{1,0:T(8,128)(2,1)}, bf16[256,512]{1,0:T(8,128)(2,1)S(1)}, u32[]{:S(2)}, u32[]{:S(2)}) %collective-permute-start.22) | collective-permute-done | bytes 262176 | tf_op jit(solution)/shard_map/ppermute | solution.py:29
  172.5 2.1 %collect.1 = bf16[256,1024]{1,0:T(8,128)(2,1)} custom-call(s32[1]{0:T(128)} %bitcast.12.pos, bf16[256,512]{1,0:T(8,128)(2,1)} %copy-done.14, bf16[256,512]{1,0:T(8,128)(2,1)} %copy-done.15, bf16[256,512]{1,0:T(8,128)(2,1)} %copy-done.16, bf16[256,512]{1,0:T(8,128)(2,1)} %copy-done.17), custom_call_target="tpu_custom_call" | custom-call | tf_op jit(solution)/shard_map/collect/pallas_call | solution.py:324
  (79 shorter events, 21.3 us)
Async XLA Ops:
  0.6 8.0 %copy-start = (bf16[2,512,1024]{2,1,0:T(8,128)(2,1)S(1)}, bf16[2,512,1024]{2,1,0:T(8,128)(2,1)}, u32[]{:S(2)}) copy-start(bf16[2,512,1024]{2,1,0:T(8,128)(2,1)} %refs_4_.1) | copy-start | bytes 6291460
  4.0 29.3 %copy-start.7 = (bf16[1040,256]{1,0:T(8,128)(2,1)S(1)}, bf16[1040,256]{1,0:T(8,128)(2,1)}, u32[]{:S(2)}) copy-start(bf16[1040,256]{1,0:T(8,128)(2,1)} %get-tuple-element.37.refs_0_) | copy-start | bytes 1597444
  4.0 17.2 %collective-permute-start.2 = (bf16[1040,256]{1,0:T(8,128)(2,1)}, bf16[1040,256]{1,0:T(8,128)(2,1)}, u32[]{:S(2)}, u32[]{:S(2)}) collective-permute-start(bf16[1040,256]{1,0:T(8,128)(2,1)} %get-tuple-element.40), channel_id=1, source_target_pairs={{0,12},{1,13},{2,14},{3,15},{4,8},{5,9},{6,10},{7,11},{8,4},{9,5},... | collective-permute-start | bytes 1597448 | tf_op jit(solution)/shard_map/ppermute | solution.py:29
  7.9 24.0 %collective-permute-start.1 = (bf16[1040,256]{1,0:T(8,128)(2,1)}, bf16[1040,256]{1,0:T(8,128)(2,1)}, u32[]{:S(2)}, u32[]{:S(2)}) collective-permute-start(bf16[1040,256]{1,0:T(8,128)(2,1)} %get-tuple-element.39), channel_id=1, source_target_pairs={{0,8},{1,9},{2,10},{3,11},{4,12},{5,13},{6,14},{7,15},{8,0},{9,1},... | collective-permute-start | bytes 1597448 | tf_op jit(solution)/shard_map/ppermute | solution.py:29
  8.4 24.3 %collective-permute-start = (bf16[1040,256]{1,0:T(8,128)(2,1)}, bf16[1040,256]{1,0:T(8,128)(2,1)}, u32[]{:S(2)}, u32[]{:S(2)}) collective-permute-start(bf16[1040,256]{1,0:T(8,128)(2,1)} %get-tuple-element.38), channel_id=1, source_target_pairs={{0,4},{1,5},{2,6},{3,7},{4,0},{5,1},{6,2},{7,3},{8,12},{9,13},{10,... | collective-permute-start | bytes 1597448 | tf_op jit(solution)/shard_map/ppermute | solution.py:29
  9.6 24.9 %collective-permute-start.3 = (bf16[2,224,1024]{2,1,0:T(8,128)(2,1)}, bf16[2,224,1024]{2,1,0:T(8,128)(2,1)}, u32[]{:S(2)}, u32[]{:S(2)}) collective-permute-start(bf16[2,224,1024]{2,1,0:T(8,128)(2,1)} %slice.44), channel_id=1, source_target_pairs={{8,16},{9,17},{10,18},{11,19},{12,20},{13,21},{14,22},{15,23},{16,... | collective-permute-start | bytes 2752520 | tf_op jit(solution)/shard_map/ppermute | solution.py:29
  34.5 14.0 %collective-permute-start.4 = (bf16[512,256]{1,0:T(8,128)(2,1)S(1)}, bf16[512,256]{1,0:T(8,128)(2,1)S(1)}, u32[]{:S(2)}, u32[]{:S(2)}) collective-permute-start(bf16[512,256]{1,0:T(8,128)(2,1)S(1)} %fusion.1), channel_id=1, source_target_pairs={{0,16},{1,17},{2,18},{3,19},{4,20},{5,21},{6,22},{7,23},{8,24},{9,... | collective-permute-start | bytes 786440 | tf_op jit(solution)/shard_map/ppermute | solution.py:29
  52.9 13.7 %collective-permute-start.6 = (bf16[2,2,128,256]{3,2,1,0:T(8,128)(2,1)S(1)}, bf16[2,2,128,256]{3,2,1,0:T(8,128)(2,1)S(1)}, u32[]{:S(2)}, u32[]{:S(2)}) collective-permute-start(bf16[2,2,128,256]{3,2,1,0:T(8,128)(2,1)S(1)} %get-tuple-element.51), channel_id=1, source_target_pairs={{0,16},{1,17},{2,18},{3,19},{4,20},{5,21},{6,22},{7,23},{8,24},{9,... | collective-permute-start | bytes 786440 | tf_op jit(solution)/shard_map/ppermute | solution.py:29
  60.4 9.5 %copy-start.12 = (bf16[2,128,256]{2,1,0:T(8,128)(2,1)}, bf16[2,128,256]{2,1,0:T(8,128)(2,1)S(1)}, u32[]{:S(2)}) copy-start(bf16[2,128,256]{2,1,0:T(8,128)(2,1)S(1)} %get-tuple-element.57) | copy-start | bytes 393220
  60.4 29.2 %collective-permute-start.9 = (bf16[2,288,1024]{2,1,0:T(8,128)(2,1)S(1)}, bf16[2,288,1024]{2,1,0:T(8,128)(2,1)S(1)}, u32[]{:S(2)}, u32[]{:S(2)}) collective-permute-start(bf16[2,288,1024]{2,1,0:T(8,128)(2,1)S(1)} %slice.45), channel_id=1, source_target_pairs={{8,16},{9,17},{10,18},{11,19},{12,20},{13,21},{14,22},{15,23},{16,... | collective-permute-start | bytes 3538952 | tf_op jit(solution)/shard_map/ppermute | solution.py:29
  61.1 28.4 %collective-permute-start.5 = (bf16[2,6,128,256]{3,2,1,0:T(8,128)(2,1)S(1)}, bf16[2,6,128,256]{3,2,1,0:T(8,128)(2,1)S(1)}, u32[]{:S(2)}, u32[]{:S(2)}) collective-permute-start(bf16[2,6,128,256]{3,2,1,0:T(8,128)(2,1)S(1)} %get-tuple-element.49), channel_id=1, source_target_pairs={{0,8},{1,9},{2,10},{3,11},{4,12},{5,13},{6,14},{7,15},{8,0},{9,1},... | collective-permute-start | bytes 2359304 | tf_op jit(solution)/shard_map/ppermute | solution.py:29
  66.7 28.5 %collective-permute-start.8 = (bf16[2048,256]{1,0:T(8,128)(2,1)S(1)}, bf16[2048,256]{1,0:T(8,128)(2,1)S(1)}, u32[]{:S(2)}, u32[]{:S(2)}) collective-permute-start(bf16[2048,256]{1,0:T(8,128)(2,1)S(1)} %bitcast.23), channel_id=1, source_target_pairs={{0,4},{1,5},{2,6},{3,7},{4,0},{5,1},{6,2},{7,3},{8,12},{9,13},{10,... | collective-permute-start | bytes 3145736 | tf_op jit(solution)/shard_map/ppermute | solution.py:29
  68.6 20.9 %collective-permute-start.7 = (bf16[2,2,128,256]{3,2,1,0:T(8,128)(2,1)S(1)}, bf16[2,2,128,256]{3,2,1,0:T(8,128)(2,1)S(1)}, u32[]{:S(2)}, u32[]{:S(2)}) collective-permute-start(bf16[2,2,128,256]{3,2,1,0:T(8,128)(2,1)S(1)} %add_convert_fusion), channel_id=1, source_target_pairs={{0,8},{1,9},{2,10},{3,11},{4,12},{5,13},{6,14},{7,15},{8,0},{9,1},... | collective-permute-start | bytes 786440 | tf_op jit(solution)/shard_map/ppermute | solution.py:29
  90.6 41.3 %collective-permute-start.15 = (bf16[2,384,1024]{2,1,0:T(8,128)(2,1)}, bf16[2,384,1024]{2,1,0:T(8,128)(2,1)}, u32[]{:S(2)}, u32[]{:S(2)}) collective-permute-start(bf16[2,384,1024]{2,1,0:T(8,128)(2,1)} %slice.46), channel_id=1, source_target_pairs={{0,24},{1,25},{2,26},{3,27},{4,28},{5,29},{6,30},{7,31},{24,0},{25... | collective-permute-start | bytes 4718600 | tf_op jit(solution)/shard_map/ppermute | solution.py:29
  96.2 23.6 %collective-permute-start.10 = (bf16[2048,256]{1,0:T(8,128)(2,1)S(1)}, bf16[2048,256]{1,0:T(8,128)(2,1)S(1)}, u32[]{:S(2)}, u32[]{:S(2)}) collective-permute-start(bf16[2048,256]{1,0:T(8,128)(2,1)S(1)} %bitcast.27), channel_id=1, source_target_pairs={{0,4},{1,5},{2,6},{3,7},{4,0},{5,1},{6,2},{7,3},{8,12},{9,13},{10,... | collective-permute-start | bytes 3145736 | tf_op jit(solution)/shard_map/ppermute | solution.py:29
  119.8 22.0 %collective-permute-start.16 = (bf16[2,128,1024]{2,1,0:T(8,128)(2,1)}, bf16[2,128,1024]{2,1,0:T(8,128)(2,1)S(1)}, u32[]{:S(2)}, u32[]{:S(2)}) collective-permute-start(bf16[2,128,1024]{2,1,0:T(8,128)(2,1)} %slice.47), channel_id=1, source_target_pairs={{0,24},{1,25},{2,26},{3,27},{4,28},{5,29},{6,30},{7,31},{24,0},{25... | collective-permute-start | bytes 1572872 | tf_op jit(solution)/shard_map/ppermute | solution.py:29
  126.0 5.9 %copy-start.3 = (bf16[2,288,1024]{2,1,0:T(8,128)(2,1)S(1)}, bf16[2,288,1024]{2,1,0:T(8,128)(2,1)}, u32[]{:S(2)}) copy-start(bf16[2,288,1024]{2,1,0:T(8,128)(2,1)} %copy-done.2) | copy-start | bytes 3538948
  126.1 5.9 %copy-start.6 = (bf16[2048,256]{1,0:T(8,128)(2,1)S(1)}, bf16[2048,256]{1,0:T(8,128)(2,1)}, u32[]{:S(2)}) copy-start(bf16[2048,256]{1,0:T(8,128)(2,1)} %copy-done.4) | copy-start | bytes 3145732
  130.9 16.7 %collective-permute-start.14 = (bf16[2,256,512]{2,1,0:T(8,128)(2,1)}, bf16[2,256,512]{2,1,0:T(8,128)(2,1)}, u32[]{:S(2)}, u32[]{:S(2)}) collective-permute-start(bf16[2,256,512]{2,1,0:T(8,128)(2,1)} %get-tuple-element.60), channel_id=1, source_target_pairs={{0,1},{1,0},{2,3},{3,2},{4,5},{5,4},{6,7},{7,6},{8,9},{9,8},{10,11... | collective-permute-start | bytes 1572872 | tf_op jit(solution)/shard_map/ppermute | solution.py:29
  136.5 9.4 %copy-start.9 = (bf16[2,256,384]{2,1,0:T(8,128)(2,1)}, bf16[2,256,384]{2,1,0:T(8,128)(2,1)S(1)}, u32[]{:S(2)}) copy-start(bf16[2,256,384]{2,1,0:T(8,128)(2,1)S(1)} %get-tuple-element.62.refs_2_) | copy-start | bytes 1179652
  136.5 12.3 %collective-permute-start.17 = (bf16[2,256,384]{2,1,0:T(8,128)(2,1)S(1)}, bf16[2,256,384]{2,1,0:T(8,128)(2,1)}, u32[]{:S(2)}, u32[]{:S(2)}) collective-permute-start(bf16[2,256,384]{2,1,0:T(8,128)(2,1)S(1)} %get-tuple-element.66), channel_id=1, source_target_pairs={{0,1},{1,0},{2,3},{3,2},{4,5},{5,4},{6,7},{7,6},{8,9},{9,8},{10,11... | collective-permute-start | bytes 1179656 | tf_op jit(solution)/shard_map/ppermute | solution.py:29
  136.6 10.0 %collective-permute-start.13 = (bf16[256,256]{1,0:T(8,128)(2,1)S(1)}, bf16[256,256]{1,0:T(8,128)(2,1)S(1)}, u32[]{:S(2)}, u32[]{:S(2)}) collective-permute-start(bf16[256,256]{1,0:T(8,128)(2,1)S(1)} %bitcast.32), channel_id=1, source_target_pairs={{0,12},{1,13},{2,14},{3,15},{4,8},{5,9},{6,10},{7,11},{8,4},{9,5},... | collective-permute-start | bytes 393224 | tf_op jit(solution)/shard_map/ppermute | solution.py:29
  136.7 10.6 %collective-permute-start.12 = (bf16[256,256]{1,0:T(8,128)(2,1)}, bf16[256,256]{1,0:T(8,128)(2,1)}, u32[]{:S(2)}, u32[]{:S(2)}) collective-permute-start(bf16[256,256]{1,0:T(8,128)(2,1)} %bitcast.10), channel_id=1, source_target_pairs={{0,8},{1,9},{2,10},{3,11},{4,12},{5,13},{6,14},{7,15},{8,0},{9,1},... | collective-permute-start | bytes 393224 | tf_op jit(solution)/shard_map/ppermute | solution.py:29
  141.8 5.8 %collective-permute-start.11 = (bf16[256,256]{1,0:T(8,128)(2,1)}, bf16[256,256]{1,0:T(8,128)(2,1)}, u32[]{:S(2)}, u32[]{:S(2)}) collective-permute-start(bf16[256,256]{1,0:T(8,128)(2,1)} %bitcast.7), channel_id=1, source_target_pairs={{0,4},{1,5},{2,6},{3,7},{4,0},{5,1},{6,2},{7,3},{8,12},{9,13},{10,... | collective-permute-start | bytes 393224 | tf_op jit(solution)/shard_map/ppermute | solution.py:29
  147.3 1.6 collective-permute-start.18
  152.2 6.9 %collective-permute-start.19 = (bf16[256,512]{1,0:T(8,128)(2,1)}, bf16[256,512]{1,0:T(8,128)(2,1)S(1)}, u32[]{:S(2)}, u32[]{:S(2)}) collective-permute-start(bf16[256,512]{1,0:T(8,128)(2,1)} %get-tuple-element.68), channel_id=1, source_target_pairs={{0,0},{1,8},{2,3},{3,11},{4,4},{5,12},{6,7},{7,15},{8,1},{9,9},{10... | collective-permute-start | bytes 786440 | tf_op jit(solution)/shard_map/ppermute | solution.py:29
  153.8 6.6 %collective-permute-start.20 = (bf16[256,512]{1,0:T(8,128)(2,1)}, bf16[256,512]{1,0:T(8,128)(2,1)S(1)}, u32[]{:S(2)}, u32[]{:S(2)}) collective-permute-start(bf16[256,512]{1,0:T(8,128)(2,1)} %get-tuple-element.69), channel_id=1, source_target_pairs={{0,3},{1,11},{2,0},{3,8},{4,7},{5,15},{6,4},{7,12},{8,2},{9,10},{1... | collective-permute-start | bytes 786440 | tf_op jit(solution)/shard_map/ppermute | solution.py:29
  155.5 6.6 %collective-permute-start.21 = (bf16[256,512]{1,0:T(8,128)(2,1)}, bf16[256,512]{1,0:T(8,128)(2,1)S(1)}, u32[]{:S(2)}, u32[]{:S(2)}) collective-permute-start(bf16[256,512]{1,0:T(8,128)(2,1)} %get-tuple-element.70), channel_id=1, source_target_pairs={{0,4},{1,12},{2,7},{3,15},{4,0},{5,8},{6,3},{7,11},{8,5},{9,13},{1... | collective-permute-start | bytes 786440 | tf_op jit(solution)/shard_map/ppermute | solution.py:29
  156.0 15.8 %collective-permute-start.22 = (bf16[256,512]{1,0:T(8,128)(2,1)}, bf16[256,512]{1,0:T(8,128)(2,1)S(1)}, u32[]{:S(2)}, u32[]{:S(2)}) collective-permute-start(bf16[256,512]{1,0:T(8,128)(2,1)} %get-tuple-element.71), channel_id=1, source_target_pairs={{0,7},{1,15},{2,4},{3,12},{4,3},{5,11},{6,0},{7,8},{8,6},{9,14},{1... | collective-permute-start | bytes 786440 | tf_op jit(solution)/shard_map/ppermute | solution.py:29
  159.0 12.8 %copy-start.14 = (bf16[256,512]{1,0:T(8,128)(2,1)}, bf16[256,512]{1,0:T(8,128)(2,1)S(1)}, u32[]{:S(2)}) copy-start(bf16[256,512]{1,0:T(8,128)(2,1)S(1)} %collective-permute-done.19.refs_0_) | copy-start | bytes 786436
  160.4 11.4 %copy-start.15 = (bf16[256,512]{1,0:T(8,128)(2,1)}, bf16[256,512]{1,0:T(8,128)(2,1)S(1)}, u32[]{:S(2)}) copy-start(bf16[256,512]{1,0:T(8,128)(2,1)S(1)} %collective-permute-done.20.refs_1_) | copy-start | bytes 786436
  162.1 9.7 %copy-start.16 = (bf16[256,512]{1,0:T(8,128)(2,1)}, bf16[256,512]{1,0:T(8,128)(2,1)S(1)}, u32[]{:S(2)}) copy-start(bf16[256,512]{1,0:T(8,128)(2,1)S(1)} %collective-permute-done.21.refs_2_) | copy-start | bytes 786436
  (11 other events, 14.6 us)

commit v6 on v5

--- a/solution.py
+++ b/solution.py
@@ -94,7 +94,10 @@
         part = slice(own + n * per_dev, own + (n + 1) * per_dev)
         keys[part] = halo[:size].reshape(block)
         values[part] = halo[size:].reshape(block)
-    if not with_state:
+    if with_state:
+        acc[...] = state[0][...]
+        dq_all[...] = state[1][...]
+    else:
         acc[...] = jnp.zeros_like(acc)
         dq_all[...] = jnp.zeros_like(dq_all)
     lane_head = lax.broadcasted_iota(jnp.int32, (BLOCK, width), 1) // HEAD_DIM
@@ -192,7 +195,6 @@
         in_specs=[scalars] * 2 + [whole] * (GROUP + len(halos) + len(state)),
         out_specs=[whole] * len(shapes),
         scratch_shapes=scratch,
-        input_output_aliases={2 + GROUP + len(halos) + n: n for n in range(len(state))},
         compiler_params=pltpu.CompilerParams(vmem_limit_bytes=20 * 2**20),
         cost_estimate=pl.CostEstimate(
             flops=turns * 10 * SLOTS * BLOCK * heads * BLOCK * width,

time: 175 us -> 176 us (level)
  transfers between devices with their start and end apart: 23 -> 23, of which waited for: 13 -> 12; matrix products, arithmetic and copies ran while one was open for 5% -> 5% of each run, Pallas kernels for 15% -> 15%
where the time goes in v6:
time: 176 us; the launch traced here: 175 us
  waiting for transfers between devices  82.6 us (47%)
  Pallas kernels  39.5 us (22%)
  starting transfers between devices  35.5 us (20%)
  local copies, waits for them, and re-layouts  15.3 us (9%)
    ppermute x23, waiting for transfers between devices, send(): return lax.ppermute(block, AXES, pairs)  82.6 us
    ppermute x23, starting transfers between devices, send(): return lax.ppermute(block, AXES, pairs)  35.5 us
    pallas_call x3, Pallas kernels, attend(): pl.pallas_call(functools.partial(attend_kernel, span, n_halo, bool(halos)...  18.3 us
    pallas_call x3, Pallas kernels, project(): pl.pallas_call(functools.partial(project_kernel, [part for _, part in par...  11.1 us
    unnamed x40, local copies, waits for them, and re-layouts  8.29 us
    slice x4, local copies, waits for them, and re-layouts, rows_of(): return kv_weight[:, cuts[n] * unit:cuts[n + 1] * unit]  4.25 us
  transfers between devices with their start and end apart: 23, of which 12 were waited for; matrix products, arithmetic and copies ran while one was open for 5% of the time, Pallas kernels for 15%

profile of v6, /device:TPU:0, one launch (start us, length us, event | category | flops | bytes accessed | tf_op | source)
XLA Modules:
  0.0 175.2 jit_solution(1022132774968375886)
XLA Ops:
  0.6 3.3 %pack.1 = (bf16[1040,256]{1,0:T(8,128)(2,1)}, bf16[1040,256]{1,0:T(8,128)(2,1)}, bf16[1040,256]{1,0:T(8,128)(2,1)}, bf16[1040,256]{1,0:T(8,128)(2,1)}) custom-call(s32[2,4]{1,0:T(2,128)} %block_ids.1, s32[2]{0:T(128)} %block_count.1, bf16[256,1024]{1,0:T(8,128)(2,1)} %queries.1, bf16[256,1024]{1,0:T(8,128)(2,1)} %grad_out.1, bf16[2,256,1024]{2,1,0:T(8,128)(2,1)} %key_values.1), custom_call_target="tpu_custom_call" | custom-call | tf_op jit(solution)/shard_map/pack/pallas_call | solution.py:66
  3.9 4.0 %collective-permute-start.2 = (bf16[1040,256]{1,0:T(8,128)(2,1)}, bf16[1040,256]{1,0:T(8,128)(2,1)}, u32[]{:S(2)}, u32[]{:S(2)}) collective-permute-start(bf16[1040,256]{1,0:T(8,128)(2,1)} %get-tuple-element.40), channel_id=1, source_target_pairs={{0,12},{1,13},{2,14},{3,15},{4,8},{5,9},{6,10},{7,11},{8,4},{9,5},... | collective-permute-start | bytes 1597448 | tf_op jit(solution)/shard_map/ppermute | solution.py:29
  9.5 1.6 collective-permute-start.3
  11.9 9.3 %collective-permute-done.2.refs_3_ = bf16[1040,256]{1,0:T(8,128)(2,1)} collective-permute-done((bf16[1040,256]{1,0:T(8,128)(2,1)}, bf16[1040,256]{1,0:T(8,128)(2,1)}, u32[]{:S(2)}, u32[]{:S(2)}) %collective-permute-start.2) | collective-permute-done | bytes 532512 | tf_op jit(solution)/shard_map/ppermute | solution.py:29
  21.8 10.1 %collective-permute-done.1.refs_2_ = bf16[1040,256]{1,0:T(8,128)(2,1)} collective-permute-done((bf16[1040,256]{1,0:T(8,128)(2,1)}, bf16[1040,256]{1,0:T(8,128)(2,1)}, u32[]{:S(2)}, u32[]{:S(2)}) %collective-permute-start.1) | collective-permute-done | bytes 532512 | tf_op jit(solution)/shard_map/ppermute | solution.py:29
  34.4 2.7 %collective-permute-start.4 = (bf16[512,256]{1,0:T(8,128)(2,1)S(1)}, bf16[512,256]{1,0:T(8,128)(2,1)S(1)}, u32[]{:S(2)}, u32[]{:S(2)}) collective-permute-start(bf16[512,256]{1,0:T(8,128)(2,1)S(1)} %fusion.1), channel_id=1, source_target_pairs={{0,16},{1,17},{2,18},{3,19},{4,20},{5,21},{6,22},{7,23},{8,24},{9,... | collective-permute-start | bytes 786440 | tf_op jit(solution)/shard_map/ppermute | solution.py:29
  37.1 6.0 %attend.3 = (f32[2,10,128,256]{3,2,1,0:T(8,128)S(1)}, bf16[8,128,256]{2,1,0:T(8,128)(2,1)S(1)}) custom-call(s32[4,2,5]{2,1,0:T(2,128)S(1)} %maximum_convert_fusion.meta, s32[2]{0:T(128)S(1)} %pad_add_fusion.pos, bf16[1040,256]{1,0:T(8,128)(2,1)S(1)} %copy-done.7, bf16[1040,256]{1,0:T(8,128)(2,1)} %collective-permute-done.refs_1_, ...), custom_call_target="tpu_custom_call" | custom-call | flops 2013265920 | bytes 4194304 | tf_op jit(solution)/shard_map/attend/pallas_call | solution.py:192
  43.1 5.4 %collective-permute-done.4.refs_4_ = bf16[512,256]{1,0:T(8,128)(2,1)S(1)} collective-permute-done((bf16[512,256]{1,0:T(8,128)(2,1)S(1)}, bf16[512,256]{1,0:T(8,128)(2,1)S(1)}, u32[]{:S(2)}, u32[]{:S(2)}) %collective-permute-start.4) | collective-permute-done | bytes 262176 | tf_op jit(solution)/shard_map/ppermute | solution.py:29
  48.5 4.6 %attend.4 = (f32[2,10,128,256]{3,2,1,0:T(8,128)S(1)}, bf16[8,128,256]{2,1,0:T(8,128)(2,1)S(1)}, bf16[2,2,128,256]{3,2,1,0:T(8,128)(2,1)S(1)}) custom-call(s32[4,2,5]{2,1,0:T(2,128)S(1)} %maximum_convert_fusion.meta, s32[2]{0:T(128)S(1)} %pad_add_fusion.pos, bf16[1040,256]{1,0:T(8,128)(2,1)S(1)} %copy-done.7, bf16[1040,256]{1,0:T(8,128)(2,1)} %collective-permute-done.refs_1_, ...), custom_call_target="tpu_custom_call" | custom-call | flops 1342177280 | bytes 4194304 | tf_op jit(solution)/shard_map/attend/pallas_call | solution.py:192
  53.2 7.8 %attend.5 = (f32[2,10,128,256]{3,2,1,0:T(8,128)}, bf16[8,128,256]{2,1,0:T(8,128)(2,1)}, bf16[2,128,256]{2,1,0:T(8,128)(2,1)S(1)}, bf16[2,128,256]{2,1,0:T(8,128)...) custom-call(s32[4,2,5]{2,1,0:T(2,128)S(1)} %maximum_convert_fusion.m, ...), custom_call_target="tpu_custom_call" | custom-call | flops 2013265920 | bytes 4194304 | tf_op jit(solution)/shard_map/attend/pallas_call | solution.py:192
  61.7 5.3 %collective-permute-start.5 = (bf16[2,6,128,256]{3,2,1,0:T(8,128)(2,1)S(1)}, bf16[2,6,128,256]{3,2,1,0:T(8,128)(2,1)S(1)}, u32[]{:S(2)}, u32[]{:S(2)}) collective-permute-start(bf16[2,6,128,256]{3,2,1,0:T(8,128)(2,1)S(1)} %get-tuple-element.49), channel_id=1, source_target_pairs={{0,8},{1,9},{2,10},{3,11},{4,12},{5,13},{6,14},{7,15},{8,0},{9,1},... | collective-permute-start | bytes 2359304 | tf_op jit(solution)/shard_map/ppermute | solution.py:29
  67.2 1.6 collective-permute-start.8
  70.1 20.0 %collective-permute-done.7 = bf16[2,2,128,256]{3,2,1,0:T(8,128)(2,1)S(1)} collective-permute-done((bf16[2,2,128,256]{3,2,1,0:T(8,128)(2,1)S(1)}, bf16[2,2,128,256]{3,2,1,0:T(8,128)(2,1)S(1)}, u32[]{:S(2)}, u32[]{:S(2)}) %collective-permute-start.7) | collective-permute-done | bytes 262176 | tf_op jit(solution)/shard_map/ppermute | solution.py:29
  91.2 4.5 %collective-permute-start.15 = (bf16[2,384,1024]{2,1,0:T(8,128)(2,1)}, bf16[2,384,1024]{2,1,0:T(8,128)(2,1)}, u32[]{:S(2)}, u32[]{:S(2)}) collective-permute-start(bf16[2,384,1024]{2,1,0:T(8,128)(2,1)} %slice.46), channel_id=1, source_target_pairs={{0,24},{1,25},{2,26},{3,27},{4,28},{5,29},{6,30},{7,31},{24,0},{25... | collective-permute-start | bytes 4718600 | tf_op jit(solution)/shard_map/ppermute | solution.py:29
  96.8 1.5 collective-permute-start.10
  98.3 1.9 %slice.47 = bf16[2,128,1024]{2,1,0:T(8,128)(2,1)} slice(bf16[2,512,1024]{2,1,0:T(8,128)(2,1)} %refs_4_.1), slice={[0:2], [384:512], [0:1024]} | slice | bytes 1048576 | tf_op jit(solution)/shard_map/slice | solution.py:421
  100.2 20.2 %collective-permute-done.10.refs_3_ = bf16[2048,256]{1,0:T(8,128)(2,1)S(1)} collective-permute-done((bf16[2048,256]{1,0:T(8,128)(2,1)S(1)}, bf16[2048,256]{1,0:T(8,128)(2,1)S(1)}, u32[]{:S(2)}, u32[]{:S(2)}) %collective-permute-start.10) | collective-permute-done | bytes 1048608 | tf_op jit(solution)/shard_map/ppermute | solution.py:29
  120.4 3.4 %collective-permute-start.16 = (bf16[2,128,1024]{2,1,0:T(8,128)(2,1)}, bf16[2,128,1024]{2,1,0:T(8,128)(2,1)S(1)}, u32[]{:S(2)}, u32[]{:S(2)}) collective-permute-start(bf16[2,128,1024]{2,1,0:T(8,128)(2,1)} %slice.47), channel_id=1, source_target_pairs={{0,24},{1,25},{2,26},{3,27},{4,28},{5,29},{6,30},{7,31},{24,0},{25... | collective-permute-start | bytes 1572872 | tf_op jit(solution)/shard_map/ppermute | solution.py:29
  123.8 1.6 copy-done.1
  126.6 4.0 %project.3 = (bf16[2,256,512]{2,1,0:T(8,128)(2,1)}, bf16[2,256,512]{2,1,0:T(8,128)(2,1)S(1)}) custom-call(s32[7]{0:T(128)S(1)} %stack.74.pos, bf16[2048,256]{1,0:T(8,128)(2,1)S(1)} %bitcast.24, bf16[2048,256]{1,0:T(8,128)(2,1)S(1)} %copy-done.5, bf16[2048,256]{1,0:T(8,128)(2,1)S(1)} %bitcast.28, bf16[2048,256]{1,0:T(8,128)(2,1)S(1)} %collective-permute-done.10.refs_3_, ...), custom_call_target="tpu_custom_call" | custom-call | flops 2147483648 | bytes 6291456 | tf_op jit(solution)/shard_map/project/pallas_call | solution.py:261
  132.6 4.5 %project.4 = (bf16[2,256,384]{2,1,0:T(8,128)(2,1)S(1)}, bf16[2,256,384]{2,1,0:T(8,128)(2,1)S(1)}) custom-call(s32[7]{0:T(128)S(1)} %stack.74.pos, bf16[2048,256]{1,0:T(8,128)(2,1)S(1)} %bitcast.25, bf16[2048,256]{1,0:T(8,128)(2,1)S(1)} %copy-done.6, bf16[2048,256]{1,0:T(8,128)(2,1)S(1)} %bitcast.29, bf16[2048,256]{1,0:T(8,128)(2,1)S(1)} %collective-permute-done.10.refs_3_, ...), custom_call_target="tpu_custom_call" | custom-call | flops 1610612736 | bytes 6291456 | tf_op jit(solution)/shard_map/project/pallas_call | solution.py:261
  137.3 2.9 %collective-permute-start.12 = (bf16[256,256]{1,0:T(8,128)(2,1)}, bf16[256,256]{1,0:T(8,128)(2,1)}, u32[]{:S(2)}, u32[]{:S(2)}) collective-permute-start(bf16[256,256]{1,0:T(8,128)(2,1)} %bitcast.10), channel_id=1, source_target_pairs={{0,8},{1,9},{2,10},{3,11},{4,12},{5,13},{6,14},{7,15},{8,0},{9,1},... | collective-permute-start | bytes 393224 | tf_op jit(solution)/shard_map/ppermute | solution.py:29
  140.2 2.2 %collective-permute-done.16.refs_5_ = bf16[2,128,1024]{2,1,0:T(8,128)(2,1)S(1)} collective-permute-done((bf16[2,128,1024]{2,1,0:T(8,128)(2,1)}, bf16[2,128,1024]{2,1,0:T(8,128)(2,1)S(1)}, u32[]{:S(2)}, u32[]{:S(2)}) %collective-permute-start.16) | collective-permute-done | bytes 524320 | tf_op jit(solution)/shard_map/ppermute | solution.py:29
  142.4 1.5 collective-permute-start.11
  144.0 2.6 %project.5 = (bf16[2,256,128]{2,1,0:T(8,128)(2,1)}, bf16[2,256,128]{2,1,0:T(8,128)(2,1)S(1)}) custom-call(s32[7]{0:T(128)S(1)} %stack.74.pos, bf16[2048,256]{1,0:T(8,128)(2,1)S(1)} %bitcast.26, bf16[2048,256]{1,0:T(8,128)(2,1)S(1)} %copy-done.6, bf16[2048,256]{1,0:T(8,128)(2,1)S(1)} %bitcast.30, bf16[2048,256]{1,0:T(8,128)(2,1)S(1)} %collective-permute-done.10.refs_3_, ...), custom_call_target="tpu_custom_call" | custom-call | flops 536870912 | bytes 6291456 | tf_op jit(solution)/shard_map/project/pallas_call | solution.py:261
  150.1 2.7 %merge.1 = (bf16[256,512]{1,0:T(8,128)(2,1)}, bf16[256,512]{1,0:T(8,128)(2,1)}, bf16[256,512]{1,0:T(8,128)(2,1)}, bf16[256,512]{1,0:T(8,128)(2,1)}) custom-call(s32[1]{0:T(128)} %bitcast.13.flip, bf16[2,256,512]{2,1,0:T(8,128)(2,1)} %copy-done.8, bf16[2,256,512]{2,1,0:T(8,128)(2,1)} %collective-permute-done.14.refs_1_, bf16[2,256,384]{2,1,0:T(8,128)(2,1)} %copy-done.9, ...), custom_call_target="tpu_custom_call" | custom-call | tf_op jit(solution)/shard_map/merge/pallas_call | solution.py:306
  152.8 1.6 collective-permute-start.19
  154.4 1.7 collective-permute-start.20
  157.7 2.0 %place_columns.1 = bf16[256,1024]{1,0:T(8,128)(2,1)} custom-call(s32[1]{0:T(128)} %bitcast.pos, bf16[256,256]{1,0:T(8,128)(2,1)} %bitcast.31, bf16[256,256]{1,0:T(8,128)(2,1)} %collective-permute-done.11.refs_1_, bf16[256,256]{1,0:T(8,128)(2,1)} %collective-permute-done.12.refs_2_, bf16[256,256]{1,0:T(8,128)(2,1)} %copy-done.19), custom_call_target="tpu_custom_call" | custom-call | tf_op jit(solution)/shard_map/place_columns/pallas_call | solution.py:346
  161.0 1.7 collective-permute-done.21.refs_2_
  162.7 9.7 %collective-permute-done.22.refs_3_ = bf16[256,512]{1,0:T(8,128)(2,1)S(1)} collective-permute-done((bf16[256,512]{1,0:T(8,128)(2,1)}, bf16[256,512]{1,0:T(8,128)(2,1)S(1)}, u32[]{:S(2)}, u32[]{:S(2)}) %collective-permute-start.22) | collective-permute-done | bytes 262176 | tf_op jit(solution)/shard_map/ppermute | solution.py:29
  173.1 2.1 %collect.1 = bf16[256,1024]{1,0:T(8,128)(2,1)} custom-call(s32[1]{0:T(128)} %bitcast.12.pos, bf16[256,512]{1,0:T(8,128)(2,1)} %copy-done.14, bf16[256,512]{1,0:T(8,128)(2,1)} %copy-done.15, bf16[256,512]{1,0:T(8,128)(2,1)} %copy-done.16, bf16[256,512]{1,0:T(8,128)(2,1)} %copy-done.17), custom_call_target="tpu_custom_call" | custom-call | tf_op jit(solution)/shard_map/collect/pallas_call | solution.py:326
  (79 shorter events, 20.5 us)
Async XLA Ops:
  0.6 7.9 %copy-start = (bf16[2,512,1024]{2,1,0:T(8,128)(2,1)S(1)}, bf16[2,512,1024]{2,1,0:T(8,128)(2,1)}, u32[]{:S(2)}) copy-start(bf16[2,512,1024]{2,1,0:T(8,128)(2,1)} %refs_4_.1) | copy-start | bytes 6291460
  3.9 29.3 %copy-start.7 = (bf16[1040,256]{1,0:T(8,128)(2,1)S(1)}, bf16[1040,256]{1,0:T(8,128)(2,1)}, u32[]{:S(2)}) copy-start(bf16[1040,256]{1,0:T(8,128)(2,1)} %get-tuple-element.37.refs_0_) | copy-start | bytes 1597444
  3.9 17.2 %collective-permute-start.2 = (bf16[1040,256]{1,0:T(8,128)(2,1)}, bf16[1040,256]{1,0:T(8,128)(2,1)}, u32[]{:S(2)}, u32[]{:S(2)}) collective-permute-start(bf16[1040,256]{1,0:T(8,128)(2,1)} %get-tuple-element.40), channel_id=1, source_target_pairs={{0,12},{1,13},{2,14},{3,15},{4,8},{5,9},{6,10},{7,11},{8,4},{9,5},... | collective-permute-start | bytes 1597448 | tf_op jit(solution)/shard_map/ppermute | solution.py:29
  7.9 24.0 %collective-permute-start.1 = (bf16[1040,256]{1,0:T(8,128)(2,1)}, bf16[1040,256]{1,0:T(8,128)(2,1)}, u32[]{:S(2)}, u32[]{:S(2)}) collective-permute-start(bf16[1040,256]{1,0:T(8,128)(2,1)} %get-tuple-element.39), channel_id=1, source_target_pairs={{0,8},{1,9},{2,10},{3,11},{4,12},{5,13},{6,14},{7,15},{8,0},{9,1},... | collective-permute-start | bytes 1597448 | tf_op jit(solution)/shard_map/ppermute | solution.py:29
  8.3 24.3 %collective-permute-start = (bf16[1040,256]{1,0:T(8,128)(2,1)}, bf16[1040,256]{1,0:T(8,128)(2,1)}, u32[]{:S(2)}, u32[]{:S(2)}) collective-permute-start(bf16[1040,256]{1,0:T(8,128)(2,1)} %get-tuple-element.38), channel_id=1, source_target_pairs={{0,4},{1,5},{2,6},{3,7},{4,0},{5,1},{6,2},{7,3},{8,12},{9,13},{10,... | collective-permute-start | bytes 1597448 | tf_op jit(solution)/shard_map/ppermute | solution.py:29
  9.5 24.9 %collective-permute-start.3 = (bf16[2,224,1024]{2,1,0:T(8,128)(2,1)}, bf16[2,224,1024]{2,1,0:T(8,128)(2,1)}, u32[]{:S(2)}, u32[]{:S(2)}) collective-permute-start(bf16[2,224,1024]{2,1,0:T(8,128)(2,1)} %slice.44), channel_id=1, source_target_pairs={{8,16},{9,17},{10,18},{11,19},{12,20},{13,21},{14,22},{15,23},{16,... | collective-permute-start | bytes 2752520 | tf_op jit(solution)/shard_map/ppermute | solution.py:29
  34.4 14.0 %collective-permute-start.4 = (bf16[512,256]{1,0:T(8,128)(2,1)S(1)}, bf16[512,256]{1,0:T(8,128)(2,1)S(1)}, u32[]{:S(2)}, u32[]{:S(2)}) collective-permute-start(bf16[512,256]{1,0:T(8,128)(2,1)S(1)} %fusion.1), channel_id=1, source_target_pairs={{0,16},{1,17},{2,18},{3,19},{4,20},{5,21},{6,22},{7,23},{8,24},{9,... | collective-permute-start | bytes 786440 | tf_op jit(solution)/shard_map/ppermute | solution.py:29
  53.0 14.0 %collective-permute-start.6 = (bf16[2,2,128,256]{3,2,1,0:T(8,128)(2,1)S(1)}, bf16[2,2,128,256]{3,2,1,0:T(8,128)(2,1)S(1)}, u32[]{:S(2)}, u32[]{:S(2)}) collective-permute-start(bf16[2,2,128,256]{3,2,1,0:T(8,128)(2,1)S(1)} %get-tuple-element.51), channel_id=1, source_target_pairs={{0,16},{1,17},{2,18},{3,19},{4,20},{5,21},{6,22},{7,23},{8,24},{9,... | collective-permute-start | bytes 786440 | tf_op jit(solution)/shard_map/ppermute | solution.py:29
  61.0 9.1 %copy-start.11 = (bf16[2,128,256]{2,1,0:T(8,128)(2,1)}, bf16[2,128,256]{2,1,0:T(8,128)(2,1)S(1)}, u32[]{:S(2)}) copy-start(bf16[2,128,256]{2,1,0:T(8,128)(2,1)S(1)} %get-tuple-element.47) | copy-start | bytes 393220
  61.0 9.1 %copy-start.12 = (bf16[2,128,256]{2,1,0:T(8,128)(2,1)}, bf16[2,128,256]{2,1,0:T(8,128)(2,1)S(1)}, u32[]{:S(2)}) copy-start(bf16[2,128,256]{2,1,0:T(8,128)(2,1)S(1)} %get-tuple-element.57) | copy-start | bytes 393220
  61.0 29.2 %collective-permute-start.9 = (bf16[2,288,1024]{2,1,0:T(8,128)(2,1)S(1)}, bf16[2,288,1024]{2,1,0:T(8,128)(2,1)S(1)}, u32[]{:S(2)}, u32[]{:S(2)}) collective-permute-start(bf16[2,288,1024]{2,1,0:T(8,128)(2,1)S(1)} %slice.45), channel_id=1, source_target_pairs={{8,16},{9,17},{10,18},{11,19},{12,20},{13,21},{14,22},{15,23},{16,... | collective-permute-start | bytes 3538952 | tf_op jit(solution)/shard_map/ppermute | solution.py:29
  61.7 28.4 %collective-permute-start.5 = (bf16[2,6,128,256]{3,2,1,0:T(8,128)(2,1)S(1)}, bf16[2,6,128,256]{3,2,1,0:T(8,128)(2,1)S(1)}, u32[]{:S(2)}, u32[]{:S(2)}) collective-permute-start(bf16[2,6,128,256]{3,2,1,0:T(8,128)(2,1)S(1)} %get-tuple-element.49), channel_id=1, source_target_pairs={{0,8},{1,9},{2,10},{3,11},{4,12},{5,13},{6,14},{7,15},{8,0},{9,1},... | collective-permute-start | bytes 2359304 | tf_op jit(solution)/shard_map/ppermute | solution.py:29
  67.2 28.6 %collective-permute-start.8 = (bf16[2048,256]{1,0:T(8,128)(2,1)S(1)}, bf16[2048,256]{1,0:T(8,128)(2,1)S(1)}, u32[]{:S(2)}, u32[]{:S(2)}) collective-permute-start(bf16[2048,256]{1,0:T(8,128)(2,1)S(1)} %bitcast.23), channel_id=1, source_target_pairs={{0,4},{1,5},{2,6},{3,7},{4,0},{5,1},{6,2},{7,3},{8,12},{9,13},{10,... | collective-permute-start | bytes 3145736 | tf_op jit(solution)/shard_map/ppermute | solution.py:29
  68.8 21.3 %collective-permute-start.7 = (bf16[2,2,128,256]{3,2,1,0:T(8,128)(2,1)S(1)}, bf16[2,2,128,256]{3,2,1,0:T(8,128)(2,1)S(1)}, u32[]{:S(2)}, u32[]{:S(2)}) collective-permute-start(bf16[2,2,128,256]{3,2,1,0:T(8,128)(2,1)S(1)} %add_convert_fusion), channel_id=1, source_target_pairs={{0,8},{1,9},{2,10},{3,11},{4,12},{5,13},{6,14},{7,15},{8,0},{9,1},... | collective-permute-start | bytes 786440 | tf_op jit(solution)/shard_map/ppermute | solution.py:29
  91.2 41.3 %collective-permute-start.15 = (bf16[2,384,1024]{2,1,0:T(8,128)(2,1)}, bf16[2,384,1024]{2,1,0:T(8,128)(2,1)}, u32[]{:S(2)}, u32[]{:S(2)}) collective-permute-start(bf16[2,384,1024]{2,1,0:T(8,128)(2,1)} %slice.46), channel_id=1, source_target_pairs={{0,24},{1,25},{2,26},{3,27},{4,28},{5,29},{6,30},{7,31},{24,0},{25... | collective-permute-start | bytes 4718600 | tf_op jit(solution)/shard_map/ppermute | solution.py:29
  96.8 23.6 %collective-permute-start.10 = (bf16[2048,256]{1,0:T(8,128)(2,1)S(1)}, bf16[2048,256]{1,0:T(8,128)(2,1)S(1)}, u32[]{:S(2)}, u32[]{:S(2)}) collective-permute-start(bf16[2048,256]{1,0:T(8,128)(2,1)S(1)} %bitcast.27), channel_id=1, source_target_pairs={{0,4},{1,5},{2,6},{3,7},{4,0},{5,1},{6,2},{7,3},{8,12},{9,13},{10,... | collective-permute-start | bytes 3145736 | tf_op jit(solution)/shard_map/ppermute | solution.py:29
  120.4 22.0 %collective-permute-start.16 = (bf16[2,128,1024]{2,1,0:T(8,128)(2,1)}, bf16[2,128,1024]{2,1,0:T(8,128)(2,1)S(1)}, u32[]{:S(2)}, u32[]{:S(2)}) collective-permute-start(bf16[2,128,1024]{2,1,0:T(8,128)(2,1)} %slice.47), channel_id=1, source_target_pairs={{0,24},{1,25},{2,26},{3,27},{4,28},{5,29},{6,30},{7,31},{24,0},{25... | collective-permute-start | bytes 1572872 | tf_op jit(solution)/shard_map/ppermute | solution.py:29
  126.6 5.9 %copy-start.6 = (bf16[2048,256]{1,0:T(8,128)(2,1)S(1)}, bf16[2048,256]{1,0:T(8,128)(2,1)}, u32[]{:S(2)}) copy-start(bf16[2048,256]{1,0:T(8,128)(2,1)} %copy-done.4) | copy-start | bytes 3145732
  131.5 16.8 %collective-permute-start.14 = (bf16[2,256,512]{2,1,0:T(8,128)(2,1)}, bf16[2,256,512]{2,1,0:T(8,128)(2,1)}, u32[]{:S(2)}, u32[]{:S(2)}) collective-permute-start(bf16[2,256,512]{2,1,0:T(8,128)(2,1)} %get-tuple-element.60), channel_id=1, source_target_pairs={{0,1},{1,0},{2,3},{3,2},{4,5},{5,4},{6,7},{7,6},{8,9},{9,8},{10,11... | collective-permute-start | bytes 1572872 | tf_op jit(solution)/shard_map/ppermute | solution.py:29
  137.1 9.5 %copy-start.9 = (bf16[2,256,384]{2,1,0:T(8,128)(2,1)}, bf16[2,256,384]{2,1,0:T(8,128)(2,1)S(1)}, u32[]{:S(2)}) copy-start(bf16[2,256,384]{2,1,0:T(8,128)(2,1)S(1)} %get-tuple-element.62.refs_2_) | copy-start | bytes 1179652
  137.1 12.3 %collective-permute-start.17 = (bf16[2,256,384]{2,1,0:T(8,128)(2,1)S(1)}, bf16[2,256,384]{2,1,0:T(8,128)(2,1)}, u32[]{:S(2)}, u32[]{:S(2)}) collective-permute-start(bf16[2,256,384]{2,1,0:T(8,128)(2,1)S(1)} %get-tuple-element.66), channel_id=1, source_target_pairs={{0,1},{1,0},{2,3},{3,2},{4,5},{5,4},{6,7},{7,6},{8,9},{9,8},{10,11... | collective-permute-start | bytes 1179656 | tf_op jit(solution)/shard_map/ppermute | solution.py:29
  137.2 10.0 %collective-permute-start.13 = (bf16[256,256]{1,0:T(8,128)(2,1)S(1)}, bf16[256,256]{1,0:T(8,128)(2,1)S(1)}, u32[]{:S(2)}, u32[]{:S(2)}) collective-permute-start(bf16[256,256]{1,0:T(8,128)(2,1)S(1)} %bitcast.32), channel_id=1, source_target_pairs={{0,12},{1,13},{2,14},{3,15},{4,8},{5,9},{6,10},{7,11},{8,4},{9,5},... | collective-permute-start | bytes 393224 | tf_op jit(solution)/shard_map/ppermute | solution.py:29
  137.3 10.6 %collective-permute-start.12 = (bf16[256,256]{1,0:T(8,128)(2,1)}, bf16[256,256]{1,0:T(8,128)(2,1)}, u32[]{:S(2)}, u32[]{:S(2)}) collective-permute-start(bf16[256,256]{1,0:T(8,128)(2,1)} %bitcast.10), channel_id=1, source_target_pairs={{0,8},{1,9},{2,10},{3,11},{4,12},{5,13},{6,14},{7,15},{8,0},{9,1},... | collective-permute-start | bytes 393224 | tf_op jit(solution)/shard_map/ppermute | solution.py:29
  142.4 5.8 %collective-permute-start.11 = (bf16[256,256]{1,0:T(8,128)(2,1)}, bf16[256,256]{1,0:T(8,128)(2,1)}, u32[]{:S(2)}, u32[]{:S(2)}) collective-permute-start(bf16[256,256]{1,0:T(8,128)(2,1)} %bitcast.7), channel_id=1, source_target_pairs={{0,4},{1,5},{2,6},{3,7},{4,0},{5,1},{6,2},{7,3},{8,12},{9,13},{10,... | collective-permute-start | bytes 393224 | tf_op jit(solution)/shard_map/ppermute | solution.py:29
  147.9 1.6 collective-permute-start.18
  152.8 6.8 %collective-permute-start.19 = (bf16[256,512]{1,0:T(8,128)(2,1)}, bf16[256,512]{1,0:T(8,128)(2,1)S(1)}, u32[]{:S(2)}, u32[]{:S(2)}) collective-permute-start(bf16[256,512]{1,0:T(8,128)(2,1)} %get-tuple-element.68), channel_id=1, source_target_pairs={{0,0},{1,8},{2,3},{3,11},{4,4},{5,12},{6,7},{7,15},{8,1},{9,9},{10... | collective-permute-start | bytes 786440 | tf_op jit(solution)/shard_map/ppermute | solution.py:29
  154.4 6.6 %collective-permute-start.20 = (bf16[256,512]{1,0:T(8,128)(2,1)}, bf16[256,512]{1,0:T(8,128)(2,1)S(1)}, u32[]{:S(2)}, u32[]{:S(2)}) collective-permute-start(bf16[256,512]{1,0:T(8,128)(2,1)} %get-tuple-element.69), channel_id=1, source_target_pairs={{0,3},{1,11},{2,0},{3,8},{4,7},{5,15},{6,4},{7,12},{8,2},{9,10},{1... | collective-permute-start | bytes 786440 | tf_op jit(solution)/shard_map/ppermute | solution.py:29
  156.1 6.6 %collective-permute-start.21 = (bf16[256,512]{1,0:T(8,128)(2,1)}, bf16[256,512]{1,0:T(8,128)(2,1)S(1)}, u32[]{:S(2)}, u32[]{:S(2)}) collective-permute-start(bf16[256,512]{1,0:T(8,128)(2,1)} %get-tuple-element.70), channel_id=1, source_target_pairs={{0,4},{1,12},{2,7},{3,15},{4,0},{5,8},{6,3},{7,11},{8,5},{9,13},{1... | collective-permute-start | bytes 786440 | tf_op jit(solution)/shard_map/ppermute | solution.py:29
  156.6 15.8 %collective-permute-start.22 = (bf16[256,512]{1,0:T(8,128)(2,1)}, bf16[256,512]{1,0:T(8,128)(2,1)S(1)}, u32[]{:S(2)}, u32[]{:S(2)}) collective-permute-start(bf16[256,512]{1,0:T(8,128)(2,1)} %get-tuple-element.71), channel_id=1, source_target_pairs={{0,7},{1,15},{2,4},{3,12},{4,3},{5,11},{6,0},{7,8},{8,6},{9,14},{1... | collective-permute-start | bytes 786440 | tf_op jit(solution)/shard_map/ppermute | solution.py:29
  159.6 12.8 %copy-start.14 = (bf16[256,512]{1,0:T(8,128)(2,1)}, bf16[256,512]{1,0:T(8,128)(2,1)S(1)}, u32[]{:S(2)}) copy-start(bf16[256,512]{1,0:T(8,128)(2,1)S(1)} %collective-permute-done.19.refs_0_) | copy-start | bytes 786436
  161.0 11.4 %copy-start.15 = (bf16[256,512]{1,0:T(8,128)(2,1)}, bf16[256,512]{1,0:T(8,128)(2,1)S(1)}, u32[]{:S(2)}) copy-start(bf16[256,512]{1,0:T(8,128)(2,1)S(1)} %collective-permute-done.20.refs_1_) | copy-start | bytes 786436
  162.7 9.7 %copy-start.16 = (bf16[256,512]{1,0:T(8,128)(2,1)}, bf16[256,512]{1,0:T(8,128)(2,1)S(1)}, u32[]{:S(2)}) copy-start(bf16[256,512]{1,0:T(8,128)(2,1)S(1)} %collective-permute-done.21.refs_2_) | copy-start | bytes 786436
  (11 other events, 19.9 us)

commit v7 on v6

--- a/solution.py
+++ b/solution.py
@@ -313,7 +313,7 @@
 
 
 def collect_kernel(pos, *refs):
-    parts, out = refs[:-1], refs[-1]
+    parts, out = refs[-2::-1], refs[-1]
     wide = out.shape[1] // 2
     for a in range(2):
         total = parts[2 * a][...].astype(jnp.float32) + parts[2 * a + 1][...].astype(jnp.float32)
@@ -329,7 +329,7 @@
         in_specs=[pl.BlockSpec(memory_space=pltpu.SMEM)] + [whole] * 4,
         out_specs=whole,
         name="collect",
-    )(pos, *parts)
+    )(pos, *parts[::-1])
 
 
 def place_kernel(pos, *refs):
@@ -357,8 +357,8 @@
 
 
 def deliver(parts):
-    arrived = []
-    for n, part in enumerate(parts):
+    arrived = [None] * len(parts)
+    for n in reversed(range(len(parts))):
         a1, a2 = n // 2, n % 2
 
         def route(t, s):
@@ -366,7 +366,7 @@
             y, core = s // 2, s % 2
             return (g * GROUP + 2 * core + (x ^ a1), 2 * (y ^ a2) + (z ^ y ^ a2 ^ g))
 
-        arrived.append(send(part, route))
+        arrived[n] = send(parts[n], route)
     return arrived
 
 

time: 176 us -> 173 us (0.983)
  waiting for transfers between devices: 82.6 us -> 79.9 us
    ppermute x23, waiting for transfers between devices: 82.6 us -> 79.9 us  [send(): return lax.ppermute(block, AXES, pairs)]
  transfers between devices with their start and end apart: 23 -> 23, of which waited for: 12 -> 11; matrix products, arithmetic and copies ran while one was open for 5% -> 5% of each run, Pallas kernels for 15% -> 16%
where the time goes in v7:
time: 173 us; the launch traced here: 172 us
  waiting for transfers between devices  79.9 us (46%)
  Pallas kernels  39.5 us (23%)
  starting transfers between devices  34.9 us (20%)
  local copies, waits for them, and re-layouts  15.5 us (9%)
    ppermute x23, waiting for transfers between devices, send(): return lax.ppermute(block, AXES, pairs)  79.9 us
    ppermute x23, starting transfers between devices, send(): return lax.ppermute(block, AXES, pairs)  34.9 us
    pallas_call x3, Pallas kernels, attend(): pl.pallas_call(functools.partial(attend_kernel, span, n_halo, bool(halos)...  18.3 us
    pallas_call x3, Pallas kernels, project(): pl.pallas_call(functools.partial(project_kernel, [part for _, part in par...  11.1 us
    unnamed x40, local copies, waits for them, and re-layouts  8.48 us
    slice x4, local copies, waits for them, and re-layouts, rows_of(): return kv_weight[:, cuts[n] * unit:cuts[n + 1] * unit]  4.25 us
  transfers between devices with their start and end apart: 23, of which 11 were waited for; matrix products, arithmetic and copies ran while one was open for 5% of the time, Pallas kernels for 16%

profile of v7, /device:TPU:0, one launch (start us, length us, event | category | flops | bytes accessed | tf_op | source)
XLA Modules:
  0.0 172.2 jit_solution(3600036040568466342)
XLA Ops:
  0.6 3.3 %pack.1 = (bf16[1040,256]{1,0:T(8,128)(2,1)}, bf16[1040,256]{1,0:T(8,128)(2,1)}, bf16[1040,256]{1,0:T(8,128)(2,1)}, bf16[1040,256]{1,0:T(8,128)(2,1)}) custom-call(s32[2,4]{1,0:T(2,128)} %block_ids.1, s32[2]{0:T(128)} %block_count.1, bf16[256,1024]{1,0:T(8,128)(2,1)} %queries.1, bf16[256,1024]{1,0:T(8,128)(2,1)} %grad_out.1, bf16[2,256,1024]{2,1,0:T(8,128)(2,1)} %key_values.1), custom_call_target="tpu_custom_call" | custom-call | tf_op jit(solution)/shard_map/pack/pallas_call | solution.py:66
  3.9 4.0 %collective-permute-start.2 = (bf16[1040,256]{1,0:T(8,128)(2,1)}, bf16[1040,256]{1,0:T(8,128)(2,1)}, u32[]{:S(2)}, u32[]{:S(2)}) collective-permute-start(bf16[1040,256]{1,0:T(8,128)(2,1)} %get-tuple-element.40), channel_id=1, source_target_pairs={{0,12},{1,13},{2,14},{3,15},{4,8},{5,9},{6,10},{7,11},{8,4},{9,5},... | collective-permute-start | bytes 1597448 | tf_op jit(solution)/shard_map/ppermute | solution.py:29
  9.5 1.6 collective-permute-start.3
  11.9 9.3 %collective-permute-done.2.refs_3_ = bf16[1040,256]{1,0:T(8,128)(2,1)} collective-permute-done((bf16[1040,256]{1,0:T(8,128)(2,1)}, bf16[1040,256]{1,0:T(8,128)(2,1)}, u32[]{:S(2)}, u32[]{:S(2)}) %collective-permute-start.2) | collective-permute-done | bytes 532512 | tf_op jit(solution)/shard_map/ppermute | solution.py:29
  21.8 10.1 %collective-permute-done.1.refs_2_ = bf16[1040,256]{1,0:T(8,128)(2,1)} collective-permute-done((bf16[1040,256]{1,0:T(8,128)(2,1)}, bf16[1040,256]{1,0:T(8,128)(2,1)}, u32[]{:S(2)}, u32[]{:S(2)}) %collective-permute-start.1) | collective-permute-done | bytes 532512 | tf_op jit(solution)/shard_map/ppermute | solution.py:29
  34.4 2.7 %collective-permute-start.4 = (bf16[512,256]{1,0:T(8,128)(2,1)S(1)}, bf16[512,256]{1,0:T(8,128)(2,1)S(1)}, u32[]{:S(2)}, u32[]{:S(2)}) collective-permute-start(bf16[512,256]{1,0:T(8,128)(2,1)S(1)} %fusion.1), channel_id=1, source_target_pairs={{0,16},{1,17},{2,18},{3,19},{4,20},{5,21},{6,22},{7,23},{8,24},{9,... | collective-permute-start | bytes 786440 | tf_op jit(solution)/shard_map/ppermute | solution.py:29
  37.1 6.0 %attend.3 = (f32[2,10,128,256]{3,2,1,0:T(8,128)S(1)}, bf16[8,128,256]{2,1,0:T(8,128)(2,1)S(1)}) custom-call(s32[4,2,5]{2,1,0:T(2,128)S(1)} %maximum_convert_fusion.meta, s32[2]{0:T(128)S(1)} %pad_add_fusion.pos, bf16[1040,256]{1,0:T(8,128)(2,1)S(1)} %copy-done.7, bf16[1040,256]{1,0:T(8,128)(2,1)} %collective-permute-done.refs_1_, ...), custom_call_target="tpu_custom_call" | custom-call | flops 2013265920 | bytes 4194304 | tf_op jit(solution)/shard_map/attend/pallas_call | solution.py:192
  43.1 5.4 %collective-permute-done.4.refs_4_ = bf16[512,256]{1,0:T(8,128)(2,1)S(1)} collective-permute-done((bf16[512,256]{1,0:T(8,128)(2,1)S(1)}, bf16[512,256]{1,0:T(8,128)(2,1)S(1)}, u32[]{:S(2)}, u32[]{:S(2)}) %collective-permute-start.4) | collective-permute-done | bytes 262176 | tf_op jit(solution)/shard_map/ppermute | solution.py:29
  48.5 4.6 %attend.4 = (f32[2,10,128,256]{3,2,1,0:T(8,128)S(1)}, bf16[8,128,256]{2,1,0:T(8,128)(2,1)S(1)}, bf16[2,2,128,256]{3,2,1,0:T(8,128)(2,1)S(1)}) custom-call(s32[4,2,5]{2,1,0:T(2,128)S(1)} %maximum_convert_fusion.meta, s32[2]{0:T(128)S(1)} %pad_add_fusion.pos, bf16[1040,256]{1,0:T(8,128)(2,1)S(1)} %copy-done.7, bf16[1040,256]{1,0:T(8,128)(2,1)} %collective-permute-done.refs_1_, ...), custom_call_target="tpu_custom_call" | custom-call | flops 1342177280 | bytes 4194304 | tf_op jit(solution)/shard_map/attend/pallas_call | solution.py:192
  53.2 7.8 %attend.5 = (f32[2,10,128,256]{3,2,1,0:T(8,128)}, bf16[8,128,256]{2,1,0:T(8,128)(2,1)}, bf16[2,128,256]{2,1,0:T(8,128)(2,1)S(1)}, bf16[2,128,256]{2,1,0:T(8,128)...) custom-call(s32[4,2,5]{2,1,0:T(2,128)S(1)} %maximum_convert_fusion.m, ...), custom_call_target="tpu_custom_call" | custom-call | flops 2013265920 | bytes 4194304 | tf_op jit(solution)/shard_map/attend/pallas_call | solution.py:192
  61.7 5.3 %collective-permute-start.5 = (bf16[2,6,128,256]{3,2,1,0:T(8,128)(2,1)S(1)}, bf16[2,6,128,256]{3,2,1,0:T(8,128)(2,1)S(1)}, u32[]{:S(2)}, u32[]{:S(2)}) collective-permute-start(bf16[2,6,128,256]{3,2,1,0:T(8,128)(2,1)S(1)} %get-tuple-element.49), channel_id=1, source_target_pairs={{0,8},{1,9},{2,10},{3,11},{4,12},{5,13},{6,14},{7,15},{8,0},{9,1},... | collective-permute-start | bytes 2359304 | tf_op jit(solution)/shard_map/ppermute | solution.py:29
  67.2 1.6 collective-permute-start.8
  70.1 20.0 %collective-permute-done.7 = bf16[2,2,128,256]{3,2,1,0:T(8,128)(2,1)S(1)} collective-permute-done((bf16[2,2,128,256]{3,2,1,0:T(8,128)(2,1)S(1)}, bf16[2,2,128,256]{3,2,1,0:T(8,128)(2,1)S(1)}, u32[]{:S(2)}, u32[]{:S(2)}) %collective-permute-start.7) | collective-permute-done | bytes 262176 | tf_op jit(solution)/shard_map/ppermute | solution.py:29
  91.2 4.5 %collective-permute-start.15 = (bf16[2,384,1024]{2,1,0:T(8,128)(2,1)}, bf16[2,384,1024]{2,1,0:T(8,128)(2,1)}, u32[]{:S(2)}, u32[]{:S(2)}) collective-permute-start(bf16[2,384,1024]{2,1,0:T(8,128)(2,1)} %slice.46), channel_id=1, source_target_pairs={{0,24},{1,25},{2,26},{3,27},{4,28},{5,29},{6,30},{7,31},{24,0},{25... | collective-permute-start | bytes 4718600 | tf_op jit(solution)/shard_map/ppermute | solution.py:29
  96.8 1.5 collective-permute-start.10
  98.3 1.9 %slice.47 = bf16[2,128,1024]{2,1,0:T(8,128)(2,1)} slice(bf16[2,512,1024]{2,1,0:T(8,128)(2,1)} %refs_4_.1), slice={[0:2], [384:512], [0:1024]} | slice | bytes 1048576 | tf_op jit(solution)/shard_map/slice | solution.py:421
  100.2 20.2 %collective-permute-done.10.refs_3_ = bf16[2048,256]{1,0:T(8,128)(2,1)S(1)} collective-permute-done((bf16[2048,256]{1,0:T(8,128)(2,1)S(1)}, bf16[2048,256]{1,0:T(8,128)(2,1)S(1)}, u32[]{:S(2)}, u32[]{:S(2)}) %collective-permute-start.10) | collective-permute-done | bytes 1048608 | tf_op jit(solution)/shard_map/ppermute | solution.py:29
  120.4 3.4 %collective-permute-start.16 = (bf16[2,128,1024]{2,1,0:T(8,128)(2,1)}, bf16[2,128,1024]{2,1,0:T(8,128)(2,1)S(1)}, u32[]{:S(2)}, u32[]{:S(2)}) collective-permute-start(bf16[2,128,1024]{2,1,0:T(8,128)(2,1)} %slice.47), channel_id=1, source_target_pairs={{0,24},{1,25},{2,26},{3,27},{4,28},{5,29},{6,30},{7,31},{24,0},{25... | collective-permute-start | bytes 1572872 | tf_op jit(solution)/shard_map/ppermute | solution.py:29
  123.8 1.6 copy-done.1
  126.6 4.0 %project.3 = (bf16[2,256,512]{2,1,0:T(8,128)(2,1)}, bf16[2,256,512]{2,1,0:T(8,128)(2,1)S(1)}) custom-call(s32[7]{0:T(128)S(1)} %stack.74.pos, bf16[2048,256]{1,0:T(8,128)(2,1)S(1)} %bitcast.24, bf16[2048,256]{1,0:T(8,128)(2,1)S(1)} %copy-done.5, bf16[2048,256]{1,0:T(8,128)(2,1)S(1)} %bitcast.28, bf16[2048,256]{1,0:T(8,128)(2,1)S(1)} %collective-permute-done.10.refs_3_, ...), custom_call_target="tpu_custom_call" | custom-call | flops 2147483648 | bytes 6291456 | tf_op jit(solution)/shard_map/project/pallas_call | solution.py:261
  132.6 4.5 %project.4 = (bf16[2,256,384]{2,1,0:T(8,128)(2,1)S(1)}, bf16[2,256,384]{2,1,0:T(8,128)(2,1)S(1)}) custom-call(s32[7]{0:T(128)S(1)} %stack.74.pos, bf16[2048,256]{1,0:T(8,128)(2,1)S(1)} %bitcast.25, bf16[2048,256]{1,0:T(8,128)(2,1)S(1)} %copy-done.6, bf16[2048,256]{1,0:T(8,128)(2,1)S(1)} %bitcast.29, bf16[2048,256]{1,0:T(8,128)(2,1)S(1)} %collective-permute-done.10.refs_3_, ...), custom_call_target="tpu_custom_call" | custom-call | flops 1610612736 | bytes 6291456 | tf_op jit(solution)/shard_map/project/pallas_call | solution.py:261
  137.3 2.9 %collective-permute-start.12 = (bf16[256,256]{1,0:T(8,128)(2,1)}, bf16[256,256]{1,0:T(8,128)(2,1)}, u32[]{:S(2)}, u32[]{:S(2)}) collective-permute-start(bf16[256,256]{1,0:T(8,128)(2,1)} %bitcast.10), channel_id=1, source_target_pairs={{0,8},{1,9},{2,10},{3,11},{4,12},{5,13},{6,14},{7,15},{8,0},{9,1},... | collective-permute-start | bytes 393224 | tf_op jit(solution)/shard_map/ppermute | solution.py:29
  140.2 2.2 %collective-permute-done.16.refs_5_ = bf16[2,128,1024]{2,1,0:T(8,128)(2,1)S(1)} collective-permute-done((bf16[2,128,1024]{2,1,0:T(8,128)(2,1)}, bf16[2,128,1024]{2,1,0:T(8,128)(2,1)S(1)}, u32[]{:S(2)}, u32[]{:S(2)}) %collective-permute-start.16) | collective-permute-done | bytes 524320 | tf_op jit(solution)/shard_map/ppermute | solution.py:29
  142.4 1.5 collective-permute-start.11
  144.0 2.6 %project.5 = (bf16[2,256,128]{2,1,0:T(8,128)(2,1)}, bf16[2,256,128]{2,1,0:T(8,128)(2,1)S(1)}) custom-call(s32[7]{0:T(128)S(1)} %stack.74.pos, bf16[2048,256]{1,0:T(8,128)(2,1)S(1)} %bitcast.26, bf16[2048,256]{1,0:T(8,128)(2,1)S(1)} %copy-done.6, bf16[2048,256]{1,0:T(8,128)(2,1)S(1)} %bitcast.30, bf16[2048,256]{1,0:T(8,128)(2,1)S(1)} %collective-permute-done.10.refs_3_, ...), custom_call_target="tpu_custom_call" | custom-call | flops 536870912 | bytes 6291456 | tf_op jit(solution)/shard_map/project/pallas_call | solution.py:261
  150.1 2.7 %merge.1 = (bf16[256,512]{1,0:T(8,128)(2,1)}, bf16[256,512]{1,0:T(8,128)(2,1)}, bf16[256,512]{1,0:T(8,128)(2,1)}, bf16[256,512]{1,0:T(8,128)(2,1)}) custom-call(s32[1]{0:T(128)} %bitcast.13.flip, bf16[2,256,512]{2,1,0:T(8,128)(2,1)} %copy-done.8, bf16[2,256,512]{2,1,0:T(8,128)(2,1)} %collective-permute-done.14.refs_1_, bf16[2,256,384]{2,1,0:T(8,128)(2,1)} %copy-done.9, ...), custom_call_target="tpu_custom_call" | custom-call | tf_op jit(solution)/shard_map/merge/pallas_call | solution.py:306
  154.0 1.5 collective-permute-start.20
  155.5 1.6 collective-permute-start.22
  157.1 2.0 %place_columns.1 = bf16[256,1024]{1,0:T(8,128)(2,1)} custom-call(s32[1]{0:T(128)} %bitcast.pos, bf16[256,256]{1,0:T(8,128)(2,1)} %bitcast.31, bf16[256,256]{1,0:T(8,128)(2,1)} %collective-permute-done.11.refs_1_, bf16[256,256]{1,0:T(8,128)(2,1)} %collective-permute-done.12.refs_2_, bf16[256,256]{1,0:T(8,128)(2,1)} %copy-done.19), custom_call_target="tpu_custom_call" | custom-call | tf_op jit(solution)/shard_map/place_columns/pallas_call | solution.py:346
  159.1 8.8 %collective-permute-done.19.refs_0_ = bf16[256,512]{1,0:T(8,128)(2,1)S(1)} collective-permute-done((bf16[256,512]{1,0:T(8,128)(2,1)}, bf16[256,512]{1,0:T(8,128)(2,1)S(1)}, u32[]{:S(2)}, u32[]{:S(2)}) %collective-permute-start.19) | collective-permute-done | bytes 262176 | tf_op jit(solution)/shard_map/ppermute | solution.py:29
  167.9 1.3 collective-permute-done.20.refs_1_
  170.1 2.1 %collect.1 = bf16[256,1024]{1,0:T(8,128)(2,1)} custom-call(s32[1]{0:T(128)} %bitcast.12.pos, bf16[256,512]{1,0:T(8,128)(2,1)} %copy-done.14, bf16[256,512]{1,0:T(8,128)(2,1)} %copy-done.15, bf16[256,512]{1,0:T(8,128)(2,1)} %copy-done.16, bf16[256,512]{1,0:T(8,128)(2,1)} %copy-done.17), custom_call_target="tpu_custom_call" | custom-call | tf_op jit(solution)/shard_map/collect/pallas_call | solution.py:326
  (79 shorter events, 19.0 us)
Async XLA Ops:
  0.6 7.9 %copy-start = (bf16[2,512,1024]{2,1,0:T(8,128)(2,1)S(1)}, bf16[2,512,1024]{2,1,0:T(8,128)(2,1)}, u32[]{:S(2)}) copy-start(bf16[2,512,1024]{2,1,0:T(8,128)(2,1)} %refs_4_.1) | copy-start | bytes 6291460
  3.9 29.3 %copy-start.7 = (bf16[1040,256]{1,0:T(8,128)(2,1)S(1)}, bf16[1040,256]{1,0:T(8,128)(2,1)}, u32[]{:S(2)}) copy-start(bf16[1040,256]{1,0:T(8,128)(2,1)} %get-tuple-element.37.refs_0_) | copy-start | bytes 1597444
  3.9 17.2 %collective-permute-start.2 = (bf16[1040,256]{1,0:T(8,128)(2,1)}, bf16[1040,256]{1,0:T(8,128)(2,1)}, u32[]{:S(2)}, u32[]{:S(2)}) collective-permute-start(bf16[1040,256]{1,0:T(8,128)(2,1)} %get-tuple-element.40), channel_id=1, source_target_pairs={{0,12},{1,13},{2,14},{3,15},{4,8},{5,9},{6,10},{7,11},{8,4},{9,5},... | collective-permute-start | bytes 1597448 | tf_op jit(solution)/shard_map/ppermute | solution.py:29
  7.9 24.0 %collective-permute-start.1 = (bf16[1040,256]{1,0:T(8,128)(2,1)}, bf16[1040,256]{1,0:T(8,128)(2,1)}, u32[]{:S(2)}, u32[]{:S(2)}) collective-permute-start(bf16[1040,256]{1,0:T(8,128)(2,1)} %get-tuple-element.39), channel_id=1, source_target_pairs={{0,8},{1,9},{2,10},{3,11},{4,12},{5,13},{6,14},{7,15},{8,0},{9,1},... | collective-permute-start | bytes 1597448 | tf_op jit(solution)/shard_map/ppermute | solution.py:29
  8.3 24.3 %collective-permute-start = (bf16[1040,256]{1,0:T(8,128)(2,1)}, bf16[1040,256]{1,0:T(8,128)(2,1)}, u32[]{:S(2)}, u32[]{:S(2)}) collective-permute-start(bf16[1040,256]{1,0:T(8,128)(2,1)} %get-tuple-element.38), channel_id=1, source_target_pairs={{0,4},{1,5},{2,6},{3,7},{4,0},{5,1},{6,2},{7,3},{8,12},{9,13},{10,... | collective-permute-start | bytes 1597448 | tf_op jit(solution)/shard_map/ppermute | solution.py:29
  9.5 24.9 %collective-permute-start.3 = (bf16[2,224,1024]{2,1,0:T(8,128)(2,1)}, bf16[2,224,1024]{2,1,0:T(8,128)(2,1)}, u32[]{:S(2)}, u32[]{:S(2)}) collective-permute-start(bf16[2,224,1024]{2,1,0:T(8,128)(2,1)} %slice.44), channel_id=1, source_target_pairs={{8,16},{9,17},{10,18},{11,19},{12,20},{13,21},{14,22},{15,23},{16,... | collective-permute-start | bytes 2752520 | tf_op jit(solution)/shard_map/ppermute | solution.py:29
  34.4 14.0 %collective-permute-start.4 = (bf16[512,256]{1,0:T(8,128)(2,1)S(1)}, bf16[512,256]{1,0:T(8,128)(2,1)S(1)}, u32[]{:S(2)}, u32[]{:S(2)}) collective-permute-start(bf16[512,256]{1,0:T(8,128)(2,1)S(1)} %fusion.1), channel_id=1, source_target_pairs={{0,16},{1,17},{2,18},{3,19},{4,20},{5,21},{6,22},{7,23},{8,24},{9,... | collective-permute-start | bytes 786440 | tf_op jit(solution)/shard_map/ppermute | solution.py:29
  53.0 14.0 %collective-permute-start.6 = (bf16[2,2,128,256]{3,2,1,0:T(8,128)(2,1)S(1)}, bf16[2,2,128,256]{3,2,1,0:T(8,128)(2,1)S(1)}, u32[]{:S(2)}, u32[]{:S(2)}) collective-permute-start(bf16[2,2,128,256]{3,2,1,0:T(8,128)(2,1)S(1)} %get-tuple-element.51), channel_id=1, source_target_pairs={{0,16},{1,17},{2,18},{3,19},{4,20},{5,21},{6,22},{7,23},{8,24},{9,... | collective-permute-start | bytes 786440 | tf_op jit(solution)/shard_map/ppermute | solution.py:29
  61.0 9.1 %copy-start.11 = (bf16[2,128,256]{2,1,0:T(8,128)(2,1)}, bf16[2,128,256]{2,1,0:T(8,128)(2,1)S(1)}, u32[]{:S(2)}) copy-start(bf16[2,128,256]{2,1,0:T(8,128)(2,1)S(1)} %get-tuple-element.47) | copy-start | bytes 393220
  61.0 9.1 %copy-start.12 = (bf16[2,128,256]{2,1,0:T(8,128)(2,1)}, bf16[2,128,256]{2,1,0:T(8,128)(2,1)S(1)}, u32[]{:S(2)}) copy-start(bf16[2,128,256]{2,1,0:T(8,128)(2,1)S(1)} %get-tuple-element.57) | copy-start | bytes 393220
  61.0 29.2 %collective-permute-start.9 = (bf16[2,288,1024]{2,1,0:T(8,128)(2,1)S(1)}, bf16[2,288,1024]{2,1,0:T(8,128)(2,1)S(1)}, u32[]{:S(2)}, u32[]{:S(2)}) collective-permute-start(bf16[2,288,1024]{2,1,0:T(8,128)(2,1)S(1)} %slice.45), channel_id=1, source_target_pairs={{8,16},{9,17},{10,18},{11,19},{12,20},{13,21},{14,22},{15,23},{16,... | collective-permute-start | bytes 3538952 | tf_op jit(solution)/shard_map/ppermute | solution.py:29
  61.7 28.4 %collective-permute-start.5 = (bf16[2,6,128,256]{3,2,1,0:T(8,128)(2,1)S(1)}, bf16[2,6,128,256]{3,2,1,0:T(8,128)(2,1)S(1)}, u32[]{:S(2)}, u32[]{:S(2)}) collective-permute-start(bf16[2,6,128,256]{3,2,1,0:T(8,128)(2,1)S(1)} %get-tuple-element.49), channel_id=1, source_target_pairs={{0,8},{1,9},{2,10},{3,11},{4,12},{5,13},{6,14},{7,15},{8,0},{9,1},... | collective-permute-start | bytes 2359304 | tf_op jit(solution)/shard_map/ppermute | solution.py:29
  67.2 28.6 %collective-permute-start.8 = (bf16[2048,256]{1,0:T(8,128)(2,1)S(1)}, bf16[2048,256]{1,0:T(8,128)(2,1)S(1)}, u32[]{:S(2)}, u32[]{:S(2)}) collective-permute-start(bf16[2048,256]{1,0:T(8,128)(2,1)S(1)} %bitcast.23), channel_id=1, source_target_pairs={{0,4},{1,5},{2,6},{3,7},{4,0},{5,1},{6,2},{7,3},{8,12},{9,13},{10,... | collective-permute-start | bytes 3145736 | tf_op jit(solution)/shard_map/ppermute | solution.py:29
  68.8 21.3 %collective-permute-start.7 = (bf16[2,2,128,256]{3,2,1,0:T(8,128)(2,1)S(1)}, bf16[2,2,128,256]{3,2,1,0:T(8,128)(2,1)S(1)}, u32[]{:S(2)}, u32[]{:S(2)}) collective-permute-start(bf16[2,2,128,256]{3,2,1,0:T(8,128)(2,1)S(1)} %add_convert_fusion), channel_id=1, source_target_pairs={{0,8},{1,9},{2,10},{3,11},{4,12},{5,13},{6,14},{7,15},{8,0},{9,1},... | collective-permute-start | bytes 786440 | tf_op jit(solution)/shard_map/ppermute | solution.py:29
  91.2 41.3 %collective-permute-start.15 = (bf16[2,384,1024]{2,1,0:T(8,128)(2,1)}, bf16[2,384,1024]{2,1,0:T(8,128)(2,1)}, u32[]{:S(2)}, u32[]{:S(2)}) collective-permute-start(bf16[2,384,1024]{2,1,0:T(8,128)(2,1)} %slice.46), channel_id=1, source_target_pairs={{0,24},{1,25},{2,26},{3,27},{4,28},{5,29},{6,30},{7,31},{24,0},{25... | collective-permute-start | bytes 4718600 | tf_op jit(solution)/shard_map/ppermute | solution.py:29
  96.8 23.6 %collective-permute-start.10 = (bf16[2048,256]{1,0:T(8,128)(2,1)S(1)}, bf16[2048,256]{1,0:T(8,128)(2,1)S(1)}, u32[]{:S(2)}, u32[]{:S(2)}) collective-permute-start(bf16[2048,256]{1,0:T(8,128)(2,1)S(1)} %bitcast.27), channel_id=1, source_target_pairs={{0,4},{1,5},{2,6},{3,7},{4,0},{5,1},{6,2},{7,3},{8,12},{9,13},{10,... | collective-permute-start | bytes 3145736 | tf_op jit(solution)/shard_map/ppermute | solution.py:29
  120.4 22.0 %collective-permute-start.16 = (bf16[2,128,1024]{2,1,0:T(8,128)(2,1)}, bf16[2,128,1024]{2,1,0:T(8,128)(2,1)S(1)}, u32[]{:S(2)}, u32[]{:S(2)}) collective-permute-start(bf16[2,128,1024]{2,1,0:T(8,128)(2,1)} %slice.47), channel_id=1, source_target_pairs={{0,24},{1,25},{2,26},{3,27},{4,28},{5,29},{6,30},{7,31},{24,0},{25... | collective-permute-start | bytes 1572872 | tf_op jit(solution)/shard_map/ppermute | solution.py:29
  123.8 1.6 copy-start.1
  126.6 5.9 %copy-start.3 = (bf16[2,288,1024]{2,1,0:T(8,128)(2,1)S(1)}, bf16[2,288,1024]{2,1,0:T(8,128)(2,1)}, u32[]{:S(2)}) copy-start(bf16[2,288,1024]{2,1,0:T(8,128)(2,1)} %copy-done.2) | copy-start | bytes 3538948
  126.6 5.9 %copy-start.6 = (bf16[2048,256]{1,0:T(8,128)(2,1)S(1)}, bf16[2048,256]{1,0:T(8,128)(2,1)}, u32[]{:S(2)}) copy-start(bf16[2048,256]{1,0:T(8,128)(2,1)} %copy-done.4) | copy-start | bytes 3145732
  131.5 5.7 %copy-start.13 = (bf16[2,128,256]{2,1,0:T(8,128)(2,1)S(1)}, bf16[2,128,256]{2,1,0:T(8,128)(2,1)}, u32[]{:S(2)}) copy-start(bf16[2,128,256]{2,1,0:T(8,128)(2,1)} %copy-done.12) | copy-start | bytes 393220
  131.5 16.8 %collective-permute-start.14 = (bf16[2,256,512]{2,1,0:T(8,128)(2,1)}, bf16[2,256,512]{2,1,0:T(8,128)(2,1)}, u32[]{:S(2)}, u32[]{:S(2)}) collective-permute-start(bf16[2,256,512]{2,1,0:T(8,128)(2,1)} %get-tuple-element.60), channel_id=1, source_target_pairs={{0,1},{1,0},{2,3},{3,2},{4,5},{5,4},{6,7},{7,6},{8,9},{9,8},{10,11... | collective-permute-start | bytes 1572872 | tf_op jit(solution)/shard_map/ppermute | solution.py:29
  137.1 9.5 %copy-start.9 = (bf16[2,256,384]{2,1,0:T(8,128)(2,1)}, bf16[2,256,384]{2,1,0:T(8,128)(2,1)S(1)}, u32[]{:S(2)}) copy-start(bf16[2,256,384]{2,1,0:T(8,128)(2,1)S(1)} %get-tuple-element.62.refs_2_) | copy-start | bytes 1179652
  137.1 12.3 %collective-permute-start.17 = (bf16[2,256,384]{2,1,0:T(8,128)(2,1)S(1)}, bf16[2,256,384]{2,1,0:T(8,128)(2,1)}, u32[]{:S(2)}, u32[]{:S(2)}) collective-permute-start(bf16[2,256,384]{2,1,0:T(8,128)(2,1)S(1)} %get-tuple-element.66), channel_id=1, source_target_pairs={{0,1},{1,0},{2,3},{3,2},{4,5},{5,4},{6,7},{7,6},{8,9},{9,8},{10,11... | collective-permute-start | bytes 1179656 | tf_op jit(solution)/shard_map/ppermute | solution.py:29
  137.2 10.0 %collective-permute-start.13 = (bf16[256,256]{1,0:T(8,128)(2,1)S(1)}, bf16[256,256]{1,0:T(8,128)(2,1)S(1)}, u32[]{:S(2)}, u32[]{:S(2)}) collective-permute-start(bf16[256,256]{1,0:T(8,128)(2,1)S(1)} %bitcast.32), channel_id=1, source_target_pairs={{0,12},{1,13},{2,14},{3,15},{4,8},{5,9},{6,10},{7,11},{8,4},{9,5},... | collective-permute-start | bytes 393224 | tf_op jit(solution)/shard_map/ppermute | solution.py:29
  137.3 10.6 %collective-permute-start.12 = (bf16[256,256]{1,0:T(8,128)(2,1)}, bf16[256,256]{1,0:T(8,128)(2,1)}, u32[]{:S(2)}, u32[]{:S(2)}) collective-permute-start(bf16[256,256]{1,0:T(8,128)(2,1)} %bitcast.10), channel_id=1, source_target_pairs={{0,8},{1,9},{2,10},{3,11},{4,12},{5,13},{6,14},{7,15},{8,0},{9,1},... | collective-permute-start | bytes 393224 | tf_op jit(solution)/shard_map/ppermute | solution.py:29
  142.4 5.8 %collective-permute-start.11 = (bf16[256,256]{1,0:T(8,128)(2,1)}, bf16[256,256]{1,0:T(8,128)(2,1)}, u32[]{:S(2)}, u32[]{:S(2)}) collective-permute-start(bf16[256,256]{1,0:T(8,128)(2,1)} %bitcast.7), channel_id=1, source_target_pairs={{0,4},{1,5},{2,6},{3,7},{4,0},{5,1},{6,2},{7,3},{8,12},{9,13},{10,... | collective-permute-start | bytes 393224 | tf_op jit(solution)/shard_map/ppermute | solution.py:29
  147.9 1.6 collective-permute-start.18
  152.8 15.0 %collective-permute-start.19 = (bf16[256,512]{1,0:T(8,128)(2,1)}, bf16[256,512]{1,0:T(8,128)(2,1)S(1)}, u32[]{:S(2)}, u32[]{:S(2)}) collective-permute-start(bf16[256,512]{1,0:T(8,128)(2,1)} %get-tuple-element.68), channel_id=1, source_target_pairs={{0,7},{1,15},{2,4},{3,12},{4,3},{5,11},{6,0},{7,8},{8,6},{9,14},{1... | collective-permute-start | bytes 786440 | tf_op jit(solution)/shard_map/ppermute | solution.py:29
  154.0 15.1 %collective-permute-start.20 = (bf16[256,512]{1,0:T(8,128)(2,1)}, bf16[256,512]{1,0:T(8,128)(2,1)S(1)}, u32[]{:S(2)}, u32[]{:S(2)}) collective-permute-start(bf16[256,512]{1,0:T(8,128)(2,1)} %get-tuple-element.69), channel_id=1, source_target_pairs={{0,4},{1,12},{2,7},{3,15},{4,0},{5,8},{6,3},{7,11},{8,5},{9,13},{1... | collective-permute-start | bytes 786440 | tf_op jit(solution)/shard_map/ppermute | solution.py:29
  155.5 13.6 %collective-permute-start.21 = (bf16[256,512]{1,0:T(8,128)(2,1)}, bf16[256,512]{1,0:T(8,128)(2,1)S(1)}, u32[]{:S(2)}, u32[]{:S(2)}) collective-permute-start(bf16[256,512]{1,0:T(8,128)(2,1)} %get-tuple-element.70), channel_id=1, source_target_pairs={{0,3},{1,11},{2,0},{3,8},{4,7},{5,15},{6,4},{7,12},{8,2},{9,10},{1... | collective-permute-start | bytes 786440 | tf_op jit(solution)/shard_map/ppermute | solution.py:29
  155.5 13.6 %collective-permute-start.22 = (bf16[256,512]{1,0:T(8,128)(2,1)}, bf16[256,512]{1,0:T(8,128)(2,1)S(1)}, u32[]{:S(2)}, u32[]{:S(2)}) collective-permute-start(bf16[256,512]{1,0:T(8,128)(2,1)} %get-tuple-element.71), channel_id=1, source_target_pairs={{0,0},{1,8},{2,3},{3,11},{4,4},{5,12},{6,7},{7,15},{8,1},{9,9},{10... | collective-permute-start | bytes 786440 | tf_op jit(solution)/shard_map/ppermute | solution.py:29
  (11 other events, 9.7 us)

commit v8 on v7

--- a/solution.py
+++ b/solution.py
@@ -479,7 +479,7 @@
                     begin, end = max(first, lo), min(last, hi)
                     if begin < end:
                         span = ((begin - first) * unit, (end - begin) * unit, (begin - lo) * unit)
-                        parts.append((weight, (where,) + span))
+                        parts.append((after(weight, dq[1]), (where,) + span))
             give_other, keep_other = project(pos, order, 2, grads, parts)
             kept.append(keep_other)
             given.append(other_core(give_other))

time: 173 us -> 172 us (level)
  waiting for transfers between devices: 79.9 us -> 77.7 us
    ppermute x23, waiting for transfers between devices: 79.9 us -> 77.7 us  [send(): return lax.ppermute(block, AXES, pairs)]
    unnamed x40 -> x36, local copies, waits for them, and re-layouts: 8.48 us -> 8.6 us
  transfers between devices with their start and end apart: 23 -> 23, of which waited for: 11 -> 9; matrix products, arithmetic and copies ran while one was open for 5% -> 5% of each run, Pallas kernels for 16% -> 16%
where the time goes in v8:
time: 172 us; the launch traced here: 170 us
  waiting for transfers between devices  77.7 us (45%)
  Pallas kernels  39.5 us (23%)
  starting transfers between devices  34.4 us (20%)
  local copies, waits for them, and re-layouts  15.6 us (9%)
    ppermute x23, waiting for transfers between devices, send(): return lax.ppermute(block, AXES, pairs)  77.7 us
    ppermute x23, starting transfers between devices, send(): return lax.ppermute(block, AXES, pairs)  34.4 us
    pallas_call x3, Pallas kernels, attend(): pl.pallas_call(functools.partial(attend_kernel, span, n_halo, bool(halos)...  18.3 us
    pallas_call x3, Pallas kernels, project(): pl.pallas_call(functools.partial(project_kernel, [part for _, part in par...  11.1 us
    unnamed x36, local copies, waits for them, and re-layouts  8.6 us
    slice x4, local copies, waits for them, and re-layouts, rows_of(): return kv_weight[:, cuts[n] * unit:cuts[n + 1] * unit]  4.24 us
  transfers between devices with their start and end apart: 23, of which 9 were waited for; matrix products, arithmetic and copies ran while one was open for 5% of the time, Pallas kernels for 16%

profile of v8, /device:TPU:0, one launch (start us, length us, event | category | flops | bytes accessed | tf_op | source)
XLA Modules:
  0.0 169.6 jit_solution(2017951491266750102)
XLA Ops:
  0.6 3.3 %pack.1 = (bf16[1040,256]{1,0:T(8,128)(2,1)}, bf16[1040,256]{1,0:T(8,128)(2,1)}, bf16[1040,256]{1,0:T(8,128)(2,1)}, bf16[1040,256]{1,0:T(8,128)(2,1)}) custom-call(s32[2,4]{1,0:T(2,128)} %block_ids.1, s32[2]{0:T(128)} %block_count.1, bf16[256,1024]{1,0:T(8,128)(2,1)} %queries.1, bf16[256,1024]{1,0:T(8,128)(2,1)} %grad_out.1, bf16[2,256,1024]{2,1,0:T(8,128)(2,1)} %key_values.1), custom_call_target="tpu_custom_call" | custom-call | tf_op jit(solution)/shard_map/pack/pallas_call | solution.py:66
  4.0 4.0 %collective-permute-start.2 = (bf16[1040,256]{1,0:T(8,128)(2,1)}, bf16[1040,256]{1,0:T(8,128)(2,1)}, u32[]{:S(2)}, u32[]{:S(2)}) collective-permute-start(bf16[1040,256]{1,0:T(8,128)(2,1)} %get-tuple-element.44), channel_id=1, source_target_pairs={{0,12},{1,13},{2,14},{3,15},{4,8},{5,9},{6,10},{7,11},{8,4},{9,5},... | collective-permute-start | bytes 1597448 | tf_op jit(solution)/shard_map/ppermute | solution.py:29
  9.6 1.6 collective-permute-start.3
  11.9 9.3 %collective-permute-done.2.refs_3_ = bf16[1040,256]{1,0:T(8,128)(2,1)} collective-permute-done((bf16[1040,256]{1,0:T(8,128)(2,1)}, bf16[1040,256]{1,0:T(8,128)(2,1)}, u32[]{:S(2)}, u32[]{:S(2)}) %collective-permute-start.2) | collective-permute-done | bytes 532512 | tf_op jit(solution)/shard_map/ppermute | solution.py:29
  21.8 10.1 %collective-permute-done.1.refs_2_ = bf16[1040,256]{1,0:T(8,128)(2,1)} collective-permute-done((bf16[1040,256]{1,0:T(8,128)(2,1)}, bf16[1040,256]{1,0:T(8,128)(2,1)}, u32[]{:S(2)}, u32[]{:S(2)}) %collective-permute-start.1) | collective-permute-done | bytes 532512 | tf_op jit(solution)/shard_map/ppermute | solution.py:29
  34.5 2.7 %collective-permute-start.4 = (bf16[512,256]{1,0:T(8,128)(2,1)S(1)}, bf16[512,256]{1,0:T(8,128)(2,1)S(1)}, u32[]{:S(2)}, u32[]{:S(2)}) collective-permute-start(bf16[512,256]{1,0:T(8,128)(2,1)S(1)} %fusion.1), channel_id=1, source_target_pairs={{0,16},{1,17},{2,18},{3,19},{4,20},{5,21},{6,22},{7,23},{8,24},{9,... | collective-permute-start | bytes 786440 | tf_op jit(solution)/shard_map/ppermute | solution.py:29
  37.1 6.0 %attend.3 = (f32[2,10,128,256]{3,2,1,0:T(8,128)S(1)}, bf16[8,128,256]{2,1,0:T(8,128)(2,1)S(1)}) custom-call(s32[4,2,5]{2,1,0:T(2,128)S(1)} %maximum_convert_fusion.meta, s32[2]{0:T(128)S(1)} %pad_add_fusion.pos, bf16[1040,256]{1,0:T(8,128)(2,1)S(1)} %copy-done.7, bf16[1040,256]{1,0:T(8,128)(2,1)} %collective-permute-done.refs_1_, ...), custom_call_target="tpu_custom_call" | custom-call | flops 2013265920 | bytes 4194304 | tf_op jit(solution)/shard_map/attend/pallas_call | solution.py:192
  43.1 5.4 %collective-permute-done.4.refs_4_ = bf16[512,256]{1,0:T(8,128)(2,1)S(1)} collective-permute-done((bf16[512,256]{1,0:T(8,128)(2,1)S(1)}, bf16[512,256]{1,0:T(8,128)(2,1)S(1)}, u32[]{:S(2)}, u32[]{:S(2)}) %collective-permute-start.4) | collective-permute-done | bytes 262176 | tf_op jit(solution)/shard_map/ppermute | solution.py:29
  48.5 4.6 %attend.4 = (f32[2,10,128,256]{3,2,1,0:T(8,128)S(1)}, bf16[8,128,256]{2,1,0:T(8,128)(2,1)S(1)}, bf16[2,2,128,256]{3,2,1,0:T(8,128)(2,1)S(1)}) custom-call(s32[4,2,5]{2,1,0:T(2,128)S(1)} %maximum_convert_fusion.meta, s32[2]{0:T(128)S(1)} %pad_add_fusion.pos, bf16[1040,256]{1,0:T(8,128)(2,1)S(1)} %copy-done.7, bf16[1040,256]{1,0:T(8,128)(2,1)} %collective-permute-done.refs_1_, ...), custom_call_target="tpu_custom_call" | custom-call | flops 1342177280 | bytes 4194304 | tf_op jit(solution)/shard_map/attend/pallas_call | solution.py:192
  53.2 7.8 %attend.5 = (f32[2,10,128,256]{3,2,1,0:T(8,128)}, bf16[8,128,256]{2,1,0:T(8,128)(2,1)}, bf16[2,128,256]{2,1,0:T(8,128)(2,1)S(1)}, bf16[2,128,256]{2,1,0:T(8,128)...) custom-call(s32[4,2,5]{2,1,0:T(2,128)S(1)} %maximum_convert_fusion.m, ...), custom_call_target="tpu_custom_call" | custom-call | flops 2013265920 | bytes 4194304 | tf_op jit(solution)/shard_map/attend/pallas_call | solution.py:192
  61.7 5.3 %collective-permute-start.5 = (bf16[2,6,128,256]{3,2,1,0:T(8,128)(2,1)S(1)}, bf16[2,6,128,256]{3,2,1,0:T(8,128)(2,1)S(1)}, u32[]{:S(2)}, u32[]{:S(2)}) collective-permute-start(bf16[2,6,128,256]{3,2,1,0:T(8,128)(2,1)S(1)} %get-tuple-element.53), channel_id=1, source_target_pairs={{0,8},{1,9},{2,10},{3,11},{4,12},{5,13},{6,14},{7,15},{8,0},{9,1},... | collective-permute-start | bytes 2359304 | tf_op jit(solution)/shard_map/ppermute | solution.py:29
  67.2 1.6 collective-permute-start.8
  68.8 1.3 slice.46
  70.1 20.0 %collective-permute-done.7 = bf16[2,2,128,256]{3,2,1,0:T(8,128)(2,1)S(1)} collective-permute-done((bf16[2,2,128,256]{3,2,1,0:T(8,128)(2,1)S(1)}, bf16[2,2,128,256]{3,2,1,0:T(8,128)(2,1)S(1)}, u32[]{:S(2)}, u32[]{:S(2)}) %collective-permute-start.7) | collective-permute-done | bytes 262176 | tf_op jit(solution)/shard_map/ppermute | solution.py:29
  91.3 4.5 %collective-permute-start.15 = (bf16[2,384,1024]{2,1,0:T(8,128)(2,1)}, bf16[2,384,1024]{2,1,0:T(8,128)(2,1)}, u32[]{:S(2)}, u32[]{:S(2)}) collective-permute-start(bf16[2,384,1024]{2,1,0:T(8,128)(2,1)} %slice.46), channel_id=1, source_target_pairs={{0,24},{1,25},{2,26},{3,27},{4,28},{5,29},{6,30},{7,31},{24,0},{25... | collective-permute-start | bytes 4718600 | tf_op jit(solution)/shard_map/ppermute | solution.py:29
  96.8 1.5 collective-permute-start.10
  98.3 1.9 %slice.47 = bf16[2,128,1024]{2,1,0:T(8,128)(2,1)} slice(bf16[2,512,1024]{2,1,0:T(8,128)(2,1)} %refs_4_.1), slice={[0:2], [384:512], [0:1024]} | slice | bytes 1048576 | tf_op jit(solution)/shard_map/slice | solution.py:421
  100.3 20.2 %collective-permute-done.10.refs_3_ = bf16[2048,256]{1,0:T(8,128)(2,1)S(1)} collective-permute-done((bf16[2048,256]{1,0:T(8,128)(2,1)S(1)}, bf16[2048,256]{1,0:T(8,128)(2,1)S(1)}, u32[]{:S(2)}, u32[]{:S(2)}) %collective-permute-start.10) | collective-permute-done | bytes 1048608 | tf_op jit(solution)/shard_map/ppermute | solution.py:29
  120.4 3.4 %collective-permute-start.16 = (bf16[2,128,1024]{2,1,0:T(8,128)(2,1)}, bf16[2,128,1024]{2,1,0:T(8,128)(2,1)S(1)}, u32[]{:S(2)}, u32[]{:S(2)}) collective-permute-start(bf16[2,128,1024]{2,1,0:T(8,128)(2,1)} %slice.47), channel_id=1, source_target_pairs={{0,24},{1,25},{2,26},{3,27},{4,28},{5,29},{6,30},{7,31},{24,0},{25... | collective-permute-start | bytes 1572872 | tf_op jit(solution)/shard_map/ppermute | solution.py:29
  123.9 1.6 collective-permute-start.11
  125.4 1.6 copy-done.1
  128.2 4.0 %project.3 = (bf16[2,256,512]{2,1,0:T(8,128)(2,1)}, bf16[2,256,512]{2,1,0:T(8,128)(2,1)S(1)}) custom-call(s32[7]{0:T(128)S(1)} %stack.74.pos, bf16[2048,256]{1,0:T(8,128)(2,1)S(1)} %bitcast.24, bf16[2048,256]{1,0:T(8,128)(2,1)S(1)} %copy-done.5, bf16[2048,256]{1,0:T(8,128)(2,1)S(1)} %bitcast.28, bf16[2048,256]{1,0:T(8,128)(2,1)S(1)} %collective-permute-done.10.refs_3_, ...), custom_call_target="tpu_custom_call" | custom-call | flops 2147483648 | bytes 6291456 | tf_op jit(solution)/shard_map/project/pallas_call | solution.py:261
  133.8 4.5 %project.4 = (bf16[2,256,384]{2,1,0:T(8,128)(2,1)S(1)}, bf16[2,256,384]{2,1,0:T(8,128)(2,1)S(1)}) custom-call(s32[7]{0:T(128)S(1)} %stack.74.pos, bf16[2048,256]{1,0:T(8,128)(2,1)S(1)} %bitcast.25, bf16[2048,256]{1,0:T(8,128)(2,1)S(1)} %copy-done.6, bf16[2048,256]{1,0:T(8,128)(2,1)S(1)} %bitcast.29, bf16[2048,256]{1,0:T(8,128)(2,1)S(1)} %collective-permute-done.10.refs_3_, ...), custom_call_target="tpu_custom_call" | custom-call | flops 1610612736 | bytes 6291456 | tf_op jit(solution)/shard_map/project/pallas_call | solution.py:261
  138.9 2.0 %collective-permute-start.12 = (bf16[256,256]{1,0:T(8,128)(2,1)}, bf16[256,256]{1,0:T(8,128)(2,1)}, u32[]{:S(2)}, u32[]{:S(2)}) collective-permute-start(bf16[256,256]{1,0:T(8,128)(2,1)} %bitcast.10), channel_id=1, source_target_pairs={{0,8},{1,9},{2,10},{3,11},{4,12},{5,13},{6,14},{7,15},{8,0},{9,1},... | collective-permute-start | bytes 393224 | tf_op jit(solution)/shard_map/ppermute | solution.py:29
  141.9 2.6 %project.5 = (bf16[2,256,128]{2,1,0:T(8,128)(2,1)}, bf16[2,256,128]{2,1,0:T(8,128)(2,1)S(1)}) custom-call(s32[7]{0:T(128)S(1)} %stack.74.pos, bf16[2048,256]{1,0:T(8,128)(2,1)S(1)} %bitcast.26, bf16[2048,256]{1,0:T(8,128)(2,1)S(1)} %copy-done.6, bf16[2048,256]{1,0:T(8,128)(2,1)S(1)} %bitcast.30, bf16[2048,256]{1,0:T(8,128)(2,1)S(1)} %collective-permute-done.10.refs_3_, ...), custom_call_target="tpu_custom_call" | custom-call | flops 536870912 | bytes 6291456 | tf_op jit(solution)/shard_map/project/pallas_call | solution.py:261
  145.1 1.3 collective-permute-done.13.refs_3_
  148.3 2.7 %merge.1 = (bf16[256,512]{1,0:T(8,128)(2,1)}, bf16[256,512]{1,0:T(8,128)(2,1)}, bf16[256,512]{1,0:T(8,128)(2,1)}, bf16[256,512]{1,0:T(8,128)(2,1)}) custom-call(s32[1]{0:T(128)} %bitcast.13.flip, bf16[2,256,512]{2,1,0:T(8,128)(2,1)} %copy-done.8, bf16[2,256,512]{2,1,0:T(8,128)(2,1)} %collective-permute-done.14.refs_1_, bf16[2,256,384]{2,1,0:T(8,128)(2,1)} %copy-done.9, ...), custom_call_target="tpu_custom_call" | custom-call | tf_op jit(solution)/shard_map/merge/pallas_call | solution.py:306
  151.0 1.7 %collective-permute-start.19 = (bf16[256,512]{1,0:T(8,128)(2,1)}, bf16[256,512]{1,0:T(8,128)(2,1)S(1)}, u32[]{:S(2)}, u32[]{:S(2)}) collective-permute-start(bf16[256,512]{1,0:T(8,128)(2,1)} %get-tuple-element.76), channel_id=1, source_target_pairs={{0,7},{1,15},{2,4},{3,12},{4,3},{5,11},{6,0},{7,8},{8,6},{9,14},{1... | collective-permute-start | bytes 786440 | tf_op jit(solution)/shard_map/ppermute | solution.py:29
  153.7 1.6 collective-permute-start.22
  155.3 2.0 %place_columns.1 = bf16[256,1024]{1,0:T(8,128)(2,1)} custom-call(s32[1]{0:T(128)} %bitcast.pos, bf16[256,256]{1,0:T(8,128)(2,1)} %bitcast.31, bf16[256,256]{1,0:T(8,128)(2,1)} %copy-done.17, bf16[256,256]{1,0:T(8,128)(2,1)} %collective-permute-done.12.refs_2_, bf16[256,256]{1,0:T(8,128)(2,1)} %collective-permute-done.13.refs_3_), custom_call_target="tpu_custom_call" | custom-call | tf_op jit(solution)/shard_map/place_columns/pallas_call | solution.py:346
  157.2 9.3 %collective-permute-done.19.refs_0_ = bf16[256,512]{1,0:T(8,128)(2,1)S(1)} collective-permute-done((bf16[256,512]{1,0:T(8,128)(2,1)}, bf16[256,512]{1,0:T(8,128)(2,1)S(1)}, u32[]{:S(2)}, u32[]{:S(2)}) %collective-permute-start.19) | collective-permute-done | bytes 262176 | tf_op jit(solution)/shard_map/ppermute | solution.py:29
  167.5 2.1 %collect.1 = bf16[256,1024]{1,0:T(8,128)(2,1)} custom-call(s32[1]{0:T(128)} %bitcast.12.pos, bf16[256,512]{1,0:T(8,128)(2,1)} %copy-done.12, bf16[256,512]{1,0:T(8,128)(2,1)} %copy-done.13, bf16[256,512]{1,0:T(8,128)(2,1)} %copy-done.14, bf16[256,512]{1,0:T(8,128)(2,1)} %copy-done.15), custom_call_target="tpu_custom_call" | custom-call | tf_op jit(solution)/shard_map/collect/pallas_call | solution.py:326
  (75 shorter events, 17.5 us)
Async XLA Ops:
  0.6 7.9 %copy-start = (bf16[2,512,1024]{2,1,0:T(8,128)(2,1)S(1)}, bf16[2,512,1024]{2,1,0:T(8,128)(2,1)}, u32[]{:S(2)}) copy-start(bf16[2,512,1024]{2,1,0:T(8,128)(2,1)} %refs_4_.1) | copy-start | bytes 6291460
  4.0 29.3 %copy-start.7 = (bf16[1040,256]{1,0:T(8,128)(2,1)S(1)}, bf16[1040,256]{1,0:T(8,128)(2,1)}, u32[]{:S(2)}) copy-start(bf16[1040,256]{1,0:T(8,128)(2,1)} %get-tuple-element.41.refs_0_) | copy-start | bytes 1597444
  4.0 17.2 %collective-permute-start.2 = (bf16[1040,256]{1,0:T(8,128)(2,1)}, bf16[1040,256]{1,0:T(8,128)(2,1)}, u32[]{:S(2)}, u32[]{:S(2)}) collective-permute-start(bf16[1040,256]{1,0:T(8,128)(2,1)} %get-tuple-element.44), channel_id=1, source_target_pairs={{0,12},{1,13},{2,14},{3,15},{4,8},{5,9},{6,10},{7,11},{8,4},{9,5},... | collective-permute-start | bytes 1597448 | tf_op jit(solution)/shard_map/ppermute | solution.py:29
  7.9 24.0 %collective-permute-start.1 = (bf16[1040,256]{1,0:T(8,128)(2,1)}, bf16[1040,256]{1,0:T(8,128)(2,1)}, u32[]{:S(2)}, u32[]{:S(2)}) collective-permute-start(bf16[1040,256]{1,0:T(8,128)(2,1)} %get-tuple-element.43), channel_id=1, source_target_pairs={{0,8},{1,9},{2,10},{3,11},{4,12},{5,13},{6,14},{7,15},{8,0},{9,1},... | collective-permute-start | bytes 1597448 | tf_op jit(solution)/shard_map/ppermute | solution.py:29
  8.4 24.3 %collective-permute-start = (bf16[1040,256]{1,0:T(8,128)(2,1)}, bf16[1040,256]{1,0:T(8,128)(2,1)}, u32[]{:S(2)}, u32[]{:S(2)}) collective-permute-start(bf16[1040,256]{1,0:T(8,128)(2,1)} %get-tuple-element.42), channel_id=1, source_target_pairs={{0,4},{1,5},{2,6},{3,7},{4,0},{5,1},{6,2},{7,3},{8,12},{9,13},{10,... | collective-permute-start | bytes 1597448 | tf_op jit(solution)/shard_map/ppermute | solution.py:29
  9.6 24.9 %collective-permute-start.3 = (bf16[2,224,1024]{2,1,0:T(8,128)(2,1)}, bf16[2,224,1024]{2,1,0:T(8,128)(2,1)}, u32[]{:S(2)}, u32[]{:S(2)}) collective-permute-start(bf16[2,224,1024]{2,1,0:T(8,128)(2,1)} %slice.44), channel_id=1, source_target_pairs={{8,16},{9,17},{10,18},{11,19},{12,20},{13,21},{14,22},{15,23},{16,... | collective-permute-start | bytes 2752520 | tf_op jit(solution)/shard_map/ppermute | solution.py:29
  34.5 14.0 %collective-permute-start.4 = (bf16[512,256]{1,0:T(8,128)(2,1)S(1)}, bf16[512,256]{1,0:T(8,128)(2,1)S(1)}, u32[]{:S(2)}, u32[]{:S(2)}) collective-permute-start(bf16[512,256]{1,0:T(8,128)(2,1)S(1)} %fusion.1), channel_id=1, source_target_pairs={{0,16},{1,17},{2,18},{3,19},{4,20},{5,21},{6,22},{7,23},{8,24},{9,... | collective-permute-start | bytes 786440 | tf_op jit(solution)/shard_map/ppermute | solution.py:29
  53.1 14.0 %collective-permute-start.6 = (bf16[2,2,128,256]{3,2,1,0:T(8,128)(2,1)S(1)}, bf16[2,2,128,256]{3,2,1,0:T(8,128)(2,1)S(1)}, u32[]{:S(2)}, u32[]{:S(2)}) collective-permute-start(bf16[2,2,128,256]{3,2,1,0:T(8,128)(2,1)S(1)} %get-tuple-element.55), channel_id=1, source_target_pairs={{0,16},{1,17},{2,18},{3,19},{4,20},{5,21},{6,22},{7,23},{8,24},{9,... | collective-permute-start | bytes 786440 | tf_op jit(solution)/shard_map/ppermute | solution.py:29
  61.0 9.1 %copy-start.11 = (bf16[2,128,256]{2,1,0:T(8,128)(2,1)}, bf16[2,128,256]{2,1,0:T(8,128)(2,1)S(1)}, u32[]{:S(2)}) copy-start(bf16[2,128,256]{2,1,0:T(8,128)(2,1)S(1)} %get-tuple-element.51) | copy-start | bytes 393220
  61.0 29.2 %collective-permute-start.9 = (bf16[2,288,1024]{2,1,0:T(8,128)(2,1)S(1)}, bf16[2,288,1024]{2,1,0:T(8,128)(2,1)S(1)}, u32[]{:S(2)}, u32[]{:S(2)}) collective-permute-start(bf16[2,288,1024]{2,1,0:T(8,128)(2,1)S(1)} %slice.45), channel_id=1, source_target_pairs={{8,16},{9,17},{10,18},{11,19},{12,20},{13,21},{14,22},{15,23},{16,... | collective-permute-start | bytes 3538952 | tf_op jit(solution)/shard_map/ppermute | solution.py:29
  61.7 28.4 %collective-permute-start.5 = (bf16[2,6,128,256]{3,2,1,0:T(8,128)(2,1)S(1)}, bf16[2,6,128,256]{3,2,1,0:T(8,128)(2,1)S(1)}, u32[]{:S(2)}, u32[]{:S(2)}) collective-permute-start(bf16[2,6,128,256]{3,2,1,0:T(8,128)(2,1)S(1)} %get-tuple-element.53), channel_id=1, source_target_pairs={{0,8},{1,9},{2,10},{3,11},{4,12},{5,13},{6,14},{7,15},{8,0},{9,1},... | collective-permute-start | bytes 2359304 | tf_op jit(solution)/shard_map/ppermute | solution.py:29
  67.2 28.6 %collective-permute-start.8 = (bf16[2048,256]{1,0:T(8,128)(2,1)S(1)}, bf16[2048,256]{1,0:T(8,128)(2,1)S(1)}, u32[]{:S(2)}, u32[]{:S(2)}) collective-permute-start(bf16[2048,256]{1,0:T(8,128)(2,1)S(1)} %bitcast.23), channel_id=1, source_target_pairs={{0,4},{1,5},{2,6},{3,7},{4,0},{5,1},{6,2},{7,3},{8,12},{9,13},{10,... | collective-permute-start | bytes 3145736 | tf_op jit(solution)/shard_map/ppermute | solution.py:29
  68.8 21.3 %collective-permute-start.7 = (bf16[2,2,128,256]{3,2,1,0:T(8,128)(2,1)S(1)}, bf16[2,2,128,256]{3,2,1,0:T(8,128)(2,1)S(1)}, u32[]{:S(2)}, u32[]{:S(2)}) collective-permute-start(bf16[2,2,128,256]{3,2,1,0:T(8,128)(2,1)S(1)} %add_convert_fusion), channel_id=1, source_target_pairs={{0,8},{1,9},{2,10},{3,11},{4,12},{5,13},{6,14},{7,15},{8,0},{9,1},... | collective-permute-start | bytes 786440 | tf_op jit(solution)/shard_map/ppermute | solution.py:29
  90.2 1.0 copy-start.2
  91.3 42.5 %collective-permute-start.15 = (bf16[2,384,1024]{2,1,0:T(8,128)(2,1)}, bf16[2,384,1024]{2,1,0:T(8,128)(2,1)}, u32[]{:S(2)}, u32[]{:S(2)}) collective-permute-start(bf16[2,384,1024]{2,1,0:T(8,128)(2,1)} %slice.46), channel_id=1, source_target_pairs={{0,24},{1,25},{2,26},{3,27},{4,28},{5,29},{6,30},{7,31},{24,0},{25... | collective-permute-start | bytes 4718600 | tf_op jit(solution)/shard_map/ppermute | solution.py:29
  96.8 23.6 %collective-permute-start.10 = (bf16[2048,256]{1,0:T(8,128)(2,1)S(1)}, bf16[2048,256]{1,0:T(8,128)(2,1)S(1)}, u32[]{:S(2)}, u32[]{:S(2)}) collective-permute-start(bf16[2048,256]{1,0:T(8,128)(2,1)S(1)} %bitcast.27), channel_id=1, source_target_pairs={{0,4},{1,5},{2,6},{3,7},{4,0},{5,1},{6,2},{7,3},{8,12},{9,13},{10,... | collective-permute-start | bytes 3145736 | tf_op jit(solution)/shard_map/ppermute | solution.py:29
  120.4 21.4 %collective-permute-start.16 = (bf16[2,128,1024]{2,1,0:T(8,128)(2,1)}, bf16[2,128,1024]{2,1,0:T(8,128)(2,1)S(1)}, u32[]{:S(2)}, u32[]{:S(2)}) collective-permute-start(bf16[2,128,1024]{2,1,0:T(8,128)(2,1)} %slice.47), channel_id=1, source_target_pairs={{0,24},{1,25},{2,26},{3,27},{4,28},{5,29},{6,30},{7,31},{24,0},{25... | collective-permute-start | bytes 1572872 | tf_op jit(solution)/shard_map/ppermute | solution.py:29
  123.9 9.2 %collective-permute-start.11 = (bf16[256,256]{1,0:T(8,128)(2,1)S(1)}, bf16[256,256]{1,0:T(8,128)(2,1)S(1)}, u32[]{:S(2)}, u32[]{:S(2)}) collective-permute-start(bf16[256,256]{1,0:T(8,128)(2,1)S(1)} %bitcast.32), channel_id=1, source_target_pairs={{0,4},{1,5},{2,6},{3,7},{4,0},{5,1},{6,2},{7,3},{8,12},{9,13},{10,... | collective-permute-start | bytes 393224 | tf_op jit(solution)/shard_map/ppermute | solution.py:29
  125.4 1.6 copy-start.1
  127.0 1.2 copy-start.5
  128.2 5.5 %copy-start.3 = (bf16[2,288,1024]{2,1,0:T(8,128)(2,1)S(1)}, bf16[2,288,1024]{2,1,0:T(8,128)(2,1)}, u32[]{:S(2)}) copy-start(bf16[2,288,1024]{2,1,0:T(8,128)(2,1)} %copy-done.2) | copy-start | bytes 3538948
  128.2 5.5 %copy-start.6 = (bf16[2048,256]{1,0:T(8,128)(2,1)S(1)}, bf16[2048,256]{1,0:T(8,128)(2,1)}, u32[]{:S(2)}) copy-start(bf16[2048,256]{1,0:T(8,128)(2,1)} %copy-done.4) | copy-start | bytes 3145732
  133.1 14.5 %collective-permute-start.14 = (bf16[2,256,512]{2,1,0:T(8,128)(2,1)}, bf16[2,256,512]{2,1,0:T(8,128)(2,1)}, u32[]{:S(2)}, u32[]{:S(2)}) collective-permute-start(bf16[2,256,512]{2,1,0:T(8,128)(2,1)} %get-tuple-element.64), channel_id=1, source_target_pairs={{0,1},{1,0},{2,3},{3,2},{4,5},{5,4},{6,7},{7,6},{8,9},{9,8},{10,11... | collective-permute-start | bytes 1572872 | tf_op jit(solution)/shard_map/ppermute | solution.py:29
  138.3 6.2 %copy-start.9 = (bf16[2,256,384]{2,1,0:T(8,128)(2,1)}, bf16[2,256,384]{2,1,0:T(8,128)(2,1)S(1)}, u32[]{:S(2)}) copy-start(bf16[2,256,384]{2,1,0:T(8,128)(2,1)S(1)} %get-tuple-element.69.refs_2_) | copy-start | bytes 1179652
  138.3 9.3 %collective-permute-start.17 = (bf16[2,256,384]{2,1,0:T(8,128)(2,1)S(1)}, bf16[2,256,384]{2,1,0:T(8,128)(2,1)}, u32[]{:S(2)}, u32[]{:S(2)}) collective-permute-start(bf16[2,256,384]{2,1,0:T(8,128)(2,1)S(1)} %get-tuple-element.74), channel_id=1, source_target_pairs={{0,1},{1,0},{2,3},{3,2},{4,5},{5,4},{6,7},{7,6},{8,9},{9,8},{10,11... | collective-permute-start | bytes 1179656 | tf_op jit(solution)/shard_map/ppermute | solution.py:29
  138.9 7.6 %collective-permute-start.13 = (bf16[256,256]{1,0:T(8,128)(2,1)}, bf16[256,256]{1,0:T(8,128)(2,1)}, u32[]{:S(2)}, u32[]{:S(2)}) collective-permute-start(bf16[256,256]{1,0:T(8,128)(2,1)} %bitcast.11), channel_id=1, source_target_pairs={{0,12},{1,13},{2,14},{3,15},{4,8},{5,9},{6,10},{7,11},{8,4},{9,5},... | collective-permute-start | bytes 393224 | tf_op jit(solution)/shard_map/ppermute | solution.py:29
  138.9 8.7 %collective-permute-start.12 = (bf16[256,256]{1,0:T(8,128)(2,1)}, bf16[256,256]{1,0:T(8,128)(2,1)}, u32[]{:S(2)}, u32[]{:S(2)}) collective-permute-start(bf16[256,256]{1,0:T(8,128)(2,1)} %bitcast.10), channel_id=1, source_target_pairs={{0,8},{1,9},{2,10},{3,11},{4,12},{5,13},{6,14},{7,15},{8,0},{9,1},... | collective-permute-start | bytes 393224 | tf_op jit(solution)/shard_map/ppermute | solution.py:29
  145.1 2.5 %collective-permute-start.18 = (bf16[2,256,128]{2,1,0:T(8,128)(2,1)}, bf16[2,256,128]{2,1,0:T(8,128)(2,1)S(1)}, u32[]{:S(2)}, u32[]{:S(2)}) collective-permute-start(bf16[2,256,128]{2,1,0:T(8,128)(2,1)} %get-tuple-element.75), channel_id=1, source_target_pairs={{0,1},{1,0},{2,3},{3,2},{4,5},{5,4},{6,7},{7,6},{8,9},{9,8},{10,11... | collective-permute-start | bytes 393224 | tf_op jit(solution)/shard_map/ppermute | solution.py:29
  151.0 15.5 %collective-permute-start.19 = (bf16[256,512]{1,0:T(8,128)(2,1)}, bf16[256,512]{1,0:T(8,128)(2,1)S(1)}, u32[]{:S(2)}, u32[]{:S(2)}) collective-permute-start(bf16[256,512]{1,0:T(8,128)(2,1)} %get-tuple-element.76), channel_id=1, source_target_pairs={{0,7},{1,15},{2,4},{3,12},{4,3},{5,11},{6,0},{7,8},{8,6},{9,14},{1... | collective-permute-start | bytes 786440 | tf_op jit(solution)/shard_map/ppermute | solution.py:29
  152.7 13.7 %collective-permute-start.20 = (bf16[256,512]{1,0:T(8,128)(2,1)}, bf16[256,512]{1,0:T(8,128)(2,1)S(1)}, u32[]{:S(2)}, u32[]{:S(2)}) collective-permute-start(bf16[256,512]{1,0:T(8,128)(2,1)} %get-tuple-element.77), channel_id=1, source_target_pairs={{0,4},{1,12},{2,7},{3,15},{4,0},{5,8},{6,3},{7,11},{8,5},{9,13},{1... | collective-permute-start | bytes 786440 | tf_op jit(solution)/shard_map/ppermute | solution.py:29
  153.0 13.5 %collective-permute-start.21 = (bf16[256,512]{1,0:T(8,128)(2,1)}, bf16[256,512]{1,0:T(8,128)(2,1)S(1)}, u32[]{:S(2)}, u32[]{:S(2)}) collective-permute-start(bf16[256,512]{1,0:T(8,128)(2,1)} %get-tuple-element.78), channel_id=1, source_target_pairs={{0,3},{1,11},{2,0},{3,8},{4,7},{5,15},{6,4},{7,12},{8,2},{9,10},{1... | collective-permute-start | bytes 786440 | tf_op jit(solution)/shard_map/ppermute | solution.py:29
  153.7 12.8 %collective-permute-start.22 = (bf16[256,512]{1,0:T(8,128)(2,1)}, bf16[256,512]{1,0:T(8,128)(2,1)S(1)}, u32[]{:S(2)}, u32[]{:S(2)}) collective-permute-start(bf16[256,512]{1,0:T(8,128)(2,1)} %get-tuple-element.79), channel_id=1, source_target_pairs={{0,0},{1,8},{2,3},{3,11},{4,4},{5,12},{6,7},{7,15},{8,1},{9,9},{10... | collective-permute-start | bytes 786440 | tf_op jit(solution)/shard_map/ppermute | solution.py:29
  (9 other events, 7.2 us)
